TPU v7x, 512 devices: a whole 4x4x16 slice. The times are simulated.
512 devices in a mesh: dom: 512 (over z, x, y, core).
Axes of the slice: x: 4, y: 4, z: 16, core: 2. Of those that a mesh axis runs over, the one named last changes fastest.
Arguments:
- features: bfloat16 [262144, 256], P('dom'), may hold values from -20 to 20, as said below
- w_self: bfloat16 [256, 256], replicated, may hold values from -0.375 to 0.375
- w_neigh: bfloat16 [256, 256], replicated, may hold values from -0.375 to 0.375
- neighbors: int32 [262144, 10], P('dom'), may hold values from 0 to 1663
- degree: int32 [262144], P('dom'), may hold values from 1 to 10
- boundary: int32 [512, 9, 128], P('dom'), may hold values from 0 to 511
- upstream: bfloat16 [262144, 256], P('dom'), may hold values from -6 to 6
Outputs:
- hidden: bfloat16 [262144, 256], P('dom')
- node_grad: bfloat16 [262144, 256], P('dom')
- weight_step: float32 [512, 256], replicated
Inputs may be any that keep to these rules, and one draw needn't show every extreme that they name: `features`: feature values lie in the stated range.
All inputs are finite; a program needn't handle non-finite values.
Results may differ from a plain program's by a relative error of at most 0.006.
Values may be sent and summed in bfloat16 or wider, within the bound.
No kernel may reach another device: no remote copies, remote signals or barrier semaphores. Data moves between devices by JAX's collectives and lax.ppermute only.
A program may use at most 64 MiB of HBM per device.

v0:
```python
import jax
import jax.numpy as jnp
from jax import lax
from jax.sharding import PartitionSpec as P

epsilon = 1e-06


def swapped(x, axis, apart):
    return lax.ppermute(x, axis, [(i, i ^ 1 << apart) for i in range(lax.axis_size(axis))])


def swap_rows(features, boundary_rows, levels):
    received = []
    for level in range(levels):
        received.append(swapped(features[boundary_rows[level]], "dom", level))
    return received


def scatter_slots(values, neighbors, degree, total_rows):
    table = jnp.zeros((total_rows, values.shape[1]), jnp.float32)
    for slot in range(neighbors.shape[1]):
        usable = (slot < degree)[:, None]
        table = table.at[neighbors[:, slot]].add(jnp.where(usable, values, jnp.float32(0.0)))
    return table


def per_device(features, w_self, w_neigh, neighbors, degree, boundary, upstream):
    levels = lax.axis_size("dom").bit_length() - 1
    node_dev = features.shape[0]
    feature_width = features.shape[1]
    slot_count = neighbors.shape[1]
    boundary_rows = boundary[0]
    bnd_rows = boundary_rows.shape[1]
    degree_float = degree.astype(jnp.float32)[:, None]
    extended = jnp.concatenate([features] + swap_rows(features, boundary_rows, levels), axis=0)
    summed = jnp.zeros((node_dev, feature_width), jnp.float32)
    for slot in range(slot_count):
        usable = (slot < degree)[:, None]
        summed = summed + jnp.where(
            usable, extended[neighbors[:, slot]].astype(jnp.float32), jnp.float32(0.0)
        )
    agg = (summed / degree_float).astype(jnp.bfloat16)
    pre_sum = jnp.dot(features, w_self, preferred_element_type=jnp.float32) + jnp.dot(
        agg, w_neigh, preferred_element_type=jnp.float32
    )
    hidden = jax.nn.silu(pre_sum).astype(jnp.bfloat16)
    sigmoid_pre = jax.nn.sigmoid(pre_sum)
    pre_grad = (
        upstream.astype(jnp.float32) * sigmoid_pre * (1.0 + pre_sum * (1.0 - sigmoid_pre))
    ).astype(jnp.bfloat16)
    row_contract = (((0,), (0,)), ((), ()))
    grad_self = lax.dot_general(
        features, pre_grad, row_contract, preferred_element_type=jnp.float32
    )
    grad_neigh = lax.dot_general(agg, pre_grad, row_contract, preferred_element_type=jnp.float32)
    stacked = jnp.concatenate([grad_self, grad_neigh], axis=0)
    total_grad = lax.psum(stacked, "dom")
    weight_step = total_grad * lax.rsqrt(jnp.mean(total_grad * total_grad) + epsilon)
    column_contract = (((1,), (1,)), ((), ()))
    self_grad = lax.dot_general(
        pre_grad, w_self, column_contract, preferred_element_type=jnp.float32
    )
    total_rows = node_dev + levels * bnd_rows
    slot_share = (
        lax.dot_general(pre_grad, w_neigh, column_contract, preferred_element_type=jnp.float32)
        / degree_float
    )
    ext_grad = scatter_slots(slot_share, neighbors, degree, total_rows)
    local_grad = self_grad + ext_grad[:node_dev]
    for level in range(levels):
        start_row = node_dev + level * bnd_rows
        returned = swapped(
            ext_grad[start_row : start_row + bnd_rows].astype(jnp.bfloat16), "dom", level
        ).astype(jnp.float32)
        local_grad = local_grad.at[boundary_rows[level]].add(returned)
    node_grad = local_grad.astype(jnp.bfloat16)
    return (hidden, node_grad, weight_step)


def solution(mesh):
    return jax.shard_map(
        per_device,
        mesh=mesh,
        in_specs=(
            P("dom", None),
            P(),
            P(),
            P("dom", None),
            P("dom"),
            P("dom", None, None),
            P("dom", None),
        ),
        out_specs=(P("dom", None), P("dom", None), P()),
        check_vma=False,
    )
```

profile of v0, /device:TPU:1, one launch (start us, length us, event | category | flops | bytes accessed | tf_op | source)
XLA Modules:
  0.0 620.9 jit_solution(8215190168502621439)
XLA Ops:
  10.0 8.8 %collective-permute-start = (bf16[128,256]{1,0:T(8,128)(2,1)S(1)}, bf16[128,256]{1,0:T(8,128)(2,1)S(1)}, u32[]{:S(2)}, u32[]{:S(2)}) collective-permute-start(bf16[128,256]{1,0:T(8,128)(2,1)S(1)} %gather_fusion), channel_id=1, source_target_pairs={{0,1},{1,0},{2,3},{3,2},{4,5},{5,4},{6,7},{7,6},{8,9},{9,8},{10,11... | collective-permute-start | bytes 196616 | tf_op jit(solution)/shard_map/ppermute | solution.py:10
  29.8 4.1 collective-permute-start.4
  39.8 3.5 collective-permute-start.5
  43.3 4.9 collective-permute-start.6
  48.3 8.8 %collective-permute-start.7 = (bf16[128,256]{1,0:T(8,128)(2,1)S(1)}, bf16[128,256]{1,0:T(8,128)(2,1)S(1)}, u32[]{:S(2)}, u32[]{:S(2)}) collective-permute-start(bf16[128,256]{1,0:T(8,128)(2,1)S(1)} %gather_fusion.7), channel_id=1, source_target_pairs={{0,128},{1,129},{2,130},{3,131},{4,132},{5,133},{6,134},{7,135},{8... | collective-permute-start | bytes 196616 | tf_op jit(solution)/shard_map/ppermute | solution.py:10
  57.1 8.5 %collective-permute-start.8 = (bf16[128,256]{1,0:T(8,128)(2,1)S(1)}, bf16[128,256]{1,0:T(8,128)(2,1)S(1)}, u32[]{:S(2)}, u32[]{:S(2)}) collective-permute-start(bf16[128,256]{1,0:T(8,128)(2,1)S(1)} %gather_fusion.8), channel_id=1, source_target_pairs={{0,256},{1,257},{2,258},{3,259},{4,260},{5,261},{6,262},{7,263},{8... | collective-permute-start | bytes 196616 | tf_op jit(solution)/shard_map/ppermute | solution.py:10
  65.7 5.2 collective-permute-done.8
  72.9 2.0 gather_fusion.17
  74.9 2.0 gather_fusion.16
  76.8 2.0 gather_fusion.15
  78.8 2.0 gather_fusion.14
  80.8 2.0 gather_fusion.13
  86.7 2.6 gather_fusion.10
  89.3 2.6 gather_fusion.9
  92.0 2.8 divide_convert_fusion
  96.8 4.0 scatter_custom_fusion
  100.8 4.4 scatter_custom_fusion.1
  105.2 4.2 scatter_custom_fusion.2
  109.4 4.2 scatter_custom_fusion.3
  113.7 4.2 scatter_custom_fusion.4
  117.9 4.2 scatter_custom_fusion.5
  122.1 4.4 scatter_custom_fusion.6
  126.6 4.1 scatter_custom_fusion.7
  130.7 4.1 scatter_custom_fusion.8
  134.8 4.1 scatter_custom_fusion.9
  139.7 5.7 collective-permute-start.9
  147.3 3.0 collective-permute-start.11
  153.1 3.3 collective-permute-start.13
  156.4 5.1 collective-permute-start.14
  163.4 2.0 collective-permute-start.16
  165.5 11.3 %collective-permute-start.17 = (bf16[128,256]{1,0:T(8,128)(2,1)S(1)}, bf16[128,256]{1,0:T(8,128)(2,1)S(1)}, u32[]{:S(2)}, u32[]{:S(2)}) collective-permute-start(bf16[128,256]{1,0:T(8,128)(2,1)S(1)} %get-tuple-element.3), channel_id=1, source_target_pairs={{0,256},{1,257},{2,258},{3,259},{4,260},{5,261},{6,262},{7,263},{8... | collective-permute-start | bytes 196616 | tf_op jit(solution)/shard_map/ppermute | solution.py:10
  193.1 416.3 %all-reduce.2.cloned.1.call-done = f32[512,256]{1,0:T(8,128)} async-done(((f32[512,256]{1,0:T(8,128)}), f32[512,256]{1,0:T(8,128)}) %all-reduce.2.cloned.1.call-update) | async-done | bytes 524304 | tf_op jit(solution)/shard_map/psum | solution.py:58
  (170 shorter events, 54.5 us)
Async XLA Ops:
  7.2 87.6 %copy-start = (bf16[256,256]{1,0:T(8,128)(2,1)S(1)}, bf16[256,256]{1,0:T(8,128)(2,1)}, u32[]{:S(2)}) copy-start(bf16[256,256]{1,0:T(8,128)(2,1)} %param.9) | copy-start | bytes 393220
  7.2 602.3 %all-reduce.2.cloned.1.call-start = ((), (), s32[]{:S(2)}) async-start(), calls=%async_computation | async-start | bytes 1048576 | tf_op jit(solution)/shard_map/psum | solution.py:58
  8.1 25.9 %copy-start.36 = (s32[128]{0:T(128)}, s32[128]{0:T(128)S(1)}, u32[]{:S(2)}) copy-start(s32[128]{0:T(128)S(1)} %get-tuple-element.27) | copy-start | bytes 1540
  8.1 27.5 %copy-start.35 = (s32[128]{0:T(128)}, s32[128]{0:T(128)S(1)}, u32[]{:S(2)}) copy-start(s32[128]{0:T(128)S(1)} %get-tuple-element.26) | copy-start | bytes 1540
  8.1 28.4 %copy-start.34 = (s32[128]{0:T(128)}, s32[128]{0:T(128)S(1)}, u32[]{:S(2)}) copy-start(s32[128]{0:T(128)S(1)} %get-tuple-element.25) | copy-start | bytes 1540
  8.1 29.3 %copy-start.33 = (s32[128]{0:T(128)}, s32[128]{0:T(128)S(1)}, u32[]{:S(2)}) copy-start(s32[128]{0:T(128)S(1)} %get-tuple-element.32) | copy-start | bytes 1540
  8.1 30.1 %copy-start.32 = (s32[128]{0:T(128)}, s32[128]{0:T(128)S(1)}, u32[]{:S(2)}) copy-start(s32[128]{0:T(128)S(1)} %get-tuple-element.24) | copy-start | bytes 1540
  8.2 26.5 %copy-start.3 = (bf16[256,256]{1,0:T(8,128)(2,1)S(1)}, bf16[256,256]{1,0:T(8,128)(2,1)}, u32[]{:S(2)}) copy-start(bf16[256,256]{1,0:T(8,128)(2,1)} %param.8) | copy-start | bytes 393220
  10.0 29.8 %collective-permute-start = (bf16[128,256]{1,0:T(8,128)(2,1)S(1)}, bf16[128,256]{1,0:T(8,128)(2,1)S(1)}, u32[]{:S(2)}, u32[]{:S(2)}) collective-permute-start(bf16[128,256]{1,0:T(8,128)(2,1)S(1)} %gather_fusion), channel_id=1, source_target_pairs={{0,1},{1,0},{2,3},{3,2},{4,5},{5,4},{6,7},{7,6},{8,9},{9,8},{10,11... | collective-permute-start | bytes 196616 | tf_op jit(solution)/shard_map/ppermute | solution.py:10
  20.5 22.8 %collective-permute-start.1 = (bf16[128,256]{1,0:T(8,128)(2,1)S(1)}, bf16[128,256]{1,0:T(8,128)(2,1)S(1)}, u32[]{:S(2)}, u32[]{:S(2)}) collective-permute-start(bf16[128,256]{1,0:T(8,128)(2,1)S(1)} %gather_fusion.1), channel_id=1, source_target_pairs={{0,2},{1,3},{2,0},{3,1},{4,6},{5,7},{6,4},{7,5},{8,10},{9,11},{10,... | collective-permute-start | bytes 196616 | tf_op jit(solution)/shard_map/ppermute | solution.py:10
  24.2 24.1 %collective-permute-start.2 = (bf16[128,256]{1,0:T(8,128)(2,1)S(1)}, bf16[128,256]{1,0:T(8,128)(2,1)S(1)}, u32[]{:S(2)}, u32[]{:S(2)}) collective-permute-start(bf16[128,256]{1,0:T(8,128)(2,1)S(1)} %gather_fusion.2), channel_id=1, source_target_pairs={{0,4},{1,5},{2,6},{3,7},{4,0},{5,1},{6,2},{7,3},{8,12},{9,13},{10,... | collective-permute-start | bytes 196616 | tf_op jit(solution)/shard_map/ppermute | solution.py:10
  27.0 30.1 %collective-permute-start.3 = (bf16[128,256]{1,0:T(8,128)(2,1)S(1)}, bf16[128,256]{1,0:T(8,128)(2,1)S(1)}, u32[]{:S(2)}, u32[]{:S(2)}) collective-permute-start(bf16[128,256]{1,0:T(8,128)(2,1)S(1)} %gather_fusion.3), channel_id=1, source_target_pairs={{0,8},{1,9},{2,10},{3,11},{4,12},{5,13},{6,14},{7,15},{8,0},{9,1},... | collective-permute-start | bytes 196616 | tf_op jit(solution)/shard_map/ppermute | solution.py:10
  29.8 35.8 %collective-permute-start.4 = (bf16[128,256]{1,0:T(8,128)(2,1)S(1)}, bf16[128,256]{1,0:T(8,128)(2,1)S(1)}, u32[]{:S(2)}, u32[]{:S(2)}) collective-permute-start(bf16[128,256]{1,0:T(8,128)(2,1)S(1)} %gather_fusion.4), channel_id=1, source_target_pairs={{0,16},{1,17},{2,18},{3,19},{4,20},{5,21},{6,22},{7,23},{8,24},{9,... | collective-permute-start | bytes 196616 | tf_op jit(solution)/shard_map/ppermute | solution.py:10
  39.2 33.7 %copy-start.6 = (s32[512,1]{0,1:T(1,128)}, s32[512,1]{0,1:T(1,128)S(1)}, u32[]{:S(2)}) copy-start(s32[512,1]{0,1:T(1,128)S(1)} %get-tuple-element.16) | copy-start | bytes 6148
  39.2 33.7 %copy-start.7 = (s32[512,1]{0,1:T(1,128)}, s32[512,1]{0,1:T(1,128)S(1)}, u32[]{:S(2)}) copy-start(s32[512,1]{0,1:T(1,128)S(1)} %get-tuple-element.17) | copy-start | bytes 6148
  39.2 33.7 %copy-start.8 = (s32[512,1]{0,1:T(1,128)}, s32[512,1]{0,1:T(1,128)S(1)}, u32[]{:S(2)}) copy-start(s32[512,1]{0,1:T(1,128)S(1)} %get-tuple-element.18) | copy-start | bytes 6148
  39.2 33.7 %copy-start.10 = (s32[512,1]{0,1:T(1,128)}, s32[512,1]{0,1:T(1,128)S(1)}, u32[]{:S(2)}) copy-start(s32[512,1]{0,1:T(1,128)S(1)} %get-tuple-element.20) | copy-start | bytes 6148
  39.2 33.7 %copy-start.11 = (s32[512,1]{0,1:T(1,128)}, s32[512,1]{0,1:T(1,128)S(1)}, u32[]{:S(2)}) copy-start(s32[512,1]{0,1:T(1,128)S(1)} %get-tuple-element.21) | copy-start | bytes 6148
  39.2 39.6 %copy-start.12 = (s32[512,1]{0,1:T(1,128)}, s32[512,1]{0,1:T(1,128)S(1)}, u32[]{:S(2)}) copy-start(s32[512,1]{0,1:T(1,128)S(1)} %get-tuple-element.14) | copy-start | bytes 6148
  39.8 25.9 %collective-permute-start.5 = (bf16[128,256]{1,0:T(8,128)(2,1)S(1)}, bf16[128,256]{1,0:T(8,128)(2,1)S(1)}, u32[]{:S(2)}, u32[]{:S(2)}) collective-permute-start(bf16[128,256]{1,0:T(8,128)(2,1)S(1)} %gather_fusion.5), channel_id=1, source_target_pairs={{0,32},{1,33},{2,34},{3,35},{4,36},{5,37},{6,38},{7,39},{8,40},{9,... | collective-permute-start | bytes 196616 | tf_op jit(solution)/shard_map/ppermute | solution.py:10
  43.3 22.3 %collective-permute-start.6 = (bf16[128,256]{1,0:T(8,128)(2,1)S(1)}, bf16[128,256]{1,0:T(8,128)(2,1)S(1)}, u32[]{:S(2)}, u32[]{:S(2)}) collective-permute-start(bf16[128,256]{1,0:T(8,128)(2,1)S(1)} %gather_fusion.6), channel_id=1, source_target_pairs={{0,64},{1,65},{2,66},{3,67},{4,68},{5,69},{6,70},{7,71},{8,72},{9,... | collective-permute-start | bytes 196616 | tf_op jit(solution)/shard_map/ppermute | solution.py:10
  48.3 17.4 %collective-permute-start.7 = (bf16[128,256]{1,0:T(8,128)(2,1)S(1)}, bf16[128,256]{1,0:T(8,128)(2,1)S(1)}, u32[]{:S(2)}, u32[]{:S(2)}) collective-permute-start(bf16[128,256]{1,0:T(8,128)(2,1)S(1)} %gather_fusion.7), channel_id=1, source_target_pairs={{0,128},{1,129},{2,130},{3,131},{4,132},{5,133},{6,134},{7,135},{8... | collective-permute-start | bytes 196616 | tf_op jit(solution)/shard_map/ppermute | solution.py:10
  57.1 13.8 %collective-permute-start.8 = (bf16[128,256]{1,0:T(8,128)(2,1)S(1)}, bf16[128,256]{1,0:T(8,128)(2,1)S(1)}, u32[]{:S(2)}, u32[]{:S(2)}) collective-permute-start(bf16[128,256]{1,0:T(8,128)(2,1)S(1)} %gather_fusion.8), channel_id=1, source_target_pairs={{0,256},{1,257},{2,258},{3,259},{4,260},{5,261},{6,262},{7,263},{8... | collective-permute-start | bytes 196616 | tf_op jit(solution)/shard_map/ppermute | solution.py:10
  139.7 16.7 %collective-permute-start.9 = (bf16[128,256]{1,0:T(8,128)(2,1)S(1)}, bf16[128,256]{1,0:T(8,128)(2,1)S(1)}, u32[]{:S(2)}, u32[]{:S(2)}) collective-permute-start(bf16[128,256]{1,0:T(8,128)(2,1)S(1)} %get-tuple-element.11), channel_id=1, source_target_pairs={{0,1},{1,0},{2,3},{3,2},{4,5},{5,4},{6,7},{7,6},{8,9},{9,8},{10,11... | collective-permute-start | bytes 196616 | tf_op jit(solution)/shard_map/ppermute | solution.py:10
  145.3 16.1 %collective-permute-start.10 = (bf16[128,256]{1,0:T(8,128)(2,1)}, bf16[128,256]{1,0:T(8,128)(2,1)S(1)}, u32[]{:S(2)}, u32[]{:S(2)}) collective-permute-start(bf16[128,256]{1,0:T(8,128)(2,1)} %get-tuple-element.10), channel_id=1, source_target_pairs={{0,2},{1,3},{2,0},{3,1},{4,6},{5,7},{6,4},{7,5},{8,10},{9,11},{10,... | collective-permute-start | bytes 196616 | tf_op jit(solution)/shard_map/ppermute | solution.py:10
  147.3 16.1 %collective-permute-start.11 = (bf16[128,256]{1,0:T(8,128)(2,1)}, bf16[128,256]{1,0:T(8,128)(2,1)S(1)}, u32[]{:S(2)}, u32[]{:S(2)}) collective-permute-start(bf16[128,256]{1,0:T(8,128)(2,1)} %get-tuple-element.9), channel_id=1, source_target_pairs={{0,4},{1,5},{2,6},{3,7},{4,0},{5,1},{6,2},{7,3},{8,12},{9,13},{10,... | collective-permute-start | bytes 196616 | tf_op jit(solution)/shard_map/ppermute | solution.py:10
  150.3 15.2 %collective-permute-start.12 = (bf16[128,256]{1,0:T(8,128)(2,1)S(1)}, bf16[128,256]{1,0:T(8,128)(2,1)S(1)}, u32[]{:S(2)}, u32[]{:S(2)}) collective-permute-start(bf16[128,256]{1,0:T(8,128)(2,1)S(1)} %get-tuple-element.8), channel_id=1, source_target_pairs={{0,8},{1,9},{2,10},{3,11},{4,12},{5,13},{6,14},{7,15},{8,0},{9,1},... | collective-permute-start | bytes 196616 | tf_op jit(solution)/shard_map/ppermute | solution.py:10
  153.1 30.7 %collective-permute-start.13 = (bf16[128,256]{1,0:T(8,128)(2,1)S(1)}, bf16[128,256]{1,0:T(8,128)(2,1)S(1)}, u32[]{:S(2)}, u32[]{:S(2)}) collective-permute-start(bf16[128,256]{1,0:T(8,128)(2,1)S(1)} %get-tuple-element.7), channel_id=1, source_target_pairs={{0,16},{1,17},{2,18},{3,19},{4,20},{5,21},{6,22},{7,23},{8,24},{9,... | collective-permute-start | bytes 196616 | tf_op jit(solution)/shard_map/ppermute | solution.py:10
  156.4 29.1 %collective-permute-start.14 = (bf16[128,256]{1,0:T(8,128)(2,1)S(1)}, bf16[128,256]{1,0:T(8,128)(2,1)S(1)}, u32[]{:S(2)}, u32[]{:S(2)}) collective-permute-start(bf16[128,256]{1,0:T(8,128)(2,1)S(1)} %get-tuple-element.6), channel_id=1, source_target_pairs={{0,32},{1,33},{2,34},{3,35},{4,36},{5,37},{6,38},{7,39},{8,40},{9,... | collective-permute-start | bytes 196616 | tf_op jit(solution)/shard_map/ppermute | solution.py:10
  161.5 25.6 %collective-permute-start.15 = (bf16[128,256]{1,0:T(8,128)(2,1)S(1)}, bf16[128,256]{1,0:T(8,128)(2,1)}, u32[]{:S(2)}, u32[]{:S(2)}) collective-permute-start(bf16[128,256]{1,0:T(8,128)(2,1)S(1)} %get-tuple-element.5), channel_id=1, source_target_pairs={{0,64},{1,65},{2,66},{3,67},{4,68},{5,69},{6,70},{7,71},{8,72},{9,... | collective-permute-start | bytes 196616 | tf_op jit(solution)/shard_map/ppermute | solution.py:10
  163.4 25.5 %collective-permute-start.16 = (bf16[128,256]{1,0:T(8,128)(2,1)S(1)}, bf16[128,256]{1,0:T(8,128)(2,1)}, u32[]{:S(2)}, u32[]{:S(2)}) collective-permute-start(bf16[128,256]{1,0:T(8,128)(2,1)S(1)} %get-tuple-element.4), channel_id=1, source_target_pairs={{0,128},{1,129},{2,130},{3,131},{4,132},{5,133},{6,134},{7,135},{8... | collective-permute-start | bytes 196616 | tf_op jit(solution)/shard_map/ppermute | solution.py:10
  165.5 25.3 %collective-permute-start.17 = (bf16[128,256]{1,0:T(8,128)(2,1)S(1)}, bf16[128,256]{1,0:T(8,128)(2,1)S(1)}, u32[]{:S(2)}, u32[]{:S(2)}) collective-permute-start(bf16[128,256]{1,0:T(8,128)(2,1)S(1)} %get-tuple-element.3), channel_id=1, source_target_pairs={{0,256},{1,257},{2,258},{3,259},{4,260},{5,261},{6,262},{7,263},{8... | collective-permute-start | bytes 196616 | tf_op jit(solution)/shard_map/ppermute | solution.py:10
  (29 other events, 235.7 us)
Sparse Core Ops, SparseCore 0:
  153.2 456.2 all-reduce.1
where the time goes:
time: 626 us; the launch traced here: 621 us
  waiting for transfers between devices  422 us (67%)
  starting transfers between devices  80.5 us (13%)
  other arithmetic  66.8 us (11%)
  local copies, waits for them, and re-layouts  32.5 us (5%)
  between operations  16.3 us (3%)
    psum x1, waiting for transfers between devices, per_device(): total_grad = lax.psum(stacked, 'dom')  416 us
    ppermute x18, starting transfers between devices, swapped(): lax.ppermute(x, axis, [(i, i ^ 1 << apart) for i in range(lax.axis_size(a...  80.5 us
    scatter-add x10, other arithmetic, scatter_slots(): table.at[neighbors[:, slot]]  41.9 us
    gather x10, local copies, waits for them, and re-layouts, per_device(): extended[neighbors[:, slot]].astype(jnp.float32)  20.8 us
    scatter-add x9, other arithmetic, per_device(): local_grad = local_grad.at[boundary_rows[level]].add(returned)  15.2 us
  transfers between devices with their start and end apart: 19, of which 2 were waited for; matrix products, arithmetic and copies ran while one was open for 4% of the time, Pallas kernels for 0%

commit v1 on v0

v1 whole, which is shorter than its diff:
```python
import jax
import jax.numpy as jnp
from jax import lax
from jax.experimental import pallas as pl
from jax.experimental.pallas import tpu as pltpu
from jax.sharding import PartitionSpec as P

epsilon = 1e-06
f32 = jnp.float32
bf16 = jnp.bfloat16
FAST_BITS = 5
VMEM_LIMIT = 48 * 1024 * 1024
TRANSPOSED_LHS = (((0,), (0,)), ((), ()))
TRANSPOSED_RHS = (((1,), (1,)), ((), ()))


def dot(a, b, dims=(((1,), (0,)), ((), ()))):
    return lax.dot_general(a, b, dims, preferred_element_type=f32)


def call(body, outs, cost, *args, scratch=()):
    flops, moved = cost
    return pl.pallas_call(
        body,
        out_shape=outs,
        scratch_shapes=scratch,
        compiler_params=pltpu.CompilerParams(vmem_limit_bytes=VMEM_LIMIT),
        cost_estimate=pl.CostEstimate(flops=flops, bytes_accessed=moved, transcendentals=0),
    )(*args)


def shape(dims, dtype):
    return jax.ShapeDtypeStruct(dims, dtype)


def one_hot_columns(rows, node_dev):
    k = rows.shape[1]
    ids = lax.broadcasted_iota(jnp.int32, (node_dev, k), 0)
    return jnp.where(ids == rows, f32(1.0), f32(0.0)).astype(bf16)


def send_body(boundary_ref, features_ref, *sent_refs):
    node_dev = features_ref.shape[0]
    features = features_ref[...]
    for level, sent_ref in enumerate(sent_refs):
        pick = one_hot_columns(boundary_ref[level : level + 1, :], node_dev)
        sent_ref[...] = dot(pick, features, TRANSPOSED_LHS).astype(bf16)


def count_body(neighbors_ref, degree_ref, counts_ref):
    slots, node_dev = neighbors_ref.shape
    degree = degree_ref[...]
    live = [
        jnp.where(degree > slot, neighbors_ref[slot : slot + 1, :], -1) for slot in range(slots)
    ]
    step = 16
    ids = lax.broadcasted_iota(jnp.int32, (step, node_dev), 0)

    def block(at, carry):
        start = pl.multiple_of(at * step, step)
        here = ids + start
        total = jnp.zeros((step, node_dev), f32)
        for row in live:
            total = total + jnp.where(here == row, f32(1.0), f32(0.0))
        counts_ref[pl.ds(start, step), :] = total.astype(bf16)
        return carry

    lax.fori_loop(0, counts_ref.shape[0] // step, block, 0)


def layer_body(levels, *refs):
    counts_ref, features_ref, degree_ref, upstream_ref, w_self_ref, w_neigh_ref = refs[:6]
    received = refs[6 : 6 + levels]
    hidden_ref, stacked_ref, local_ref = refs[6 + levels : 9 + levels]
    returned = refs[9 + levels : 9 + 2 * levels]
    extended_ref = refs[9 + 2 * levels]
    node_dev, width = features_ref.shape
    bnd = received[0].shape[0]
    extended_ref[:node_dev, :] = features_ref[...]
    for level in range(levels):
        start = node_dev + level * bnd
        extended_ref[start : start + bnd, :] = received[level][...]
    degree = degree_ref[...].astype(f32)
    degree = jnp.transpose(jnp.broadcast_to(degree, (128, node_dev)))
    degree = jnp.concatenate([degree] * (width // 128), axis=1)
    agg = (dot(counts_ref[...], extended_ref[...], TRANSPOSED_LHS) / degree).astype(bf16)
    features = features_ref[...]
    pre_sum = dot(features, w_self_ref[...]) + dot(agg, w_neigh_ref[...])
    sigmoid_pre = jax.nn.sigmoid(pre_sum)
    hidden_ref[...] = (pre_sum * sigmoid_pre).astype(bf16)
    pre_grad = (
        upstream_ref[...].astype(f32) * sigmoid_pre * (1.0 + pre_sum * (1.0 - sigmoid_pre))
    ).astype(bf16)
    stacked_ref[:width, :] = dot(features, pre_grad, TRANSPOSED_LHS)
    stacked_ref[width:, :] = dot(agg, pre_grad, TRANSPOSED_LHS)
    share = (dot(pre_grad, w_neigh_ref[...], TRANSPOSED_RHS) / degree).astype(bf16)
    for level in range(levels):
        start = node_dev + level * bnd
        returned[level][...] = dot(counts_ref[start : start + bnd, :], share).astype(bf16)
    local_ref[...] = dot(pre_grad, w_self_ref[...], TRANSPOSED_RHS) + dot(
        counts_ref[:node_dev, :], share
    )


def collect_body(boundary_ref, local_ref, *refs):
    returned, node_grad_ref = refs[:-1], refs[-1]
    node_dev = local_ref.shape[0]
    total = local_ref[...]
    for level, rows_ref in enumerate(returned):
        pick = one_hot_columns(boundary_ref[level : level + 1, :], node_dev)
        total = total + dot(pick, rows_ref[...])
    node_grad_ref[...] = total.astype(bf16)


def sum_and_repeat_body(parts_ref, out_ref):
    total = parts_ref[0].astype(f32)
    for part in range(1, parts_ref.shape[0]):
        total = total + parts_ref[part].astype(f32)
    out_ref[...] = jnp.broadcast_to(total.astype(out_ref.dtype)[None], out_ref.shape)


def normalize_body(total_ref, out_ref):
    total = total_ref[...].astype(f32)
    mean = jnp.sum(total * total) / total.size
    out_ref[...] = total * lax.rsqrt(jnp.full((1, total.shape[1]), mean + epsilon, f32))


def bit_groups(devices, bits):
    mask = sum(1 << b for b in bits)
    groups = {}
    for i in range(devices):
        groups.setdefault(i & ~mask, []).append(i)
    return list(groups.values())


def exchange(x, groups):
    return lax.all_to_all(x, "dom", 0, 0, axis_index_groups=groups, tiled=True)


def total_over_devices(stacked, devices):
    bits = devices.bit_length() - 1
    rows, width = stacked.shape
    near = bit_groups(devices, range(FAST_BITS))
    far = bit_groups(devices, range(FAST_BITS, bits))
    n_near, n_far = len(near[0]), len(far[0])
    piece = rows // n_near
    parts = exchange(stacked.reshape(n_near, piece, width), near)
    partial = call(
        sum_and_repeat_body, shape((n_far, piece, width), bf16), (10**5, 10**6), parts
    )
    parts = exchange(partial, far)
    total = call(sum_and_repeat_body, shape((n_near, piece, width), bf16), (10**5, 10**6), parts)
    return exchange(total, near).reshape(rows, width)


def per_device(features, w_self, w_neigh, neighbors, degree, boundary, upstream):
    devices = lax.axis_size("dom")
    levels = devices.bit_length() - 1
    node_dev, width = features.shape
    boundary_rows = boundary[0]
    bnd = boundary_rows.shape[1]
    rows = node_dev + levels * bnd

    def swapped(x, level):
        return lax.ppermute(x, "dom", [(i, i ^ 1 << level) for i in range(devices)])

    sent = call(
        send_body, [shape((bnd, width), bf16)] * levels, (3 * 10**8, 10**6), boundary_rows, features
    )
    received = [swapped(x, level) for level, x in enumerate(sent)]
    degree_row = degree.reshape(1, node_dev)
    counts = call(
        count_body, shape((rows, node_dev), bf16), (10**7, 2 * 10**6), neighbors.T, degree_row
    )
    hidden, stacked, local, *returned = call(
        lambda *refs: layer_body(levels, *refs),
        [
            shape((node_dev, width), bf16),
            shape((2 * width, width), f32),
            shape((node_dev, width), f32),
        ]
        + [shape((bnd, width), bf16)] * levels,
        (10**9, 6 * 10**6),
        counts,
        features,
        degree_row,
        upstream,
        w_self,
        w_neigh,
        *received,
        scratch=[pltpu.VMEM((rows, width), bf16)],
    )
    back = [swapped(x, level) for level, x in enumerate(returned)]
    total = total_over_devices(stacked, devices)
    weight_step = call(normalize_body, shape(total.shape, f32), (10**6, 10**6), total)
    node_grad = call(
        collect_body, shape((node_dev, width), bf16), (3 * 10**8, 10**6), boundary_rows, local, *back
    )
    return (hidden, node_grad, weight_step)


def solution(mesh):
    return jax.shard_map(
        per_device,
        mesh=mesh,
        in_specs=(
            P("dom", None),
            P(),
            P(),
            P("dom", None),
            P("dom"),
            P("dom", None, None),
            P("dom", None),
        ),
        out_specs=(P("dom", None), P("dom", None), P()),
        check_vma=False,
    )
```

time: 626 us -> 149 us (0.24)
  the two profiles are of different devices: /device:TPU:1 before, /device:TPU:64 now
where the time goes in v1:
time: 149 us; the launch traced here: 148 us
  starting transfers between devices  83.2 us (56%)
  blocking collectives  40.1 us (27%)
  Pallas kernels  11.5 us (8%)
  waiting for transfers between devices  9.46 us (6%)
  local copies, waits for them, and re-layouts  3.09 us (2%)
    ppermute x18, starting transfers between devices, swapped(): return lax.ppermute(x, 'dom', [(i, i ^ 1 << level) for i in range(devices)])  79.3 us
    all_to_all x2, blocking collectives, exchange(): return lax.all_to_all(x, 'dom', 0, 0, axis_index_groups=groups, tiled=True)  40.1 us
    pallas_call x7, Pallas kernels, call(): pl.pallas_call(body, out_shape=outs, scratch_shapes=scratch, compiler_par...  11.5 us
    ppermute x18, waiting for transfers between devices, swapped(): return lax.ppermute(x, 'dom', [(i, i ^ 1 << level) for i in range(devices)])  9.46 us
    all_to_all x1, starting transfers between devices, exchange(): return lax.all_to_all(x, 'dom', 0, 0, axis_index_groups=groups, tiled=True)  3.87 us
    unnamed x15, local copies, waits for them, and re-layouts  3.09 us
  transfers between devices with their start and end apart: 19, of which 2 were waited for; matrix products, arithmetic and copies ran while one was open for 0% of the time, Pallas kernels for 4%

profile of v1, /device:TPU:64, one launch (start us, length us, event | category | flops | bytes accessed | tf_op | source)
XLA Modules:
  0.0 148.3 jit_solution(7659505250090178549)
XLA Ops:
  0.6 0.7 copy.12
  1.3 0.9 copy-done.2
  2.3 0.5 shard_map.95
  2.8 1.9 %collective-permute-start = (bf16[128,256]{1,0:T(8,128)(2,1)S(1)}, bf16[128,256]{1,0:T(8,128)(2,1)S(1)}, u32[]{:S(2)}, u32[]{:S(2)}) collective-permute-start(bf16[128,256]{1,0:T(8,128)(2,1)S(1)} %get-tuple-element.24), channel_id=1, source_target_pairs={{0,1},{1,0},{2,3},{3,2},{4,5},{5,4},{6,7},{7,6},{8,9},{9,8},{10,11... | collective-permute-start | bytes 196616 | tf_op jit(solution)/shard_map/ppermute | solution.py:165
  4.7 3.5 %collective-permute-start.1 = (bf16[128,256]{1,0:T(8,128)(2,1)S(1)}, bf16[128,256]{1,0:T(8,128)(2,1)S(1)}, u32[]{:S(2)}, u32[]{:S(2)}) collective-permute-start(bf16[128,256]{1,0:T(8,128)(2,1)S(1)} %get-tuple-element.25), channel_id=1, source_target_pairs={{0,2},{1,3},{2,0},{3,1},{4,6},{5,7},{6,4},{7,5},{8,10},{9,11},{10,... | collective-permute-start | bytes 196616 | tf_op jit(solution)/shard_map/ppermute | solution.py:165
  8.2 4.8 %collective-permute-start.2 = (bf16[128,256]{1,0:T(8,128)(2,1)S(1)}, bf16[128,256]{1,0:T(8,128)(2,1)S(1)}, u32[]{:S(2)}, u32[]{:S(2)}) collective-permute-start(bf16[128,256]{1,0:T(8,128)(2,1)S(1)} %get-tuple-element.26), channel_id=1, source_target_pairs={{0,4},{1,5},{2,6},{3,7},{4,0},{5,1},{6,2},{7,3},{8,12},{9,13},{10,... | collective-permute-start | bytes 196616 | tf_op jit(solution)/shard_map/ppermute | solution.py:165
  13.1 3.4 %collective-permute-start.3 = (bf16[128,256]{1,0:T(8,128)(2,1)S(1)}, bf16[128,256]{1,0:T(8,128)(2,1)S(1)}, u32[]{:S(2)}, u32[]{:S(2)}) collective-permute-start(bf16[128,256]{1,0:T(8,128)(2,1)S(1)} %get-tuple-element.27), channel_id=1, source_target_pairs={{0,8},{1,9},{2,10},{3,11},{4,12},{5,13},{6,14},{7,15},{8,0},{9,1},... | collective-permute-start | bytes 196616 | tf_op jit(solution)/shard_map/ppermute | solution.py:165
  16.5 4.6 %collective-permute-start.4 = (bf16[128,256]{1,0:T(8,128)(2,1)S(1)}, bf16[128,256]{1,0:T(8,128)(2,1)S(1)}, u32[]{:S(2)}, u32[]{:S(2)}) collective-permute-start(bf16[128,256]{1,0:T(8,128)(2,1)S(1)} %get-tuple-element.28), channel_id=1, source_target_pairs={{0,16},{1,17},{2,18},{3,19},{4,20},{5,21},{6,22},{7,23},{8,24},{9,... | collective-permute-start | bytes 196616 | tf_op jit(solution)/shard_map/ppermute | solution.py:165
  21.1 3.8 %collective-permute-start.5 = (bf16[128,256]{1,0:T(8,128)(2,1)S(1)}, bf16[128,256]{1,0:T(8,128)(2,1)S(1)}, u32[]{:S(2)}, u32[]{:S(2)}) collective-permute-start(bf16[128,256]{1,0:T(8,128)(2,1)S(1)} %get-tuple-element.29), channel_id=1, source_target_pairs={{0,32},{1,33},{2,34},{3,35},{4,36},{5,37},{6,38},{7,39},{8,40},{9,... | collective-permute-start | bytes 196616 | tf_op jit(solution)/shard_map/ppermute | solution.py:165
  25.0 1.9 %collective-permute-start.6 = (bf16[128,256]{1,0:T(8,128)(2,1)S(1)}, bf16[128,256]{1,0:T(8,128)(2,1)S(1)}, u32[]{:S(2)}, u32[]{:S(2)}) collective-permute-start(bf16[128,256]{1,0:T(8,128)(2,1)S(1)} %get-tuple-element.30), channel_id=1, source_target_pairs={{0,64},{1,65},{2,66},{3,67},{4,68},{5,69},{6,70},{7,71},{8,72},{9,... | collective-permute-start | bytes 196616 | tf_op jit(solution)/shard_map/ppermute | solution.py:165
  26.9 9.1 %collective-permute-start.7 = (bf16[128,256]{1,0:T(8,128)(2,1)S(1)}, bf16[128,256]{1,0:T(8,128)(2,1)S(1)}, u32[]{:S(2)}, u32[]{:S(2)}) collective-permute-start(bf16[128,256]{1,0:T(8,128)(2,1)S(1)} %get-tuple-element.31), channel_id=1, source_target_pairs={{0,128},{1,129},{2,130},{3,131},{4,132},{5,133},{6,134},{7,135},{8... | collective-permute-start | bytes 196616 | tf_op jit(solution)/shard_map/ppermute | solution.py:165
  36.0 9.7 %collective-permute-start.8 = (bf16[128,256]{1,0:T(8,128)(2,1)S(1)}, bf16[128,256]{1,0:T(8,128)(2,1)S(1)}, u32[]{:S(2)}, u32[]{:S(2)}) collective-permute-start(bf16[128,256]{1,0:T(8,128)(2,1)S(1)} %get-tuple-element.32), channel_id=1, source_target_pairs={{0,256},{1,257},{2,258},{3,259},{4,260},{5,261},{6,262},{7,263},{8... | collective-permute-start | bytes 196616 | tf_op jit(solution)/shard_map/ppermute | solution.py:165
  45.7 0.7 copy-done
  46.4 0.7 copy-done.1
  47.1 4.3 %shard_map.94.refs_0_ = bf16[1664,512]{1,0:T(8,128)(2,1)S(1)} custom-call(s32[10,512]{1,0:T(8,128)S(1)} %bitcast.11, s32[1,512]{1,0:T(1,128)S(1)} %bitcast.12), custom_call_target="tpu_custom_call" | custom-call | flops 10000000 | bytes 2000000 | tf_op jit(solution)/shard_map/pallas_call | solution.py:23
  51.5 3.3 %shard_map.96 = (bf16[512,256]{1,0:T(8,128)(2,1)}, f32[512,256]{1,0:T(8,128)S(1)}, f32[512,256]{1,0:T(8,128)S(1)}, bf16[128,256]{1,0:T(8,128)(2,1)S(1)}, bf16[12...) custom-call(bf16[1664,512]{1,0:T(8,128)(2,1)S(1)} %shard_map.94.refs, ...), custom_call_target="tpu_custom_call" | custom-call | flops 1000000000 | bytes 6000000 | tf_op jit(solution)/shard_map/pallas_call | solution.py:23
  54.9 14.2 %all_to_all.15.parts_ref = f32[32,16,256]{2,1,0:T(8,128)S(1)} all-to-all(f32[32,16,256]{2,1,0:T(8,128)S(1)} %bitcast.8), channel_id=1, replica_groups={{0,1,2,3,4,5,6,7,8,9,10,11,12,13,14,15,16,17,18,19,20,21,22,23,24,25,26..., dimensions={0} | all-to-all | bytes 1048576 | tf_op jit(solution)/shard_map/all_to_all | solution.py:137
  69.1 25.9 %all_to_all.16.parts_ref = bf16[16,16,256]{2,1,0:T(8,128)(2,1)S(1)} all-to-all(bf16[16,16,256]{2,1,0:T(8,128)(2,1)S(1)} %shard_map.98), channel_id=1, replica_groups={{0,32,64,96,128,160,192,224,256,288,320,352,384,416,448,480},{1,33,65,9..., dimensions={0} | all-to-all | bytes 262144 | tf_op jit(solution)/shard_map/all_to_all | solution.py:137
  95.0 0.7 shard_map.99
  95.8 3.9 %all-to-all-start.2 = ((bf16[32,16,256]{2,1,0:T(8,128)(2,1)}), bf16[32,16,256]{2,1,0:T(8,128)(2,1)S(1)}, u32[]{:S(2)}, u32[]{:S(2)}) async-start(bf16[32,16,256]{2,1,0:T(8,128)(2,1)} %shard_map.99), calls=%async_computation.2 | async-start | bytes 524288 | tf_op jit(solution)/shard_map/all_to_all | solution.py:137
  99.6 2.1 %collective-permute-start.9 = (bf16[128,256]{1,0:T(8,128)(2,1)S(1)}, bf16[128,256]{1,0:T(8,128)(2,1)S(1)}, u32[]{:S(2)}, u32[]{:S(2)}) collective-permute-start(bf16[128,256]{1,0:T(8,128)(2,1)S(1)} %get-tuple-element.35), channel_id=1, source_target_pairs={{0,1},{1,0},{2,3},{3,2},{4,5},{5,4},{6,7},{7,6},{8,9},{9,8},{10,11... | collective-permute-start | bytes 196616 | tf_op jit(solution)/shard_map/ppermute | solution.py:165
  101.7 3.6 %collective-permute-start.10 = (bf16[128,256]{1,0:T(8,128)(2,1)S(1)}, bf16[128,256]{1,0:T(8,128)(2,1)S(1)}, u32[]{:S(2)}, u32[]{:S(2)}) collective-permute-start(bf16[128,256]{1,0:T(8,128)(2,1)S(1)} %get-tuple-element.36), channel_id=1, source_target_pairs={{0,2},{1,3},{2,0},{3,1},{4,6},{5,7},{6,4},{7,5},{8,10},{9,11},{10,... | collective-permute-start | bytes 196616 | tf_op jit(solution)/shard_map/ppermute | solution.py:165
  105.3 4.6 %collective-permute-start.11 = (bf16[128,256]{1,0:T(8,128)(2,1)S(1)}, bf16[128,256]{1,0:T(8,128)(2,1)S(1)}, u32[]{:S(2)}, u32[]{:S(2)}) collective-permute-start(bf16[128,256]{1,0:T(8,128)(2,1)S(1)} %get-tuple-element.37), channel_id=1, source_target_pairs={{0,4},{1,5},{2,6},{3,7},{4,0},{5,1},{6,2},{7,3},{8,12},{9,13},{10,... | collective-permute-start | bytes 196616 | tf_op jit(solution)/shard_map/ppermute | solution.py:165
  109.9 3.4 %collective-permute-start.12 = (bf16[128,256]{1,0:T(8,128)(2,1)S(1)}, bf16[128,256]{1,0:T(8,128)(2,1)S(1)}, u32[]{:S(2)}, u32[]{:S(2)}) collective-permute-start(bf16[128,256]{1,0:T(8,128)(2,1)S(1)} %get-tuple-element.38), channel_id=1, source_target_pairs={{0,8},{1,9},{2,10},{3,11},{4,12},{5,13},{6,14},{7,15},{8,0},{9,1},... | collective-permute-start | bytes 196616 | tf_op jit(solution)/shard_map/ppermute | solution.py:165
  113.4 4.7 %collective-permute-start.13 = (bf16[128,256]{1,0:T(8,128)(2,1)S(1)}, bf16[128,256]{1,0:T(8,128)(2,1)S(1)}, u32[]{:S(2)}, u32[]{:S(2)}) collective-permute-start(bf16[128,256]{1,0:T(8,128)(2,1)S(1)} %get-tuple-element.39), channel_id=1, source_target_pairs={{0,16},{1,17},{2,18},{3,19},{4,20},{5,21},{6,22},{7,23},{8,24},{9,... | collective-permute-start | bytes 196616 | tf_op jit(solution)/shard_map/ppermute | solution.py:165
  118.1 2.9 %collective-permute-start.14 = (bf16[128,256]{1,0:T(8,128)(2,1)S(1)}, bf16[128,256]{1,0:T(8,128)(2,1)S(1)}, u32[]{:S(2)}, u32[]{:S(2)}) collective-permute-start(bf16[128,256]{1,0:T(8,128)(2,1)S(1)} %get-tuple-element.40), channel_id=1, source_target_pairs={{0,32},{1,33},{2,34},{3,35},{4,36},{5,37},{6,38},{7,39},{8,40},{9,... | collective-permute-start | bytes 196616 | tf_op jit(solution)/shard_map/ppermute | solution.py:165
  121.0 3.1 %collective-permute-start.15 = (bf16[128,256]{1,0:T(8,128)(2,1)S(1)}, bf16[128,256]{1,0:T(8,128)(2,1)S(1)}, u32[]{:S(2)}, u32[]{:S(2)}) collective-permute-start(bf16[128,256]{1,0:T(8,128)(2,1)S(1)} %get-tuple-element.41), channel_id=1, source_target_pairs={{0,64},{1,65},{2,66},{3,67},{4,68},{5,69},{6,70},{7,71},{8,72},{9,... | collective-permute-start | bytes 196616 | tf_op jit(solution)/shard_map/ppermute | solution.py:165
  124.2 4.0 %collective-permute-start.16 = (bf16[128,256]{1,0:T(8,128)(2,1)S(1)}, bf16[128,256]{1,0:T(8,128)(2,1)S(1)}, u32[]{:S(2)}, u32[]{:S(2)}) collective-permute-start(bf16[128,256]{1,0:T(8,128)(2,1)S(1)} %get-tuple-element.42), channel_id=1, source_target_pairs={{0,128},{1,129},{2,130},{3,131},{4,132},{5,133},{6,134},{7,135},{8... | collective-permute-start | bytes 196616 | tf_op jit(solution)/shard_map/ppermute | solution.py:165
  128.1 8.2 %collective-permute-start.17 = (bf16[128,256]{1,0:T(8,128)(2,1)S(1)}, bf16[128,256]{1,0:T(8,128)(2,1)S(1)}, u32[]{:S(2)}, u32[]{:S(2)}) collective-permute-start(bf16[128,256]{1,0:T(8,128)(2,1)S(1)} %get-tuple-element.43), channel_id=1, source_target_pairs={{0,256},{1,257},{2,258},{3,259},{4,260},{5,261},{6,262},{7,263},{8... | collective-permute-start | bytes 196616 | tf_op jit(solution)/shard_map/ppermute | solution.py:165
  136.4 9.4 %collective-permute-done.17.refs_8_ = bf16[128,256]{1,0:T(8,128)(2,1)S(1)} collective-permute-done((bf16[128,256]{1,0:T(8,128)(2,1)S(1)}, bf16[128,256]{1,0:T(8,128)(2,1)S(1)}, u32[]{:S(2)}, u32[]{:S(2)}) %collective-permute-start.17) | collective-permute-done | bytes 65568 | tf_op jit(solution)/shard_map/ppermute | solution.py:165
  145.7 1.5 shard_map.97
  147.2 1.1 shard_map.100
  (30 shorter events, 0.2 us)
Async XLA Ops:
  1.3 0.9 copy-start.2
  2.3 49.2 %copy-start.3 = (bf16[512,256]{1,0:T(8,128)(2,1)S(1)}, bf16[512,256]{1,0:T(8,128)(2,1)}, u32[]{:S(2)}) copy-start(bf16[512,256]{1,0:T(8,128)(2,1)} %refs_1_.1) | copy-start | bytes 786436
  2.3 49.2 %copy-start.4 = (bf16[512,256]{1,0:T(8,128)(2,1)S(1)}, bf16[512,256]{1,0:T(8,128)(2,1)}, u32[]{:S(2)}) copy-start(bf16[512,256]{1,0:T(8,128)(2,1)} %refs_3_.1) | copy-start | bytes 786436
  2.3 49.2 %copy-start.5 = (bf16[256,256]{1,0:T(8,128)(2,1)S(1)}, bf16[256,256]{1,0:T(8,128)(2,1)}, u32[]{:S(2)}) copy-start(bf16[256,256]{1,0:T(8,128)(2,1)} %refs_4_.1) | copy-start | bytes 393220
  2.3 49.2 %copy-start.6 = (bf16[256,256]{1,0:T(8,128)(2,1)S(1)}, bf16[256,256]{1,0:T(8,128)(2,1)}, u32[]{:S(2)}) copy-start(bf16[256,256]{1,0:T(8,128)(2,1)} %refs_5_.1) | copy-start | bytes 393220
  2.8 18.3 %collective-permute-start = (bf16[128,256]{1,0:T(8,128)(2,1)S(1)}, bf16[128,256]{1,0:T(8,128)(2,1)S(1)}, u32[]{:S(2)}, u32[]{:S(2)}) collective-permute-start(bf16[128,256]{1,0:T(8,128)(2,1)S(1)} %get-tuple-element.24), channel_id=1, source_target_pairs={{0,1},{1,0},{2,3},{3,2},{4,5},{5,4},{6,7},{7,6},{8,9},{9,8},{10,11... | collective-permute-start | bytes 196616 | tf_op jit(solution)/shard_map/ppermute | solution.py:165
  4.7 20.2 %collective-permute-start.1 = (bf16[128,256]{1,0:T(8,128)(2,1)S(1)}, bf16[128,256]{1,0:T(8,128)(2,1)S(1)}, u32[]{:S(2)}, u32[]{:S(2)}) collective-permute-start(bf16[128,256]{1,0:T(8,128)(2,1)S(1)} %get-tuple-element.25), channel_id=1, source_target_pairs={{0,2},{1,3},{2,0},{3,1},{4,6},{5,7},{6,4},{7,5},{8,10},{9,11},{10,... | collective-permute-start | bytes 196616 | tf_op jit(solution)/shard_map/ppermute | solution.py:165
  8.2 18.7 %collective-permute-start.2 = (bf16[128,256]{1,0:T(8,128)(2,1)S(1)}, bf16[128,256]{1,0:T(8,128)(2,1)S(1)}, u32[]{:S(2)}, u32[]{:S(2)}) collective-permute-start(bf16[128,256]{1,0:T(8,128)(2,1)S(1)} %get-tuple-element.26), channel_id=1, source_target_pairs={{0,4},{1,5},{2,6},{3,7},{4,0},{5,1},{6,2},{7,3},{8,12},{9,13},{10,... | collective-permute-start | bytes 196616 | tf_op jit(solution)/shard_map/ppermute | solution.py:165
  13.1 23.0 %collective-permute-start.3 = (bf16[128,256]{1,0:T(8,128)(2,1)S(1)}, bf16[128,256]{1,0:T(8,128)(2,1)S(1)}, u32[]{:S(2)}, u32[]{:S(2)}) collective-permute-start(bf16[128,256]{1,0:T(8,128)(2,1)S(1)} %get-tuple-element.27), channel_id=1, source_target_pairs={{0,8},{1,9},{2,10},{3,11},{4,12},{5,13},{6,14},{7,15},{8,0},{9,1},... | collective-permute-start | bytes 196616 | tf_op jit(solution)/shard_map/ppermute | solution.py:165
  16.5 34.9 %collective-permute-start.4 = (bf16[128,256]{1,0:T(8,128)(2,1)S(1)}, bf16[128,256]{1,0:T(8,128)(2,1)S(1)}, u32[]{:S(2)}, u32[]{:S(2)}) collective-permute-start(bf16[128,256]{1,0:T(8,128)(2,1)S(1)} %get-tuple-element.28), channel_id=1, source_target_pairs={{0,16},{1,17},{2,18},{3,19},{4,20},{5,21},{6,22},{7,23},{8,24},{9,... | collective-permute-start | bytes 196616 | tf_op jit(solution)/shard_map/ppermute | solution.py:165
  21.1 30.3 %collective-permute-start.5 = (bf16[128,256]{1,0:T(8,128)(2,1)S(1)}, bf16[128,256]{1,0:T(8,128)(2,1)S(1)}, u32[]{:S(2)}, u32[]{:S(2)}) collective-permute-start(bf16[128,256]{1,0:T(8,128)(2,1)S(1)} %get-tuple-element.29), channel_id=1, source_target_pairs={{0,32},{1,33},{2,34},{3,35},{4,36},{5,37},{6,38},{7,39},{8,40},{9,... | collective-permute-start | bytes 196616 | tf_op jit(solution)/shard_map/ppermute | solution.py:165
  25.0 26.5 %collective-permute-start.6 = (bf16[128,256]{1,0:T(8,128)(2,1)S(1)}, bf16[128,256]{1,0:T(8,128)(2,1)S(1)}, u32[]{:S(2)}, u32[]{:S(2)}) collective-permute-start(bf16[128,256]{1,0:T(8,128)(2,1)S(1)} %get-tuple-element.30), channel_id=1, source_target_pairs={{0,64},{1,65},{2,66},{3,67},{4,68},{5,69},{6,70},{7,71},{8,72},{9,... | collective-permute-start | bytes 196616 | tf_op jit(solution)/shard_map/ppermute | solution.py:165
  26.9 24.5 %collective-permute-start.7 = (bf16[128,256]{1,0:T(8,128)(2,1)S(1)}, bf16[128,256]{1,0:T(8,128)(2,1)S(1)}, u32[]{:S(2)}, u32[]{:S(2)}) collective-permute-start(bf16[128,256]{1,0:T(8,128)(2,1)S(1)} %get-tuple-element.31), channel_id=1, source_target_pairs={{0,128},{1,129},{2,130},{3,131},{4,132},{5,133},{6,134},{7,135},{8... | collective-permute-start | bytes 196616 | tf_op jit(solution)/shard_map/ppermute | solution.py:165
  36.0 15.5 %collective-permute-start.8 = (bf16[128,256]{1,0:T(8,128)(2,1)S(1)}, bf16[128,256]{1,0:T(8,128)(2,1)S(1)}, u32[]{:S(2)}, u32[]{:S(2)}) collective-permute-start(bf16[128,256]{1,0:T(8,128)(2,1)S(1)} %get-tuple-element.32), channel_id=1, source_target_pairs={{0,256},{1,257},{2,258},{3,259},{4,260},{5,261},{6,262},{7,263},{8... | collective-permute-start | bytes 196616 | tf_op jit(solution)/shard_map/ppermute | solution.py:165
  45.7 0.8 copy-start
  46.4 0.7 copy-start.1
  95.8 51.4 %all-to-all-start.2 = ((bf16[32,16,256]{2,1,0:T(8,128)(2,1)}), bf16[32,16,256]{2,1,0:T(8,128)(2,1)S(1)}, u32[]{:S(2)}, u32[]{:S(2)}) async-start(bf16[32,16,256]{2,1,0:T(8,128)(2,1)} %shard_map.99), calls=%async_computation.2 | async-start | bytes 524288 | tf_op jit(solution)/shard_map/all_to_all | solution.py:137
  99.6 18.4 %collective-permute-start.9 = (bf16[128,256]{1,0:T(8,128)(2,1)S(1)}, bf16[128,256]{1,0:T(8,128)(2,1)S(1)}, u32[]{:S(2)}, u32[]{:S(2)}) collective-permute-start(bf16[128,256]{1,0:T(8,128)(2,1)S(1)} %get-tuple-element.35), channel_id=1, source_target_pairs={{0,1},{1,0},{2,3},{3,2},{4,5},{5,4},{6,7},{7,6},{8,9},{9,8},{10,11... | collective-permute-start | bytes 196616 | tf_op jit(solution)/shard_map/ppermute | solution.py:165
  101.7 19.3 %collective-permute-start.10 = (bf16[128,256]{1,0:T(8,128)(2,1)S(1)}, bf16[128,256]{1,0:T(8,128)(2,1)S(1)}, u32[]{:S(2)}, u32[]{:S(2)}) collective-permute-start(bf16[128,256]{1,0:T(8,128)(2,1)S(1)} %get-tuple-element.36), channel_id=1, source_target_pairs={{0,2},{1,3},{2,0},{3,1},{4,6},{5,7},{6,4},{7,5},{8,10},{9,11},{10,... | collective-permute-start | bytes 196616 | tf_op jit(solution)/shard_map/ppermute | solution.py:165
  105.3 18.8 %collective-permute-start.11 = (bf16[128,256]{1,0:T(8,128)(2,1)S(1)}, bf16[128,256]{1,0:T(8,128)(2,1)S(1)}, u32[]{:S(2)}, u32[]{:S(2)}) collective-permute-start(bf16[128,256]{1,0:T(8,128)(2,1)S(1)} %get-tuple-element.37), channel_id=1, source_target_pairs={{0,4},{1,5},{2,6},{3,7},{4,0},{5,1},{6,2},{7,3},{8,12},{9,13},{10,... | collective-permute-start | bytes 196616 | tf_op jit(solution)/shard_map/ppermute | solution.py:165
  109.9 18.2 %collective-permute-start.12 = (bf16[128,256]{1,0:T(8,128)(2,1)S(1)}, bf16[128,256]{1,0:T(8,128)(2,1)S(1)}, u32[]{:S(2)}, u32[]{:S(2)}) collective-permute-start(bf16[128,256]{1,0:T(8,128)(2,1)S(1)} %get-tuple-element.38), channel_id=1, source_target_pairs={{0,8},{1,9},{2,10},{3,11},{4,12},{5,13},{6,14},{7,15},{8,0},{9,1},... | collective-permute-start | bytes 196616 | tf_op jit(solution)/shard_map/ppermute | solution.py:165
  113.4 23.0 %collective-permute-start.13 = (bf16[128,256]{1,0:T(8,128)(2,1)S(1)}, bf16[128,256]{1,0:T(8,128)(2,1)S(1)}, u32[]{:S(2)}, u32[]{:S(2)}) collective-permute-start(bf16[128,256]{1,0:T(8,128)(2,1)S(1)} %get-tuple-element.39), channel_id=1, source_target_pairs={{0,16},{1,17},{2,18},{3,19},{4,20},{5,21},{6,22},{7,23},{8,24},{9,... | collective-permute-start | bytes 196616 | tf_op jit(solution)/shard_map/ppermute | solution.py:165
  118.1 18.3 %collective-permute-start.14 = (bf16[128,256]{1,0:T(8,128)(2,1)S(1)}, bf16[128,256]{1,0:T(8,128)(2,1)S(1)}, u32[]{:S(2)}, u32[]{:S(2)}) collective-permute-start(bf16[128,256]{1,0:T(8,128)(2,1)S(1)} %get-tuple-element.40), channel_id=1, source_target_pairs={{0,32},{1,33},{2,34},{3,35},{4,36},{5,37},{6,38},{7,39},{8,40},{9,... | collective-permute-start | bytes 196616 | tf_op jit(solution)/shard_map/ppermute | solution.py:165
  121.0 15.3 %collective-permute-start.15 = (bf16[128,256]{1,0:T(8,128)(2,1)S(1)}, bf16[128,256]{1,0:T(8,128)(2,1)S(1)}, u32[]{:S(2)}, u32[]{:S(2)}) collective-permute-start(bf16[128,256]{1,0:T(8,128)(2,1)S(1)} %get-tuple-element.41), channel_id=1, source_target_pairs={{0,64},{1,65},{2,66},{3,67},{4,68},{5,69},{6,70},{7,71},{8,72},{9,... | collective-permute-start | bytes 196616 | tf_op jit(solution)/shard_map/ppermute | solution.py:165
  124.2 12.2 %collective-permute-start.16 = (bf16[128,256]{1,0:T(8,128)(2,1)S(1)}, bf16[128,256]{1,0:T(8,128)(2,1)S(1)}, u32[]{:S(2)}, u32[]{:S(2)}) collective-permute-start(bf16[128,256]{1,0:T(8,128)(2,1)S(1)} %get-tuple-element.42), channel_id=1, source_target_pairs={{0,128},{1,129},{2,130},{3,131},{4,132},{5,133},{6,134},{7,135},{8... | collective-permute-start | bytes 196616 | tf_op jit(solution)/shard_map/ppermute | solution.py:165
  128.1 17.6 %collective-permute-start.17 = (bf16[128,256]{1,0:T(8,128)(2,1)S(1)}, bf16[128,256]{1,0:T(8,128)(2,1)S(1)}, u32[]{:S(2)}, u32[]{:S(2)}) collective-permute-start(bf16[128,256]{1,0:T(8,128)(2,1)S(1)} %get-tuple-element.43), channel_id=1, source_target_pairs={{0,256},{1,257},{2,258},{3,259},{4,260},{5,261},{6,262},{7,263},{8... | collective-permute-start | bytes 196616 | tf_op jit(solution)/shard_map/ppermute | solution.py:165

commit v2 on v1

--- a/solution.py
+++ b/solution.py
@@ -39,12 +39,42 @@
     return jnp.where(ids == rows, f32(1.0), f32(0.0)).astype(bf16)
 
 
-def send_body(boundary_ref, features_ref, *sent_refs):
+def core_index():
+    return lax.rem(lax.axis_index("dom"), 2)
+
+
+def level_of(pair, core):
+    return jnp.where(core == 0, pair[0], pair[1])
+
+
+def send_body(pairs, boundary_ref, features_ref, own_ref, lent_ref):
     node_dev = features_ref.shape[0]
+    bnd = boundary_ref.shape[1]
+    core = core_index()
     features = features_ref[...]
-    for level, sent_ref in enumerate(sent_refs):
-        pick = one_hot_columns(boundary_ref[level : level + 1, :], node_dev)
-        sent_ref[...] = dot(pick, features, TRANSPOSED_LHS).astype(bf16)
+
+    def rows_of(level):
+        pick = one_hot_columns(boundary_ref[pl.ds(level, 1), :], node_dev)
+        return dot(pick, features, TRANSPOSED_LHS).astype(bf16)
+
+    lent_ref[:bnd, :] = rows_of(0)
+    for k, pair in enumerate(pairs):
+        lent_ref[(k + 1) * bnd : (k + 2) * bnd, :] = rows_of(level_of(pair, 1 - core))
+        own_ref[k * bnd : (k + 1) * bnd, :] = rows_of(level_of(pair, core))
+
+
+def load_body(own_ref, borrowed_ref, *load_refs):
+    bnd = load_refs[0].shape[0] // 2
+    for k, load_ref in enumerate(load_refs):
+        load_ref[:bnd, :] = own_ref[k * bnd : (k + 1) * bnd, :]
+        load_ref[bnd:, :] = borrowed_ref[(k + 1) * bnd : (k + 2) * bnd, :]
+
+
+def unload_body(*refs):
+    load_refs, lent_ref = refs[:-1], refs[-1]
+    bnd = load_refs[0].shape[0] // 2
+    for k, load_ref in enumerate(load_refs):
+        lent_ref[k * bnd : (k + 1) * bnd, :] = load_ref[bnd:, :]
 
 
 def count_body(neighbors_ref, degree_ref, counts_ref):
@@ -53,33 +83,42 @@
     live = [
         jnp.where(degree > slot, neighbors_ref[slot : slot + 1, :], -1) for slot in range(slots)
     ]
-    step = 16
+    tile, step = 128, 16
     ids = lax.broadcasted_iota(jnp.int32, (step, node_dev), 0)
 
     def block(at, carry):
-        start = pl.multiple_of(at * step, step)
-        here = ids + start
-        total = jnp.zeros((step, node_dev), f32)
-        for row in live:
-            total = total + jnp.where(here == row, f32(1.0), f32(0.0))
-        counts_ref[pl.ds(start, step), :] = total.astype(bf16)
+        start = pl.multiple_of(at * tile, tile)
+        near = [
+            jnp.broadcast_to(row - start, (step, node_dev)).astype(f32).astype(bf16) for row in live
+        ]
+        for part in range(tile // step):
+            here = (ids + part * step).astype(f32).astype(bf16)
+            total = jnp.zeros((step, node_dev), bf16)
+            for row in near:
+                total = total + jnp.where(here == row, bf16(1.0), bf16(0.0))
+            counts_ref[pl.ds(start + part * step, step), :] = total
         return carry
 
-    lax.fori_loop(0, counts_ref.shape[0] // step, block, 0)
-
-
-def layer_body(levels, *refs):
+    lax.fori_loop(0, counts_ref.shape[0] // tile, block, 0)
+
+
+def layer_body(pairs, *refs):
     counts_ref, features_ref, degree_ref, upstream_ref, w_self_ref, w_neigh_ref = refs[:6]
-    received = refs[6 : 6 + levels]
-    hidden_ref, stacked_ref, local_ref = refs[6 + levels : 9 + levels]
-    returned = refs[9 + levels : 9 + 2 * levels]
-    extended_ref = refs[9 + 2 * levels]
+    borrowed_ref, kept_ref = refs[6:8]
+    loads = refs[8 : 8 + len(pairs)]
+    hidden_ref, stacked_ref, local_ref, own_ref, lent_ref, extended_ref = refs[8 + len(pairs) :]
     node_dev, width = features_ref.shape
-    bnd = received[0].shape[0]
+    bnd = loads[0].shape[0] // 2
+    core = core_index()
+
+    def level_rows(level):
+        return pl.ds(pl.multiple_of(node_dev + level * bnd, bnd), bnd)
+
     extended_ref[:node_dev, :] = features_ref[...]
-    for level in range(levels):
-        start = node_dev + level * bnd
-        extended_ref[start : start + bnd, :] = received[level][...]
+    extended_ref[node_dev : node_dev + bnd, :] = borrowed_ref[:bnd, :]
+    for k, pair in enumerate(pairs):
+        extended_ref[level_rows(level_of(pair, core)), :] = loads[k][:bnd, :]
+        extended_ref[level_rows(level_of(pair, 1 - core)), :] = kept_ref[k * bnd : (k + 1) * bnd, :]
     degree = degree_ref[...].astype(f32)
     degree = jnp.transpose(jnp.broadcast_to(degree, (128, node_dev)))
     degree = jnp.concatenate([degree] * (width // 128), axis=1)
@@ -94,21 +133,32 @@
     stacked_ref[:width, :] = dot(features, pre_grad, TRANSPOSED_LHS)
     stacked_ref[width:, :] = dot(agg, pre_grad, TRANSPOSED_LHS)
     share = (dot(pre_grad, w_neigh_ref[...], TRANSPOSED_RHS) / degree).astype(bf16)
-    for level in range(levels):
-        start = node_dev + level * bnd
-        returned[level][...] = dot(counts_ref[start : start + bnd, :], share).astype(bf16)
+    lent_ref[:bnd, :] = dot(counts_ref[node_dev : node_dev + bnd, :], share).astype(bf16)
+    for k, pair in enumerate(pairs):
+        lent_ref[(k + 1) * bnd : (k + 2) * bnd, :] = dot(
+            counts_ref[level_rows(level_of(pair, 1 - core)), :], share
+        ).astype(bf16)
+        own_ref[k * bnd : (k + 1) * bnd, :] = dot(
+            counts_ref[level_rows(level_of(pair, core)), :], share
+        ).astype(bf16)
     local_ref[...] = dot(pre_grad, w_self_ref[...], TRANSPOSED_RHS) + dot(
         counts_ref[:node_dev, :], share
     )
 
 
-def collect_body(boundary_ref, local_ref, *refs):
-    returned, node_grad_ref = refs[:-1], refs[-1]
+def collect_body(pairs, boundary_ref, local_ref, borrowed_ref, kept_ref, *refs):
+    loads, node_grad_ref = refs[:-1], refs[-1]
     node_dev = local_ref.shape[0]
-    total = local_ref[...]
-    for level, rows_ref in enumerate(returned):
-        pick = one_hot_columns(boundary_ref[level : level + 1, :], node_dev)
-        total = total + dot(pick, rows_ref[...])
+    bnd = boundary_ref.shape[1]
+    core = core_index()
+
+    def added(level, rows):
+        return dot(one_hot_columns(boundary_ref[pl.ds(level, 1), :], node_dev), rows)
+
+    total = local_ref[...] + added(0, borrowed_ref[:bnd, :])
+    for k, pair in enumerate(pairs):
+        total = total + added(level_of(pair, core), loads[k][:bnd, :])
+        total = total + added(level_of(pair, 1 - core), kept_ref[k * bnd : (k + 1) * bnd, :])
     node_grad_ref[...] = total.astype(bf16)
 
 
@@ -153,33 +203,59 @@
     return exchange(total, near).reshape(rows, width)
 
 
+def level_pairs(levels):
+    pairs = []
+    for top in range(levels - 1, 1, -2):
+        pairs.append((top, top - 1) if not pairs else (top - 1, top))
+    return pairs
+
+
 def per_device(features, w_self, w_neigh, neighbors, degree, boundary, upstream):
     devices = lax.axis_size("dom")
     levels = devices.bit_length() - 1
+    pairs = level_pairs(levels)
     node_dev, width = features.shape
     boundary_rows = boundary[0]
     bnd = boundary_rows.shape[1]
     rows = node_dev + levels * bnd
-
-    def swapped(x, level):
-        return lax.ppermute(x, "dom", [(i, i ^ 1 << level) for i in range(devices)])
-
-    sent = call(
-        send_body, [shape((bnd, width), bf16)] * levels, (3 * 10**8, 10**6), boundary_rows, features
-    )
-    received = [swapped(x, level) for level, x in enumerate(sent)]
+    own_shape = shape((len(pairs) * bnd, width), bf16)
+    lent_shape = shape(((len(pairs) + 1) * bnd, width), bf16)
+    load_shape = shape((2 * bnd, width), bf16)
+
+    def other_core(x):
+        return lax.ppermute(x, "dom", [(i, i ^ 1) for i in range(devices)])
+
+    def carried(own, lent):
+        borrowed = other_core(lent)
+        loads = call(load_body, [load_shape] * len(pairs), (10**5, 10**6), own, borrowed)
+        loads = [
+            lax.ppermute(x, "dom", [(i, i ^ 1 << pair[i % 2]) for i in range(devices)])
+            for x, pair in zip(loads, pairs)
+        ]
+        kept = other_core(call(unload_body, own_shape, (10**5, 10**6), *loads))
+        return borrowed, kept, *loads
+
+    own, lent = call(
+        lambda *refs: send_body(pairs, *refs),
+        [own_shape, lent_shape],
+        (3 * 10**8, 10**6),
+        boundary_rows,
+        features,
+    )
+    received = carried(own, lent)
     degree_row = degree.reshape(1, node_dev)
     counts = call(
         count_body, shape((rows, node_dev), bf16), (10**7, 2 * 10**6), neighbors.T, degree_row
     )
-    hidden, stacked, local, *returned = call(
-        lambda *refs: layer_body(levels, *refs),
+    hidden, stacked, local, own, lent = call(
+        lambda *refs: layer_body(pairs, *refs),
         [
             shape((node_dev, width), bf16),
             shape((2 * width, width), f32),
             shape((node_dev, width), f32),
-        ]
-        + [shape((bnd, width), bf16)] * levels,
+            own_shape,
+            lent_shape,
+        ],
         (10**9, 6 * 10**6),
         counts,
         features,
@@ -190,11 +266,16 @@
         *received,
         scratch=[pltpu.VMEM((rows, width), bf16)],
     )
-    back = [swapped(x, level) for level, x in enumerate(returned)]
+    back = carried(own, lent)
     total = total_over_devices(stacked, devices)
     weight_step = call(normalize_body, shape(total.shape, f32), (10**6, 10**6), total)
     node_grad = call(
-        collect_body, shape((node_dev, width), bf16), (3 * 10**8, 10**6), boundary_rows, local, *back
+        lambda *refs: collect_body(pairs, *refs),
+        shape((node_dev, width), bf16),
+        (3 * 10**8, 10**6),
+        boundary_rows,
+        local,
+        *back,
     )
     return (hidden, node_grad, weight_step)
 

time: 149 us -> 113 us (0.76)
  the two profiles are of different devices: /device:TPU:64 before, /device:TPU:1 now
where the time goes in v2:
time: 113 us; the launch traced here: 112 us
  starting transfers between devices  72.1 us (64%)
  waiting for transfers between devices  27.1 us (24%)
  Pallas kernels  10.1 us (9%)
  local copies, waits for them, and re-layouts  1.68 us (1%)
    ppermute x8, starting transfers between devices, carried(): lax.ppermute(x, 'dom', [(i, i ^ 1 << pair[i % 2]) for i in range(devices)])  34.4 us
    ppermute x4, starting transfers between devices, other_core(): return lax.ppermute(x, 'dom', [(i, i ^ 1) for i in range(devices)])  19.7 us
    all_to_all x3, starting transfers between devices, exchange(): return lax.all_to_all(x, 'dom', 0, 0, axis_index_groups=groups, tiled=True)  18.1 us
    all_to_all x3, waiting for transfers between devices, exchange(): return lax.all_to_all(x, 'dom', 0, 0, axis_index_groups=groups, tiled=True)  17 us
    pallas_call x11, Pallas kernels, call(): pl.pallas_call(body, out_shape=outs, scratch_shapes=scratch, compiler_par...  10.1 us
    ppermute x8, waiting for transfers between devices, carried(): lax.ppermute(x, 'dom', [(i, i ^ 1 << pair[i % 2]) for i in range(devices)])  8.91 us
  transfers between devices with their start and end apart: 15, of which 6 were waited for; matrix products, arithmetic and copies ran while one was open for 0% of the time, Pallas kernels for 5%

profile of v2, /device:TPU:1, one launch (start us, length us, event | category | flops | bytes accessed | tf_op | source)
XLA Modules:
  0.0 112.0 jit_solution(4223944241151447640)
XLA Ops:
  0.7 0.7 copy.12
  1.4 0.9 copy-done.2
  2.3 0.5 shard_map.95
  2.8 0.0 copy-start.4
  2.9 0.0 copy-start.5
  2.9 8.9 %collective-permute-start = (bf16[640,256]{1,0:T(8,128)(2,1)S(1)}, bf16[640,256]{1,0:T(8,128)(2,1)S(1)}, u32[]{:S(2)}, u32[]{:S(2)}) collective-permute-start(bf16[640,256]{1,0:T(8,128)(2,1)S(1)} %get-tuple-element.18), channel_id=1, source_target_pairs={{0,1},{1,0},{2,3},{3,2},{4,5},{5,4},{6,7},{7,6},{8,9},{9,8},{10,11... | collective-permute-start | bytes 983048 | tf_op jit(solution)/shard_map/ppermute | solution.py:226
  11.8 1.2 %collective-permute-done.borrowed_ref.refs_6_ = bf16[640,256]{1,0:T(8,128)(2,1)S(1)} collective-permute-done((bf16[640,256]{1,0:T(8,128)(2,1)S(1)}, bf16[640,256]{1,0:T(8,128)(2,1)S(1)}, u32[]{:S(2)}, u32[]{:S(2)}) %collective-permute-start) | collective-permute-done | bytes 327712 | tf_op jit(solution)/shard_map/ppermute | solution.py:226
  13.1 3.4 %collective-permute-start.1 = (bf16[256,256]{1,0:T(8,128)(2,1)S(1)}, bf16[256,256]{1,0:T(8,128)(2,1)S(1)}, u32[]{:S(2)}, u32[]{:S(2)}) collective-permute-start(bf16[256,256]{1,0:T(8,128)(2,1)S(1)} %get-tuple-element.20), channel_id=1, source_target_pairs={{0,256},{1,129},{2,258},{3,131},{4,260},{5,133},{6,262},{7,135},{8... | collective-permute-start | bytes 393224 | tf_op jit(solution)/shard_map/ppermute | solution.py:232
  16.5 4.9 %collective-permute-start.2 = (bf16[256,256]{1,0:T(8,128)(2,1)S(1)}, bf16[256,256]{1,0:T(8,128)(2,1)S(1)}, u32[]{:S(2)}, u32[]{:S(2)}) collective-permute-start(bf16[256,256]{1,0:T(8,128)(2,1)S(1)} %get-tuple-element.21), channel_id=1, source_target_pairs={{0,32},{1,65},{2,34},{3,67},{4,36},{5,69},{6,38},{7,71},{8,40},{9,... | collective-permute-start | bytes 393224 | tf_op jit(solution)/shard_map/ppermute | solution.py:232
  21.4 4.7 %collective-permute-start.3 = (bf16[256,256]{1,0:T(8,128)(2,1)S(1)}, bf16[256,256]{1,0:T(8,128)(2,1)S(1)}, u32[]{:S(2)}, u32[]{:S(2)}) collective-permute-start(bf16[256,256]{1,0:T(8,128)(2,1)S(1)} %get-tuple-element.22), channel_id=1, source_target_pairs={{0,8},{1,17},{2,10},{3,19},{4,12},{5,21},{6,14},{7,23},{8,0},{9,25... | collective-permute-start | bytes 393224 | tf_op jit(solution)/shard_map/ppermute | solution.py:232
  26.1 4.8 %collective-permute-start.4 = (bf16[256,256]{1,0:T(8,128)(2,1)S(1)}, bf16[256,256]{1,0:T(8,128)(2,1)S(1)}, u32[]{:S(2)}, u32[]{:S(2)}) collective-permute-start(bf16[256,256]{1,0:T(8,128)(2,1)S(1)} %get-tuple-element.23), channel_id=1, source_target_pairs={{0,2},{1,5},{2,0},{3,7},{4,6},{5,1},{6,4},{7,3},{8,10},{9,13},{10,... | collective-permute-start | bytes 393224 | tf_op jit(solution)/shard_map/ppermute | solution.py:232
  30.9 0.2 collective-permute-done.2.refs_1_.refs_9_
  31.2 2.1 %collective-permute-done.4.refs_3_.refs_11_ = bf16[256,256]{1,0:T(8,128)(2,1)S(1)} collective-permute-done((bf16[256,256]{1,0:T(8,128)(2,1)S(1)}, bf16[256,256]{1,0:T(8,128)(2,1)S(1)}, u32[]{:S(2)}, u32[]{:S(2)}) %collective-permute-start.4) | collective-permute-done | bytes 131104 | tf_op jit(solution)/shard_map/ppermute | solution.py:232
  33.3 5.6 %collective-permute-start.5 = (bf16[512,256]{1,0:T(8,128)(2,1)S(1)}, bf16[512,256]{1,0:T(8,128)(2,1)S(1)}, u32[]{:S(2)}, u32[]{:S(2)}) collective-permute-start(bf16[512,256]{1,0:T(8,128)(2,1)S(1)} %shard_map.97), channel_id=1, source_target_pairs={{0,1},{1,0},{2,3},{3,2},{4,5},{5,4},{6,7},{7,6},{8,9},{9,8},{10,11... | collective-permute-start | bytes 786440 | tf_op jit(solution)/shard_map/ppermute | solution.py:226
  39.0 2.1 %shard_map.94.refs_0_ = bf16[1664,512]{1,0:T(8,128)(2,1)S(1)} custom-call(s32[10,512]{1,0:T(8,128)S(1)} %bitcast.10, s32[1,512]{1,0:T(1,128)S(1)} %bitcast.11), custom_call_target="tpu_custom_call" | custom-call | flops 10000000 | bytes 2000000 | tf_op jit(solution)/shard_map/pallas_call | solution.py:23
  41.1 3.3 %shard_map.98 = (bf16[512,256]{1,0:T(8,128)(2,1)}, f32[512,256]{1,0:T(8,128)}, f32[512,256]{1,0:T(8,128)S(1)}, bf16[512,256]{1,0:T(8,128)(2,1)S(1)}, bf16[640,256]{1,0:T(8,128)(2,1)S(1)}) custom-call(bf16[1664,512]{1,0:T(8,128)(2,1)S(1)} %shard_map.94.refs_0_, bf16[512,256]{1,0:T(8,128)(2,1)S(1)} %copy-done.3, s32[1,512]{1,0:T(1,128)S(1)} %bitcast.12, ...), custom_call_target="tpu_custom_call" | custom-call | flops 1000000000 | bytes 6000000 | tf_op jit(solution)/shard_map/pallas_call | solution.py:23
  44.5 6.9 %all-to-all-start = ((f32[32,16,256]{2,1,0:T(8,128)}), f32[32,16,256]{2,1,0:T(8,128)S(1)}, u32[]{:S(2)}, u32[]{:S(2)}) async-start(f32[32,16,256]{2,1,0:T(8,128)} %bitcast.2), calls=%async_computation | async-start | bytes 1048576 | tf_op jit(solution)/shard_map/all_to_all | solution.py:187
  51.4 2.1 %collective-permute-start.6 = (bf16[640,256]{1,0:T(8,128)(2,1)S(1)}, bf16[640,256]{1,0:T(8,128)(2,1)S(1)}, u32[]{:S(2)}, u32[]{:S(2)}) collective-permute-start(bf16[640,256]{1,0:T(8,128)(2,1)S(1)} %get-tuple-element.26), channel_id=1, source_target_pairs={{0,1},{1,0},{2,3},{3,2},{4,5},{5,4},{6,7},{7,6},{8,9},{9,8},{10,11... | collective-permute-start | bytes 983048 | tf_op jit(solution)/shard_map/ppermute | solution.py:226
  53.6 9.5 %all-to-all-done.parts_ref = f32[32,16,256]{2,1,0:T(8,128)S(1)} async-done(((f32[32,16,256]{2,1,0:T(8,128)}), f32[32,16,256]{2,1,0:T(8,128)S(1)}, u32[]{:S(2)}, u32[]{:S(2)}) %all-to-all-start) | async-done | bytes 524320 | tf_op jit(solution)/shard_map/all_to_all | solution.py:187
  63.0 0.7 shard_map.102
  63.7 6.1 %all-to-all-start.1 = ((bf16[16,16,256]{2,1,0:T(8,128)(2,1)}), bf16[16,16,256]{2,1,0:T(8,128)(2,1)S(1)}, u32[]{:S(2)}, u32[]{:S(2)}) async-start(bf16[16,16,256]{2,1,0:T(8,128)(2,1)} %shard_map.102), calls=%async_computation.1 | async-start | bytes 262144 | tf_op jit(solution)/shard_map/all_to_all | solution.py:187
  69.9 7.2 %collective-permute-start.7 = (bf16[256,256]{1,0:T(8,128)(2,1)S(1)}, bf16[256,256]{1,0:T(8,128)(2,1)S(1)}, u32[]{:S(2)}, u32[]{:S(2)}) collective-permute-start(bf16[256,256]{1,0:T(8,128)(2,1)S(1)} %get-tuple-element.28), channel_id=1, source_target_pairs={{0,256},{1,129},{2,258},{3,131},{4,260},{5,133},{6,262},{7,135},{8... | collective-permute-start | bytes 393224 | tf_op jit(solution)/shard_map/ppermute | solution.py:232
  77.1 4.0 %collective-permute-start.8 = (bf16[256,256]{1,0:T(8,128)(2,1)S(1)}, bf16[256,256]{1,0:T(8,128)(2,1)S(1)}, u32[]{:S(2)}, u32[]{:S(2)}) collective-permute-start(bf16[256,256]{1,0:T(8,128)(2,1)S(1)} %get-tuple-element.29), channel_id=1, source_target_pairs={{0,32},{1,65},{2,34},{3,67},{4,36},{5,69},{6,38},{7,71},{8,40},{9,... | collective-permute-start | bytes 393224 | tf_op jit(solution)/shard_map/ppermute | solution.py:232
  81.1 3.0 %collective-permute-start.9 = (bf16[256,256]{1,0:T(8,128)(2,1)S(1)}, bf16[256,256]{1,0:T(8,128)(2,1)S(1)}, u32[]{:S(2)}, u32[]{:S(2)}) collective-permute-start(bf16[256,256]{1,0:T(8,128)(2,1)S(1)} %get-tuple-element.30), channel_id=1, source_target_pairs={{0,8},{1,17},{2,10},{3,19},{4,12},{5,21},{6,14},{7,23},{8,0},{9,25... | collective-permute-start | bytes 393224 | tf_op jit(solution)/shard_map/ppermute | solution.py:232
  84.1 2.3 %collective-permute-start.10 = (bf16[256,256]{1,0:T(8,128)(2,1)S(1)}, bf16[256,256]{1,0:T(8,128)(2,1)S(1)}, u32[]{:S(2)}, u32[]{:S(2)}) collective-permute-start(bf16[256,256]{1,0:T(8,128)(2,1)S(1)} %get-tuple-element.31), channel_id=1, source_target_pairs={{0,2},{1,5},{2,0},{3,7},{4,6},{5,1},{6,4},{7,3},{8,10},{9,13},{10,... | collective-permute-start | bytes 393224 | tf_op jit(solution)/shard_map/ppermute | solution.py:232
  86.5 6.5 %collective-permute-done.7.refs_0_.refs_4_ = bf16[256,256]{1,0:T(8,128)(2,1)S(1)} collective-permute-done((bf16[256,256]{1,0:T(8,128)(2,1)S(1)}, bf16[256,256]{1,0:T(8,128)(2,1)S(1)}, u32[]{:S(2)}, u32[]{:S(2)}) %collective-permute-start.7) | collective-permute-done | bytes 131104 | tf_op jit(solution)/shard_map/ppermute | solution.py:232
  93.0 3.0 %collective-permute-start.11 = (bf16[512,256]{1,0:T(8,128)(2,1)S(1)}, bf16[512,256]{1,0:T(8,128)(2,1)S(1)}, u32[]{:S(2)}, u32[]{:S(2)}) collective-permute-start(bf16[512,256]{1,0:T(8,128)(2,1)S(1)} %shard_map.100), channel_id=1, source_target_pairs={{0,1},{1,0},{2,3},{3,2},{4,5},{5,4},{6,7},{7,6},{8,9},{9,8},{10,11... | collective-permute-start | bytes 786440 | tf_op jit(solution)/shard_map/ppermute | solution.py:226
  96.0 0.7 shard_map.103
  96.8 5.1 %all-to-all-start.2 = ((bf16[32,16,256]{2,1,0:T(8,128)(2,1)}), bf16[32,16,256]{2,1,0:T(8,128)(2,1)S(1)}, u32[]{:S(2)}, u32[]{:S(2)}) async-start(bf16[32,16,256]{2,1,0:T(8,128)(2,1)} %shard_map.103), calls=%async_computation.2 | async-start | bytes 524288 | tf_op jit(solution)/shard_map/all_to_all | solution.py:187
  101.9 1.5 %shard_map.101 = bf16[512,256]{1,0:T(8,128)(2,1)} custom-call(s32[9,128]{1,0:T(8,128)S(1)} %bitcast.9, f32[512,256]{1,0:T(8,128)S(1)} %get-tuple-element.25.refs_1_, bf16[640,256]{1,0:T(8,128)(2,1)S(1)} %collective-permute-done.6.borrowed_ref.refs_2_, bf16[512,256]{1,0:T(8,128)(2,1)S(1)} %collective-permute-done.11.refs_3_, ...), custom_call_target="tpu_custom_call" | custom-call | flops 300000000 | bytes 1000000 | tf_op jit(solution)/shard_map/pallas_call | solution.py:23
  103.4 7.5 %all-to-all-done.2 = bf16[32,16,256]{2,1,0:T(8,128)(2,1)S(1)} async-done(((bf16[32,16,256]{2,1,0:T(8,128)(2,1)}), bf16[32,16,256]{2,1,0:T(8,128)(2,1)S(1)}, u32[]{:S(2)}, u32[]{:S(2)}) %all-to-all-start.2) | async-done | bytes 262176 | tf_op jit(solution)/shard_map/all_to_all | solution.py:187
  110.9 1.1 shard_map.104
  (24 shorter events, 0.2 us)
Async XLA Ops:
  0.6 38.3 %copy-start.1 = (s32[512]{0:T(512)S(1)}, s32[512]{0:T(512)}, u32[]{:S(2)}) copy-start(s32[512]{0:T(512)} %param.11) | copy-start | bytes 6148
  0.6 38.3 %copy-start = (s32[512,10]{0,1:T(8,128)S(1)}, s32[512,10]{0,1:T(8,128)}, u32[]{:S(2)}) copy-start(s32[512,10]{0,1:T(8,128)} %param.10) | copy-start | bytes 61444
  1.4 0.9 copy-start.2
  2.8 38.3 %copy-start.3 = (bf16[512,256]{1,0:T(8,128)(2,1)S(1)}, bf16[512,256]{1,0:T(8,128)(2,1)}, u32[]{:S(2)}) copy-start(bf16[512,256]{1,0:T(8,128)(2,1)} %refs_1_.3) | copy-start | bytes 786436
  2.8 38.3 %copy-start.4 = (bf16[512,256]{1,0:T(8,128)(2,1)S(1)}, bf16[512,256]{1,0:T(8,128)(2,1)}, u32[]{:S(2)}) copy-start(bf16[512,256]{1,0:T(8,128)(2,1)} %refs_3_.1) | copy-start | bytes 786436
  2.9 38.3 %copy-start.5 = (bf16[256,256]{1,0:T(8,128)(2,1)S(1)}, bf16[256,256]{1,0:T(8,128)(2,1)}, u32[]{:S(2)}) copy-start(bf16[256,256]{1,0:T(8,128)(2,1)} %refs_4_.1) | copy-start | bytes 393220
  2.9 38.3 %copy-start.6 = (bf16[256,256]{1,0:T(8,128)(2,1)S(1)}, bf16[256,256]{1,0:T(8,128)(2,1)}, u32[]{:S(2)}) copy-start(bf16[256,256]{1,0:T(8,128)(2,1)} %refs_5_.1) | copy-start | bytes 393220
  2.9 10.2 %collective-permute-start = (bf16[640,256]{1,0:T(8,128)(2,1)S(1)}, bf16[640,256]{1,0:T(8,128)(2,1)S(1)}, u32[]{:S(2)}, u32[]{:S(2)}) collective-permute-start(bf16[640,256]{1,0:T(8,128)(2,1)S(1)} %get-tuple-element.18), channel_id=1, source_target_pairs={{0,1},{1,0},{2,3},{3,2},{4,5},{5,4},{6,7},{7,6},{8,9},{9,8},{10,11... | collective-permute-start | bytes 983048 | tf_op jit(solution)/shard_map/ppermute | solution.py:226
  13.1 17.9 %collective-permute-start.1 = (bf16[256,256]{1,0:T(8,128)(2,1)S(1)}, bf16[256,256]{1,0:T(8,128)(2,1)S(1)}, u32[]{:S(2)}, u32[]{:S(2)}) collective-permute-start(bf16[256,256]{1,0:T(8,128)(2,1)S(1)} %get-tuple-element.20), channel_id=1, source_target_pairs={{0,256},{1,129},{2,258},{3,131},{4,260},{5,133},{6,262},{7,135},{8... | collective-permute-start | bytes 393224 | tf_op jit(solution)/shard_map/ppermute | solution.py:232
  16.5 14.6 %collective-permute-start.2 = (bf16[256,256]{1,0:T(8,128)(2,1)S(1)}, bf16[256,256]{1,0:T(8,128)(2,1)S(1)}, u32[]{:S(2)}, u32[]{:S(2)}) collective-permute-start(bf16[256,256]{1,0:T(8,128)(2,1)S(1)} %get-tuple-element.21), channel_id=1, source_target_pairs={{0,32},{1,65},{2,34},{3,67},{4,36},{5,69},{6,38},{7,71},{8,40},{9,... | collective-permute-start | bytes 393224 | tf_op jit(solution)/shard_map/ppermute | solution.py:232
  21.4 9.7 %collective-permute-start.3 = (bf16[256,256]{1,0:T(8,128)(2,1)S(1)}, bf16[256,256]{1,0:T(8,128)(2,1)S(1)}, u32[]{:S(2)}, u32[]{:S(2)}) collective-permute-start(bf16[256,256]{1,0:T(8,128)(2,1)S(1)} %get-tuple-element.22), channel_id=1, source_target_pairs={{0,8},{1,17},{2,10},{3,19},{4,12},{5,21},{6,14},{7,23},{8,0},{9,25... | collective-permute-start | bytes 393224 | tf_op jit(solution)/shard_map/ppermute | solution.py:232
  26.1 7.2 %collective-permute-start.4 = (bf16[256,256]{1,0:T(8,128)(2,1)S(1)}, bf16[256,256]{1,0:T(8,128)(2,1)S(1)}, u32[]{:S(2)}, u32[]{:S(2)}) collective-permute-start(bf16[256,256]{1,0:T(8,128)(2,1)S(1)} %get-tuple-element.23), channel_id=1, source_target_pairs={{0,2},{1,5},{2,0},{3,7},{4,6},{5,1},{6,4},{7,3},{8,10},{9,13},{10,... | collective-permute-start | bytes 393224 | tf_op jit(solution)/shard_map/ppermute | solution.py:232
  33.3 7.7 %collective-permute-start.5 = (bf16[512,256]{1,0:T(8,128)(2,1)S(1)}, bf16[512,256]{1,0:T(8,128)(2,1)S(1)}, u32[]{:S(2)}, u32[]{:S(2)}) collective-permute-start(bf16[512,256]{1,0:T(8,128)(2,1)S(1)} %shard_map.97), channel_id=1, source_target_pairs={{0,1},{1,0},{2,3},{3,2},{4,5},{5,4},{6,7},{7,6},{8,9},{9,8},{10,11... | collective-permute-start | bytes 786440 | tf_op jit(solution)/shard_map/ppermute | solution.py:226
  44.5 18.5 %all-to-all-start = ((f32[32,16,256]{2,1,0:T(8,128)}), f32[32,16,256]{2,1,0:T(8,128)S(1)}, u32[]{:S(2)}, u32[]{:S(2)}) async-start(f32[32,16,256]{2,1,0:T(8,128)} %bitcast.2), calls=%async_computation | async-start | bytes 1048576 | tf_op jit(solution)/shard_map/all_to_all | solution.py:187
  51.4 18.4 %collective-permute-start.6 = (bf16[640,256]{1,0:T(8,128)(2,1)S(1)}, bf16[640,256]{1,0:T(8,128)(2,1)S(1)}, u32[]{:S(2)}, u32[]{:S(2)}) collective-permute-start(bf16[640,256]{1,0:T(8,128)(2,1)S(1)} %get-tuple-element.26), channel_id=1, source_target_pairs={{0,1},{1,0},{2,3},{3,2},{4,5},{5,4},{6,7},{7,6},{8,9},{9,8},{10,11... | collective-permute-start | bytes 983048 | tf_op jit(solution)/shard_map/ppermute | solution.py:226
  63.7 32.3 %all-to-all-start.1 = ((bf16[16,16,256]{2,1,0:T(8,128)(2,1)}), bf16[16,16,256]{2,1,0:T(8,128)(2,1)S(1)}, u32[]{:S(2)}, u32[]{:S(2)}) async-start(bf16[16,16,256]{2,1,0:T(8,128)(2,1)} %shard_map.102), calls=%async_computation.1 | async-start | bytes 262144 | tf_op jit(solution)/shard_map/all_to_all | solution.py:187
  69.9 23.1 %collective-permute-start.7 = (bf16[256,256]{1,0:T(8,128)(2,1)S(1)}, bf16[256,256]{1,0:T(8,128)(2,1)S(1)}, u32[]{:S(2)}, u32[]{:S(2)}) collective-permute-start(bf16[256,256]{1,0:T(8,128)(2,1)S(1)} %get-tuple-element.28), channel_id=1, source_target_pairs={{0,256},{1,129},{2,258},{3,131},{4,260},{5,133},{6,262},{7,135},{8... | collective-permute-start | bytes 393224 | tf_op jit(solution)/shard_map/ppermute | solution.py:232
  77.1 15.9 %collective-permute-start.8 = (bf16[256,256]{1,0:T(8,128)(2,1)S(1)}, bf16[256,256]{1,0:T(8,128)(2,1)S(1)}, u32[]{:S(2)}, u32[]{:S(2)}) collective-permute-start(bf16[256,256]{1,0:T(8,128)(2,1)S(1)} %get-tuple-element.29), channel_id=1, source_target_pairs={{0,32},{1,65},{2,34},{3,67},{4,36},{5,69},{6,38},{7,71},{8,40},{9,... | collective-permute-start | bytes 393224 | tf_op jit(solution)/shard_map/ppermute | solution.py:232
  81.1 11.9 %collective-permute-start.9 = (bf16[256,256]{1,0:T(8,128)(2,1)S(1)}, bf16[256,256]{1,0:T(8,128)(2,1)S(1)}, u32[]{:S(2)}, u32[]{:S(2)}) collective-permute-start(bf16[256,256]{1,0:T(8,128)(2,1)S(1)} %get-tuple-element.30), channel_id=1, source_target_pairs={{0,8},{1,17},{2,10},{3,19},{4,12},{5,21},{6,14},{7,23},{8,0},{9,25... | collective-permute-start | bytes 393224 | tf_op jit(solution)/shard_map/ppermute | solution.py:232
  84.1 8.9 %collective-permute-start.10 = (bf16[256,256]{1,0:T(8,128)(2,1)S(1)}, bf16[256,256]{1,0:T(8,128)(2,1)S(1)}, u32[]{:S(2)}, u32[]{:S(2)}) collective-permute-start(bf16[256,256]{1,0:T(8,128)(2,1)S(1)} %get-tuple-element.31), channel_id=1, source_target_pairs={{0,2},{1,5},{2,0},{3,7},{4,6},{5,1},{6,4},{7,3},{8,10},{9,13},{10,... | collective-permute-start | bytes 393224 | tf_op jit(solution)/shard_map/ppermute | solution.py:232
  93.0 8.9 %collective-permute-start.11 = (bf16[512,256]{1,0:T(8,128)(2,1)S(1)}, bf16[512,256]{1,0:T(8,128)(2,1)S(1)}, u32[]{:S(2)}, u32[]{:S(2)}) collective-permute-start(bf16[512,256]{1,0:T(8,128)(2,1)S(1)} %shard_map.100), channel_id=1, source_target_pairs={{0,1},{1,0},{2,3},{3,2},{4,5},{5,4},{6,7},{7,6},{8,9},{9,8},{10,11... | collective-permute-start | bytes 786440 | tf_op jit(solution)/shard_map/ppermute | solution.py:226
  96.8 14.1 %all-to-all-start.2 = ((bf16[32,16,256]{2,1,0:T(8,128)(2,1)}), bf16[32,16,256]{2,1,0:T(8,128)(2,1)S(1)}, u32[]{:S(2)}, u32[]{:S(2)}) async-start(bf16[32,16,256]{2,1,0:T(8,128)(2,1)} %shard_map.103), calls=%async_computation.2 | async-start | bytes 524288 | tf_op jit(solution)/shard_map/all_to_all | solution.py:187

commit v3 on v2

v3 whole, which is shorter than its diff:
```python
import jax
import jax.numpy as jnp
from jax import lax
from jax.experimental import pallas as pl
from jax.experimental.pallas import tpu as pltpu
from jax.sharding import PartitionSpec as P

epsilon = 1e-06
f32 = jnp.float32
bf16 = jnp.bfloat16
FAST_BITS = 5
VMEM_LIMIT = 16 * 1024 * 1024
TRANSPOSED_LHS = (((0,), (0,)), ((), ()))
TRANSPOSED_RHS = (((1,), (1,)), ((), ()))


def dot(a, b, dims=(((1,), (0,)), ((), ()))):
    return lax.dot_general(a, b, dims, preferred_element_type=f32)


def call(body, outs, cost, *args, after=(), scratch=()):
    flops, moved = cost
    reads, waits = len(args), len(after)
    return pl.pallas_call(
        lambda *refs: body(*refs[:reads], *refs[reads + waits :]),
        out_shape=outs,
        in_specs=[pl.BlockSpec(memory_space=pltpu.VMEM)] * reads
        + [pl.BlockSpec(memory_space=pl.ANY)] * waits,
        scratch_shapes=scratch,
        compiler_params=pltpu.CompilerParams(vmem_limit_bytes=VMEM_LIMIT),
        cost_estimate=pl.CostEstimate(flops=flops, bytes_accessed=moved, transcendentals=0),
    )(*args, *after)


def shape(dims, dtype):
    return jax.ShapeDtypeStruct(dims, dtype)


def one_hot_columns(rows, node_dev):
    k = rows.shape[1]
    ids = lax.broadcasted_iota(jnp.int32, (node_dev, k), 0)
    return jnp.where(ids == rows, f32(1.0), f32(0.0)).astype(bf16)


def core_index():
    return lax.rem(lax.axis_index("dom"), 2)


def level_of(pair, core):
    return jnp.where(core == 0, pair[0], pair[1])


def send_body(pairs, boundary_ref, features_ref, own_ref, lent_ref):
    node_dev = features_ref.shape[0]
    bnd = boundary_ref.shape[2]
    core = core_index()
    features = features_ref[...]

    def rows_of(level):
        pick = one_hot_columns(boundary_ref[level], node_dev)
        return dot(pick, features, TRANSPOSED_LHS).astype(bf16)

    lent_ref[:bnd, :] = rows_of(0)
    for k, pair in enumerate(pairs):
        lent_ref[(k + 1) * bnd : (k + 2) * bnd, :] = rows_of(level_of(pair, 1 - core))
        own_ref[k * bnd : (k + 1) * bnd, :] = rows_of(level_of(pair, core))


def load_body(first, skip, own_ref, borrowed_ref, *load_refs):
    bnd = load_refs[0].shape[0] // 2
    for k, load_ref in enumerate(load_refs):
        load_ref[:bnd, :] = own_ref[(k + first) * bnd : (k + first + 1) * bnd, :]
        load_ref[bnd:, :] = borrowed_ref[(k + skip) * bnd : (k + skip + 1) * bnd, :]


def unload_body(*refs):
    load_refs, lent_ref = refs[:-1], refs[-1]
    bnd = load_refs[0].shape[0] // 2
    for k, load_ref in enumerate(load_refs):
        lent_ref[k * bnd : (k + 1) * bnd, :] = load_ref[bnd:, :]


def count_body(neighbors_ref, degree_ref, counts_ref):
    slots, node_dev = neighbors_ref.shape
    degree = degree_ref[...]
    live = [
        jnp.where(degree > slot, neighbors_ref[slot : slot + 1, :], -1) for slot in range(slots)
    ]
    tile, step = 128, 16
    ids = lax.broadcasted_iota(jnp.int32, (step, node_dev), 0)

    def block(at, carry):
        start = pl.multiple_of(at * tile, tile)
        near = [
            jnp.broadcast_to(row - start, (step, node_dev)).astype(f32).astype(bf16) for row in live
        ]
        for part in range(tile // step):
            here = (ids + part * step).astype(f32).astype(bf16)
            total = jnp.zeros((step, node_dev), bf16)
            for row in near:
                total = total + jnp.where(here == row, bf16(1.0), bf16(0.0))
            counts_ref[pl.ds(start + part * step, step), :] = total
        return carry

    lax.fori_loop(0, counts_ref.shape[0] // tile, block, 0)


def gather_early_body(pairs, counts_ref, features_ref, w_self_ref, borrowed_ref, *refs):
    loads, summed_ref, own_part_ref = refs[:-2], refs[-2], refs[-1]
    node_dev = features_ref.shape[0]
    bnd = borrowed_ref.shape[0] // (len(pairs) + 1)
    core = core_index()
    features = features_ref[...]
    own_part_ref[...] = dot(features, w_self_ref[...])
    summed = dot(counts_ref[:node_dev, :], features, TRANSPOSED_LHS)
    summed = summed + dot(
        counts_ref[node_dev : node_dev + bnd, :], borrowed_ref[:bnd, :], TRANSPOSED_LHS
    )
    for k, pair in enumerate(pairs):
        rows = level_rows(node_dev, bnd, level_of(pair, core))
        summed = summed + dot(counts_ref[rows, :], loads[k][:bnd, :], TRANSPOSED_LHS)
    summed_ref[...] = summed


def level_rows(node_dev, bnd, level):
    return pl.ds(pl.multiple_of(node_dev + level * bnd, bnd), bnd)


def layer_body(
    pairs,
    counts_ref,
    summed_ref,
    own_part_ref,
    kept_ref,
    features_ref,
    degree_ref,
    upstream_ref,
    w_neigh_ref,
    hidden_ref,
    stacked_ref,
    pre_grad_ref,
    share_ref,
):
    node_dev, width = features_ref.shape
    bnd = kept_ref.shape[0] // len(pairs)
    core = core_index()
    degree = degree_ref[...].astype(f32)
    degree = jnp.transpose(jnp.broadcast_to(degree, (128, node_dev)))
    degree = jnp.concatenate([degree] * (width // 128), axis=1)
    summed = summed_ref[...]
    for k, pair in enumerate(pairs):
        rows = level_rows(node_dev, bnd, level_of(pair, 1 - core))
        kept = kept_ref[k * bnd : (k + 1) * bnd, :]
        summed = summed + dot(counts_ref[rows, :], kept, TRANSPOSED_LHS)
    agg = (summed / degree).astype(bf16)
    pre_sum = own_part_ref[...] + dot(agg, w_neigh_ref[...])
    sigmoid_pre = jax.nn.sigmoid(pre_sum)
    hidden_ref[...] = (pre_sum * sigmoid_pre).astype(bf16)
    pre_grad = (
        upstream_ref[...].astype(f32) * sigmoid_pre * (1.0 + pre_sum * (1.0 - sigmoid_pre))
    ).astype(bf16)
    stacked_ref[:width, :] = dot(features_ref[...], pre_grad, TRANSPOSED_LHS).astype(bf16)
    stacked_ref[width:, :] = dot(agg, pre_grad, TRANSPOSED_LHS).astype(bf16)
    share = (dot(pre_grad, w_neigh_ref[...], TRANSPOSED_RHS) / degree).astype(bf16)
    pre_grad_ref[...] = pre_grad
    share_ref[...] = share


def spread_body(
    pairs, counts_ref, pre_grad_ref, share_ref, w_self_ref, local_ref, own_ref, lent_a_ref, lent_b_ref
):
    node_dev = pre_grad_ref.shape[0]
    bnd = own_ref.shape[0] // len(pairs)
    core = core_index()
    pre_grad, share = pre_grad_ref[...], share_ref[...]
    split = lent_a_ref.shape[0] // bnd
    for k, pair in enumerate(pairs):
        rows = level_rows(node_dev, bnd, level_of(pair, 1 - core))
        lent_ref, at = (lent_a_ref, k) if k < split else (lent_b_ref, k - split)
        lent_ref[at * bnd : (at + 1) * bnd, :] = dot(counts_ref[rows, :], share).astype(bf16)
        rows = level_rows(node_dev, bnd, level_of(pair, core))
        own_ref[k * bnd : (k + 1) * bnd, :] = dot(counts_ref[rows, :], share).astype(bf16)
    lent_b_ref[(len(pairs) - split) * bnd :, :] = dot(
        counts_ref[node_dev : node_dev + bnd, :], share
    ).astype(bf16)
    local_ref[...] = dot(pre_grad, w_self_ref[...], TRANSPOSED_RHS) + dot(
        counts_ref[:node_dev, :], share
    )


def collect_early_body(pairs, boundary_ref, local_ref, borrowed_ref, *refs):
    loads, sum_ref = refs[:-1], refs[-1]
    node_dev = local_ref.shape[0]
    bnd = boundary_ref.shape[2]
    core = core_index()
    pick = one_hot_columns(boundary_ref[0], node_dev)
    total = local_ref[...] + dot(pick, borrowed_ref[borrowed_ref.shape[0] - bnd :, :])
    for k, pair in enumerate(pairs):
        pick = one_hot_columns(boundary_ref[level_of(pair, core)], node_dev)
        total = total + dot(pick, loads[k][:bnd, :])
    sum_ref[...] = total


def collect_body(pairs, boundary_ref, sum_ref, kept_ref, node_grad_ref):
    node_dev = sum_ref.shape[0]
    bnd = boundary_ref.shape[2]
    core = core_index()
    total = sum_ref[...]
    for k, pair in enumerate(pairs):
        pick = one_hot_columns(boundary_ref[level_of(pair, 1 - core)], node_dev)
        total = total + dot(pick, kept_ref[k * bnd : (k + 1) * bnd, :])
    node_grad_ref[...] = total.astype(bf16)


def normalize_body(total_ref, out_ref):
    total = total_ref[...].astype(f32)
    mean = jnp.sum(total * total) / total.size
    out_ref[...] = total * lax.rsqrt(jnp.full((1, total.shape[1]), mean + epsilon, f32))


def sum_and_repeat_body(parts_ref, out_ref):
    total = parts_ref[0].astype(f32)
    for part in range(1, parts_ref.shape[0]):
        total = total + parts_ref[part].astype(f32)
    out_ref[...] = jnp.broadcast_to(total.astype(out_ref.dtype)[None], out_ref.shape)


def bit_groups(devices, bits):
    mask = sum(1 << b for b in bits)
    groups = {}
    for i in range(devices):
        groups.setdefault(i & ~mask, []).append(i)
    return list(groups.values())


def exchange(x, groups):
    return lax.all_to_all(x, "dom", 0, 0, axis_index_groups=groups, tiled=True)


def level_pairs(levels):
    pairs = []
    for top in range(levels - 1, 1, -2):
        pairs.append((top, top - 1) if not pairs else (top - 1, top))
    return pairs


def per_device(features, w_self, w_neigh, neighbors, degree, boundary, upstream):
    devices = lax.axis_size("dom")
    levels = devices.bit_length() - 1
    pairs = level_pairs(levels)
    node_dev, width = features.shape
    boundary_rows = boundary.transpose(1, 0, 2)
    bnd = boundary_rows.shape[2]
    rows = node_dev + levels * bnd
    block = (node_dev, width)
    own_shape = shape((len(pairs) * bnd, width), bf16)
    lent_shape = shape(((len(pairs) + 1) * bnd, width), bf16)
    load_shape = shape((2 * bnd, width), bf16)
    near = bit_groups(devices, range(FAST_BITS))
    far = bit_groups(devices, range(FAST_BITS, levels))
    piece = 2 * width // len(near[0])
    small = (10**8, 10**6)

    def other_core(x):
        return lax.ppermute(x, "dom", [(i, i ^ 1) for i in range(devices)])

    def across(loads, taken):
        return [
            lax.ppermute(x, "dom", [(i, i ^ 1 << pair[i % 2]) for i in range(devices)])
            for x, pair in zip(loads, taken)
        ]

    def with_pairs(body):
        return lambda *refs: body(pairs, *refs)

    def loaded(own, borrowed, first, last, skip=0):
        return call(
            lambda *refs: load_body(first, skip, *refs),
            [load_shape] * (last - first),
            small,
            own,
            borrowed,
        )

    own, lent = call(
        with_pairs(send_body), [own_shape, lent_shape], (10**9, 10**6), boundary_rows, features
    )
    borrowed = other_core(lent)
    loads = loaded(own, borrowed, 0, len(pairs), skip=1)
    degree_row = degree.reshape(1, node_dev)
    counts = call(
        count_body,
        shape((rows, node_dev), bf16),
        (2 * 10**9, 2 * 10**6),
        neighbors.T,
        degree_row,
        after=(loads[-1],),
    )
    loads = across(loads, pairs)
    kept = other_core(call(unload_body, own_shape, small, *loads, after=(counts,)))
    summed, own_part = call(
        with_pairs(gather_early_body),
        [shape(block, f32)] * 2,
        (10**9, 3 * 10**6),
        counts,
        features,
        w_self,
        borrowed,
        *loads,
    )
    hidden, stacked, pre_grad, share = call(
        with_pairs(layer_body),
        [
            shape(block, bf16),
            shape((2 * width, width), bf16),
            shape(block, bf16),
            shape(block, bf16),
        ],
        (2 * 10**9, 5 * 10**6),
        counts,
        summed,
        own_part,
        kept,
        features,
        degree_row,
        upstream,
        w_neigh,
    )

    parts = exchange(stacked.reshape(len(near[0]), piece, width), near)
    split = len(pairs) // 2
    local, own, lent_a, lent_b = call(
        with_pairs(spread_body),
        [
            shape(block, f32),
            own_shape,
            shape((split * bnd, width), bf16),
            shape(((len(pairs) - split + 1) * bnd, width), bf16),
        ],
        small,
        counts,
        pre_grad,
        share,
        w_self,
    )
    borrowed_a, borrowed_b = other_core(lent_a), other_core(lent_b)
    partial = call(
        sum_and_repeat_body,
        shape((len(far[0]), piece, width), bf16),
        small,
        parts,
        after=(borrowed_a, borrowed_b),
    )
    parts = exchange(partial, far)
    loads = loaded(own, borrowed_a, 0, split) + loaded(own, borrowed_b, split, len(pairs))
    loads = across(loads, pairs)
    total = call(sum_and_repeat_body, shape((len(near[0]), piece, width), bf16), small, parts)
    gathered = exchange(total, near).reshape(2 * width, width)
    kept = other_core(call(unload_body, own_shape, small, *loads, after=(total,)))
    early = call(
        with_pairs(collect_early_body),
        shape(block, f32),
        (10**9, 10**6),
        boundary_rows,
        local,
        borrowed_b,
        *loads,
    )
    node_grad = call(
        with_pairs(collect_body), shape(block, bf16), (10**9, 10**6), boundary_rows, early, kept
    )
    weight_step = call(normalize_body, shape(gathered.shape, f32), small, gathered)
    return (hidden, node_grad, weight_step)


def solution(mesh):
    return jax.shard_map(
        per_device,
        mesh=mesh,
        in_specs=(
            P("dom", None),
            P(),
            P(),
            P("dom", None),
            P("dom"),
            P("dom", None, None),
            P("dom", None),
        ),
        out_specs=(P("dom", None), P("dom", None), P()),
        check_vma=False,
    )
```

time: 113 us -> 104 us (0.920)
  waiting for transfers between devices: 27.1 us -> 12 us
  starting transfers between devices: 72.1 us -> 78.2 us
    ppermute x8, waiting for transfers between devices: 8.91 us -> 0.22 us  [across(): lax.ppermute(x, 'dom', [(i, i ^ 1 << pair[i % 2]) for i in range(devices)])]
    all_to_all x3, waiting for transfers between devices: 17 us -> 9.16 us  [exchange(): return lax.all_to_all(x, 'dom', 0, 0, axis_index_groups=groups, tiled=True)]
    all_to_all x3, starting transfers between devices: 18.1 us -> 21.5 us  [exchange(): return lax.all_to_all(x, 'dom', 0, 0, axis_index_groups=groups, tiled=True)]
    ppermute x4 -> x5, waiting for transfers between devices: 1.24 us -> 2.67 us  [other_core(): return lax.ppermute(x, 'dom', [(i, i ^ 1) for i in range(devices)])]
    ppermute x4 -> x5, starting transfers between devices: 19.7 us -> 21 us  [other_core(): return lax.ppermute(x, 'dom', [(i, i ^ 1) for i in range(devices)])]
    ppermute x8, starting transfers between devices: 34.4 us -> 35.6 us  [across(): lax.ppermute(x, 'dom', [(i, i ^ 1 << pair[i % 2]) for i in range(devices)])]
    pallas_call x11 -> x15, Pallas kernels: 10.1 us -> 10.3 us  [call(): pl.pallas_call(lambda *refs: body(*refs[:reads], *refs[reads + waits:]),...]
  transfers between devices with their start and end apart: 15 -> 16, of which waited for: 6 -> 6; matrix products, arithmetic and copies ran while one was open for 0% -> 0% of each run, Pallas kernels for 5% -> 6%
where the time goes in v3:
time: 104 us; the launch traced here: 103 us
  starting transfers between devices  78.2 us (75%)
  waiting for transfers between devices  12 us (12%)
  Pallas kernels  10.3 us (10%)
  local copies, waits for them, and re-layouts  1.67 us (2%)
    ppermute x8, starting transfers between devices, across(): lax.ppermute(x, 'dom', [(i, i ^ 1 << pair[i % 2]) for i in range(devices)])  35.6 us
    all_to_all x3, starting transfers between devices, exchange(): return lax.all_to_all(x, 'dom', 0, 0, axis_index_groups=groups, tiled=True)  21.5 us
    ppermute x5, starting transfers between devices, other_core(): return lax.ppermute(x, 'dom', [(i, i ^ 1) for i in range(devices)])  21 us
    pallas_call x15, Pallas kernels, call(): pl.pallas_call(lambda *refs: body(*refs[:reads], *refs[reads + waits:]),...  10.3 us
    all_to_all x3, waiting for transfers between devices, exchange(): return lax.all_to_all(x, 'dom', 0, 0, axis_index_groups=groups, tiled=True)  9.16 us
    ppermute x5, waiting for transfers between devices, other_core(): return lax.ppermute(x, 'dom', [(i, i ^ 1) for i in range(devices)])  2.67 us
  transfers between devices with their start and end apart: 16, of which 6 were waited for; matrix products, arithmetic and copies ran while one was open for 0% of the time, Pallas kernels for 6%

profile of v3, /device:TPU:1, one launch (start us, length us, event | category | flops | bytes accessed | tf_op | source)
XLA Modules:
  0.0 103.1 jit_solution(10301326421245333510)
XLA Ops:
  0.6 0.9 copy-done.1
  1.6 0.7 copy-done.6
  2.3 0.5 shard_map.94
  2.8 8.8 %collective-permute-start = (bf16[640,256]{1,0:T(8,128)(2,1)S(1)}, bf16[640,256]{1,0:T(8,128)(2,1)S(1)}, u32[]{:S(2)}, u32[]{:S(2)}) collective-permute-start(bf16[640,256]{1,0:T(8,128)(2,1)S(1)} %get-tuple-element.24), channel_id=1, source_target_pairs={{0,1},{1,0},{2,3},{3,2},{4,5},{5,4},{6,7},{7,6},{8,9},{9,8},{10,11... | collective-permute-start | bytes 983048 | tf_op jit(solution)/shard_map/ppermute | solution.py:265
  11.6 1.2 %collective-permute-done.refs_1_.refs_3_ = bf16[640,256]{1,0:T(8,128)(2,1)S(1)} collective-permute-done((bf16[640,256]{1,0:T(8,128)(2,1)S(1)}, bf16[640,256]{1,0:T(8,128)(2,1)S(1)}, u32[]{:S(2)}, u32[]{:S(2)}) %collective-permute-start) | collective-permute-done | bytes 327712 | tf_op jit(solution)/shard_map/ppermute | solution.py:265
  12.9 3.4 %collective-permute-start.1 = (bf16[256,256]{1,0:T(8,128)(2,1)S(1)}, bf16[256,256]{1,0:T(8,128)(2,1)S(1)}, u32[]{:S(2)}, u32[]{:S(2)}) collective-permute-start(bf16[256,256]{1,0:T(8,128)(2,1)S(1)} %get-tuple-element.26), channel_id=1, source_target_pairs={{0,256},{1,129},{2,258},{3,131},{4,260},{5,133},{6,262},{7,135},{8... | collective-permute-start | bytes 393224 | tf_op jit(solution)/shard_map/ppermute | solution.py:269
  16.3 4.9 %collective-permute-start.2 = (bf16[256,256]{1,0:T(8,128)(2,1)S(1)}, bf16[256,256]{1,0:T(8,128)(2,1)S(1)}, u32[]{:S(2)}, u32[]{:S(2)}) collective-permute-start(bf16[256,256]{1,0:T(8,128)(2,1)S(1)} %get-tuple-element.27), channel_id=1, source_target_pairs={{0,32},{1,65},{2,34},{3,67},{4,36},{5,69},{6,38},{7,71},{8,40},{9,... | collective-permute-start | bytes 393224 | tf_op jit(solution)/shard_map/ppermute | solution.py:269
  21.2 4.6 %collective-permute-start.3 = (bf16[256,256]{1,0:T(8,128)(2,1)S(1)}, bf16[256,256]{1,0:T(8,128)(2,1)S(1)}, u32[]{:S(2)}, u32[]{:S(2)}) collective-permute-start(bf16[256,256]{1,0:T(8,128)(2,1)S(1)} %get-tuple-element.28), channel_id=1, source_target_pairs={{0,8},{1,17},{2,10},{3,19},{4,12},{5,21},{6,14},{7,23},{8,0},{9,25... | collective-permute-start | bytes 393224 | tf_op jit(solution)/shard_map/ppermute | solution.py:269
  25.9 4.8 %collective-permute-start.4 = (bf16[256,256]{1,0:T(8,128)(2,1)S(1)}, bf16[256,256]{1,0:T(8,128)(2,1)S(1)}, u32[]{:S(2)}, u32[]{:S(2)}) collective-permute-start(bf16[256,256]{1,0:T(8,128)(2,1)S(1)} %get-tuple-element.25.refs_2_), channel_id=1, source_target_pairs={{0,2},{1,5},{2,0},{3,7},{4,6},{5,1},{6,4},{7,3},{8,10},{9,13},{10,... | collective-permute-start | bytes 393224 | tf_op jit(solution)/shard_map/ppermute | solution.py:269
  30.7 2.1 %shard_map.96.refs_0_.refs_4_ = bf16[1664,512]{1,0:T(8,128)(2,1)S(1)} custom-call(s32[10,512]{1,0:T(8,128)S(1)} %bitcast.6, s32[1,512]{1,0:T(1,128)S(1)} %bitcast.10, bf16[256,256]{1,0:T(8,128)(2,1)S(1)} %get-tuple-element.25.refs_2_), custom_call_target="tpu_custom_call" | custom-call | flops 2000000000 | bytes 2000000 | tf_op jit(solution)/shard_map/pallas_call | solution.py:24
  33.1 5.7 %collective-permute-start.5 = (bf16[512,256]{1,0:T(8,128)(2,1)S(1)}, bf16[512,256]{1,0:T(8,128)(2,1)S(1)}, u32[]{:S(2)}, u32[]{:S(2)}) collective-permute-start(bf16[512,256]{1,0:T(8,128)(2,1)S(1)} %shard_map.98), channel_id=1, source_target_pairs={{0,1},{1,0},{2,3},{3,2},{4,5},{5,4},{6,7},{7,6},{8,9},{9,8},{10,11... | collective-permute-start | bytes 786440 | tf_op jit(solution)/shard_map/ppermute | solution.py:265
  38.9 0.7 shard_map.97
  40.0 2.0 %shard_map.99 = (bf16[512,256]{1,0:T(8,128)(2,1)}, bf16[512,256]{1,0:T(8,128)(2,1)}, bf16[512,256]{1,0:T(8,128)(2,1)S(1)}, bf16[512,256]{1,0:T(8,128)(2,1)S(1)}) custom-call(bf16[1664,512]{1,0:T(8,128)(2,1)S(1)} %shard_map.96.refs_0_.refs_4_, f32[512,256]{1,0:T(8,128)S(1)} %get-tuple-element.29.refs_1_, f32[512,256]{1,0:T(8,128)S(1)} %get-tuple-element.30.refs_2_, ...), custom_call_target="tpu_custom_call" | custom-call | flops 2000000000 | bytes 5000000 | tf_op jit(solution)/shard_map/pallas_call | solution.py:24
  42.0 7.2 %all-to-all-start = ((bf16[32,16,256]{2,1,0:T(8,128)(2,1)}), bf16[32,16,256]{2,1,0:T(8,128)(2,1)S(1)}, u32[]{:S(2)}, u32[]{:S(2)}) async-start(bf16[32,16,256]{2,1,0:T(8,128)(2,1)} %bitcast.3), calls=%async_computation | async-start | bytes 524288 | tf_op jit(solution)/shard_map/all_to_all | solution.py:237
  49.2 0.7 shard_map.100
  49.9 2.1 %collective-permute-start.6 = (bf16[384,256]{1,0:T(8,128)(2,1)S(1)}, bf16[384,256]{1,0:T(8,128)(2,1)S(1)}, u32[]{:S(2)}, u32[]{:S(2)}) collective-permute-start(bf16[384,256]{1,0:T(8,128)(2,1)S(1)} %get-tuple-element.35), channel_id=1, source_target_pairs={{0,1},{1,0},{2,3},{3,2},{4,5},{5,4},{6,7},{7,6},{8,9},{9,8},{10,11... | collective-permute-start | bytes 589832 | tf_op jit(solution)/shard_map/ppermute | solution.py:265
  52.0 2.2 %collective-permute-start.7 = (bf16[256,256]{1,0:T(8,128)(2,1)S(1)}, bf16[256,256]{1,0:T(8,128)(2,1)S(1)}, u32[]{:S(2)}, u32[]{:S(2)}) collective-permute-start(bf16[256,256]{1,0:T(8,128)(2,1)S(1)} %get-tuple-element.37), channel_id=1, source_target_pairs={{0,1},{1,0},{2,3},{3,2},{4,5},{5,4},{6,7},{7,6},{8,9},{9,8},{10,11... | collective-permute-start | bytes 393224 | tf_op jit(solution)/shard_map/ppermute | solution.py:265
  54.2 1.1 %collective-permute-done.7.refs_1_ = bf16[256,256]{1,0:T(8,128)(2,1)S(1)} collective-permute-done((bf16[256,256]{1,0:T(8,128)(2,1)S(1)}, bf16[256,256]{1,0:T(8,128)(2,1)S(1)}, u32[]{:S(2)}, u32[]{:S(2)}) %collective-permute-start.7) | collective-permute-done | bytes 131104 | tf_op jit(solution)/shard_map/ppermute | solution.py:265
  55.3 2.9 %all-to-all-done.refs_0_ = bf16[32,16,256]{2,1,0:T(8,128)(2,1)S(1)} async-done(((bf16[32,16,256]{2,1,0:T(8,128)(2,1)}), bf16[32,16,256]{2,1,0:T(8,128)(2,1)S(1)}, u32[]{:S(2)}, u32[]{:S(2)}) %all-to-all-start) | async-done | bytes 262176 | tf_op jit(solution)/shard_map/all_to_all | solution.py:237
  58.2 0.7 shard_map.104
  58.9 6.2 %all-to-all-start.1 = ((bf16[16,16,256]{2,1,0:T(8,128)(2,1)}), bf16[16,16,256]{2,1,0:T(8,128)(2,1)S(1)}, u32[]{:S(2)}, u32[]{:S(2)}) async-start(bf16[16,16,256]{2,1,0:T(8,128)(2,1)} %shard_map.104), calls=%async_computation.1 | async-start | bytes 262144 | tf_op jit(solution)/shard_map/all_to_all | solution.py:237
  65.2 7.2 %collective-permute-start.8 = (bf16[256,256]{1,0:T(8,128)(2,1)S(1)}, bf16[256,256]{1,0:T(8,128)(2,1)S(1)}, u32[]{:S(2)}, u32[]{:S(2)}) collective-permute-start(bf16[256,256]{1,0:T(8,128)(2,1)S(1)} %get-tuple-element.38), channel_id=1, source_target_pairs={{0,256},{1,129},{2,258},{3,131},{4,260},{5,133},{6,262},{7,135},{8... | collective-permute-start | bytes 393224 | tf_op jit(solution)/shard_map/ppermute | solution.py:269
  72.3 4.0 %collective-permute-start.9 = (bf16[256,256]{1,0:T(8,128)(2,1)S(1)}, bf16[256,256]{1,0:T(8,128)(2,1)S(1)}, u32[]{:S(2)}, u32[]{:S(2)}) collective-permute-start(bf16[256,256]{1,0:T(8,128)(2,1)S(1)} %get-tuple-element.39), channel_id=1, source_target_pairs={{0,32},{1,65},{2,34},{3,67},{4,36},{5,69},{6,38},{7,71},{8,40},{9,... | collective-permute-start | bytes 393224 | tf_op jit(solution)/shard_map/ppermute | solution.py:269
  76.4 2.9 %collective-permute-start.10 = (bf16[256,256]{1,0:T(8,128)(2,1)S(1)}, bf16[256,256]{1,0:T(8,128)(2,1)S(1)}, u32[]{:S(2)}, u32[]{:S(2)}) collective-permute-start(bf16[256,256]{1,0:T(8,128)(2,1)S(1)} %get-tuple-element.40), channel_id=1, source_target_pairs={{0,8},{1,17},{2,10},{3,19},{4,12},{5,21},{6,14},{7,23},{8,0},{9,25... | collective-permute-start | bytes 393224 | tf_op jit(solution)/shard_map/ppermute | solution.py:269
  79.3 3.7 %collective-permute-start.11 = (bf16[256,256]{1,0:T(8,128)(2,1)S(1)}, bf16[256,256]{1,0:T(8,128)(2,1)S(1)}, u32[]{:S(2)}, u32[]{:S(2)}) collective-permute-start(bf16[256,256]{1,0:T(8,128)(2,1)S(1)} %get-tuple-element.41), channel_id=1, source_target_pairs={{0,2},{1,5},{2,0},{3,7},{4,6},{5,1},{6,4},{7,3},{8,10},{9,13},{10,... | collective-permute-start | bytes 393224 | tf_op jit(solution)/shard_map/ppermute | solution.py:269
  83.0 0.7 shard_map.105.refs_4_
  83.8 8.1 %all-to-all-start.2 = ((bf16[32,16,256]{2,1,0:T(8,128)(2,1)}), bf16[32,16,256]{2,1,0:T(8,128)(2,1)S(1)}, u32[]{:S(2)}, u32[]{:S(2)}) async-start(bf16[32,16,256]{2,1,0:T(8,128)(2,1)} %shard_map.105.refs_4_), calls=%async_computation.2 | async-start | bytes 524288 | tf_op jit(solution)/shard_map/all_to_all | solution.py:237
  92.0 2.1 %collective-permute-start.12 = (bf16[512,256]{1,0:T(8,128)(2,1)S(1)}, bf16[512,256]{1,0:T(8,128)(2,1)S(1)}, u32[]{:S(2)}, u32[]{:S(2)}) collective-permute-start(bf16[512,256]{1,0:T(8,128)(2,1)S(1)} %shard_map.106), channel_id=1, source_target_pairs={{0,1},{1,0},{2,3},{3,2},{4,5},{5,4},{6,7},{7,6},{8,9},{9,8},{10,11... | collective-permute-start | bytes 786440 | tf_op jit(solution)/shard_map/ppermute | solution.py:265
  94.2 0.5 shard_map.103.refs_1_
  94.6 6.3 %all-to-all-done.2 = bf16[32,16,256]{2,1,0:T(8,128)(2,1)S(1)} async-done(((bf16[32,16,256]{2,1,0:T(8,128)(2,1)}), bf16[32,16,256]{2,1,0:T(8,128)(2,1)S(1)}, u32[]{:S(2)}, u32[]{:S(2)}) %all-to-all-start.2) | async-done | bytes 262176 | tf_op jit(solution)/shard_map/all_to_all | solution.py:237
  100.9 1.1 %shard_map.108 = f32[512,256]{1,0:T(8,128)} custom-call(bf16[512,256]{1,0:T(8,128)(2,1)S(1)} %bitcast.5), custom_call_target="tpu_custom_call" | custom-call | flops 100000000 | bytes 1000000 | tf_op jit(solution)/shard_map/pallas_call | solution.py:24
  102.0 1.1 %shard_map.107 = bf16[512,256]{1,0:T(8,128)(2,1)} custom-call(s32[9,1,128]{2,1,0:T(1,128)S(1)} %bitcast.9, f32[512,256]{1,0:T(8,128)S(1)} %shard_map.103.refs_1_, bf16[512,256]{1,0:T(8,128)(2,1)S(1)} %collective-permute-done.12.refs_2_), custom_call_target="tpu_custom_call" | custom-call | flops 1000000000 | bytes 1000000 | tf_op jit(solution)/shard_map/pallas_call | solution.py:24
  (33 shorter events, 0.8 us)
Async XLA Ops:
  0.6 1.0 copy-start.1
  1.6 0.7 copy-start.6
  2.3 28.4 %copy-start.5 = (s32[512,10]{0,1:T(8,128)S(1)}, s32[512,10]{0,1:T(8,128)}, u32[]{:S(2)}) copy-start(s32[512,10]{0,1:T(8,128)} %param.10) | copy-start | bytes 61444
  2.3 28.5 %copy-start.8 = (s32[512]{0:T(512)S(1)}, s32[512]{0:T(512)}, u32[]{:S(2)}) copy-start(s32[512]{0:T(512)} %param.11) | copy-start | bytes 6148
  2.8 10.0 %collective-permute-start = (bf16[640,256]{1,0:T(8,128)(2,1)S(1)}, bf16[640,256]{1,0:T(8,128)(2,1)S(1)}, u32[]{:S(2)}, u32[]{:S(2)}) collective-permute-start(bf16[640,256]{1,0:T(8,128)(2,1)S(1)} %get-tuple-element.24), channel_id=1, source_target_pairs={{0,1},{1,0},{2,3},{3,2},{4,5},{5,4},{6,7},{7,6},{8,9},{9,8},{10,11... | collective-permute-start | bytes 983048 | tf_op jit(solution)/shard_map/ppermute | solution.py:265
  12.9 20.0 %collective-permute-start.1 = (bf16[256,256]{1,0:T(8,128)(2,1)S(1)}, bf16[256,256]{1,0:T(8,128)(2,1)S(1)}, u32[]{:S(2)}, u32[]{:S(2)}) collective-permute-start(bf16[256,256]{1,0:T(8,128)(2,1)S(1)} %get-tuple-element.26), channel_id=1, source_target_pairs={{0,256},{1,129},{2,258},{3,131},{4,260},{5,133},{6,262},{7,135},{8... | collective-permute-start | bytes 393224 | tf_op jit(solution)/shard_map/ppermute | solution.py:269
  16.3 16.6 %collective-permute-start.2 = (bf16[256,256]{1,0:T(8,128)(2,1)S(1)}, bf16[256,256]{1,0:T(8,128)(2,1)S(1)}, u32[]{:S(2)}, u32[]{:S(2)}) collective-permute-start(bf16[256,256]{1,0:T(8,128)(2,1)S(1)} %get-tuple-element.27), channel_id=1, source_target_pairs={{0,32},{1,65},{2,34},{3,67},{4,36},{5,69},{6,38},{7,71},{8,40},{9,... | collective-permute-start | bytes 393224 | tf_op jit(solution)/shard_map/ppermute | solution.py:269
  21.2 11.7 %collective-permute-start.3 = (bf16[256,256]{1,0:T(8,128)(2,1)S(1)}, bf16[256,256]{1,0:T(8,128)(2,1)S(1)}, u32[]{:S(2)}, u32[]{:S(2)}) collective-permute-start(bf16[256,256]{1,0:T(8,128)(2,1)S(1)} %get-tuple-element.28), channel_id=1, source_target_pairs={{0,8},{1,17},{2,10},{3,19},{4,12},{5,21},{6,14},{7,23},{8,0},{9,25... | collective-permute-start | bytes 393224 | tf_op jit(solution)/shard_map/ppermute | solution.py:269
  25.9 7.2 %collective-permute-start.4 = (bf16[256,256]{1,0:T(8,128)(2,1)S(1)}, bf16[256,256]{1,0:T(8,128)(2,1)S(1)}, u32[]{:S(2)}, u32[]{:S(2)}) collective-permute-start(bf16[256,256]{1,0:T(8,128)(2,1)S(1)} %get-tuple-element.25.refs_2_), channel_id=1, source_target_pairs={{0,2},{1,5},{2,0},{3,7},{4,6},{5,1},{6,4},{7,3},{8,10},{9,13},{10,... | collective-permute-start | bytes 393224 | tf_op jit(solution)/shard_map/ppermute | solution.py:269
  32.8 6.0 %copy-start = (bf16[256,256]{1,0:T(8,128)(2,1)S(1)}, bf16[256,256]{1,0:T(8,128)(2,1)}, u32[]{:S(2)}) copy-start(bf16[256,256]{1,0:T(8,128)(2,1)} %refs_3_.1) | copy-start | bytes 393220
  32.9 6.0 %copy-start.2 = (bf16[512,256]{1,0:T(8,128)(2,1)S(1)}, bf16[512,256]{1,0:T(8,128)(2,1)}, u32[]{:S(2)}) copy-start(bf16[512,256]{1,0:T(8,128)(2,1)} %refs_4_.1) | copy-start | bytes 786436
  33.1 6.9 %copy-start.3 = (bf16[512,256]{1,0:T(8,128)(2,1)S(1)}, bf16[512,256]{1,0:T(8,128)(2,1)}, u32[]{:S(2)}) copy-start(bf16[512,256]{1,0:T(8,128)(2,1)} %refs_6_.1) | copy-start | bytes 786436
  33.1 6.9 %copy-start.4 = (bf16[256,256]{1,0:T(8,128)(2,1)S(1)}, bf16[256,256]{1,0:T(8,128)(2,1)}, u32[]{:S(2)}) copy-start(bf16[256,256]{1,0:T(8,128)(2,1)} %refs_7_.1) | copy-start | bytes 393220
  33.1 6.9 %collective-permute-start.5 = (bf16[512,256]{1,0:T(8,128)(2,1)S(1)}, bf16[512,256]{1,0:T(8,128)(2,1)S(1)}, u32[]{:S(2)}, u32[]{:S(2)}) collective-permute-start(bf16[512,256]{1,0:T(8,128)(2,1)S(1)} %shard_map.98), channel_id=1, source_target_pairs={{0,1},{1,0},{2,3},{3,2},{4,5},{5,4},{6,7},{7,6},{8,9},{9,8},{10,11... | collective-permute-start | bytes 786440 | tf_op jit(solution)/shard_map/ppermute | solution.py:265
  42.0 16.2 %all-to-all-start = ((bf16[32,16,256]{2,1,0:T(8,128)(2,1)}), bf16[32,16,256]{2,1,0:T(8,128)(2,1)S(1)}, u32[]{:S(2)}, u32[]{:S(2)}) async-start(bf16[32,16,256]{2,1,0:T(8,128)(2,1)} %bitcast.3), calls=%async_computation | async-start | bytes 524288 | tf_op jit(solution)/shard_map/all_to_all | solution.py:237
  49.9 5.4 %collective-permute-start.6 = (bf16[384,256]{1,0:T(8,128)(2,1)S(1)}, bf16[384,256]{1,0:T(8,128)(2,1)S(1)}, u32[]{:S(2)}, u32[]{:S(2)}) collective-permute-start(bf16[384,256]{1,0:T(8,128)(2,1)S(1)} %get-tuple-element.35), channel_id=1, source_target_pairs={{0,1},{1,0},{2,3},{3,2},{4,5},{5,4},{6,7},{7,6},{8,9},{9,8},{10,11... | collective-permute-start | bytes 589832 | tf_op jit(solution)/shard_map/ppermute | solution.py:265
  52.0 3.2 %collective-permute-start.7 = (bf16[256,256]{1,0:T(8,128)(2,1)S(1)}, bf16[256,256]{1,0:T(8,128)(2,1)S(1)}, u32[]{:S(2)}, u32[]{:S(2)}) collective-permute-start(bf16[256,256]{1,0:T(8,128)(2,1)S(1)} %get-tuple-element.37), channel_id=1, source_target_pairs={{0,1},{1,0},{2,3},{3,2},{4,5},{5,4},{6,7},{7,6},{8,9},{9,8},{10,11... | collective-permute-start | bytes 393224 | tf_op jit(solution)/shard_map/ppermute | solution.py:265
  58.9 35.3 %copy-start.7 = (s32[1,9,128]{2,0,1:T(1,128)S(1)}, s32[1,9,128]{2,0,1:T(1,128)}, u32[]{:S(2)}) copy-start(s32[1,9,128]{2,0,1:T(1,128)} %param.12) | copy-start | bytes 13828
  58.9 24.1 %all-to-all-start.1 = ((bf16[16,16,256]{2,1,0:T(8,128)(2,1)}), bf16[16,16,256]{2,1,0:T(8,128)(2,1)S(1)}, u32[]{:S(2)}, u32[]{:S(2)}) async-start(bf16[16,16,256]{2,1,0:T(8,128)(2,1)} %shard_map.104), calls=%async_computation.1 | async-start | bytes 262144 | tf_op jit(solution)/shard_map/all_to_all | solution.py:237
  65.2 26.8 %collective-permute-start.8 = (bf16[256,256]{1,0:T(8,128)(2,1)S(1)}, bf16[256,256]{1,0:T(8,128)(2,1)S(1)}, u32[]{:S(2)}, u32[]{:S(2)}) collective-permute-start(bf16[256,256]{1,0:T(8,128)(2,1)S(1)} %get-tuple-element.38), channel_id=1, source_target_pairs={{0,256},{1,129},{2,258},{3,131},{4,260},{5,133},{6,262},{7,135},{8... | collective-permute-start | bytes 393224 | tf_op jit(solution)/shard_map/ppermute | solution.py:269
  72.3 19.6 %collective-permute-start.9 = (bf16[256,256]{1,0:T(8,128)(2,1)S(1)}, bf16[256,256]{1,0:T(8,128)(2,1)S(1)}, u32[]{:S(2)}, u32[]{:S(2)}) collective-permute-start(bf16[256,256]{1,0:T(8,128)(2,1)S(1)} %get-tuple-element.39), channel_id=1, source_target_pairs={{0,32},{1,65},{2,34},{3,67},{4,36},{5,69},{6,38},{7,71},{8,40},{9,... | collective-permute-start | bytes 393224 | tf_op jit(solution)/shard_map/ppermute | solution.py:269
  76.4 15.6 %collective-permute-start.10 = (bf16[256,256]{1,0:T(8,128)(2,1)S(1)}, bf16[256,256]{1,0:T(8,128)(2,1)S(1)}, u32[]{:S(2)}, u32[]{:S(2)}) collective-permute-start(bf16[256,256]{1,0:T(8,128)(2,1)S(1)} %get-tuple-element.40), channel_id=1, source_target_pairs={{0,8},{1,17},{2,10},{3,19},{4,12},{5,21},{6,14},{7,23},{8,0},{9,25... | collective-permute-start | bytes 393224 | tf_op jit(solution)/shard_map/ppermute | solution.py:269
  79.3 12.6 %collective-permute-start.11 = (bf16[256,256]{1,0:T(8,128)(2,1)S(1)}, bf16[256,256]{1,0:T(8,128)(2,1)S(1)}, u32[]{:S(2)}, u32[]{:S(2)}) collective-permute-start(bf16[256,256]{1,0:T(8,128)(2,1)S(1)} %get-tuple-element.41), channel_id=1, source_target_pairs={{0,2},{1,5},{2,0},{3,7},{4,6},{5,1},{6,4},{7,3},{8,10},{9,13},{10,... | collective-permute-start | bytes 393224 | tf_op jit(solution)/shard_map/ppermute | solution.py:269
  83.8 17.1 %all-to-all-start.2 = ((bf16[32,16,256]{2,1,0:T(8,128)(2,1)}), bf16[32,16,256]{2,1,0:T(8,128)(2,1)S(1)}, u32[]{:S(2)}, u32[]{:S(2)}) async-start(bf16[32,16,256]{2,1,0:T(8,128)(2,1)} %shard_map.105.refs_4_), calls=%async_computation.2 | async-start | bytes 524288 | tf_op jit(solution)/shard_map/all_to_all | solution.py:237
  92.0 10.0 %collective-permute-start.12 = (bf16[512,256]{1,0:T(8,128)(2,1)S(1)}, bf16[512,256]{1,0:T(8,128)(2,1)S(1)}, u32[]{:S(2)}, u32[]{:S(2)}) collective-permute-start(bf16[512,256]{1,0:T(8,128)(2,1)S(1)} %shard_map.106), channel_id=1, source_target_pairs={{0,1},{1,0},{2,3},{3,2},{4,5},{5,4},{6,7},{7,6},{8,9},{9,8},{10,11... | collective-permute-start | bytes 786440 | tf_op jit(solution)/shard_map/ppermute | solution.py:265

commit v4 on v3

--- a/solution.py
+++ b/solution.py
@@ -258,6 +258,7 @@
     load_shape = shape((2 * bnd, width), bf16)
     near = bit_groups(devices, range(FAST_BITS))
     far = bit_groups(devices, range(FAST_BITS, levels))
+    far = [group[len(group) // 2 :] + group[: len(group) // 2] for group in far]
     piece = 2 * width // len(near[0])
     small = (10**8, 10**6)
 

time: 104 us -> 100 us (0.962)
  starting transfers between devices: 78.2 us -> 74.4 us
    ppermute x8, starting transfers between devices: 35.6 us -> 28.8 us  [across(): lax.ppermute(x, 'dom', [(i, i ^ 1 << pair[i % 2]) for i in range(devices)])]
    all_to_all x3, starting transfers between devices: 21.5 us -> 24.8 us  [exchange(): return lax.all_to_all(x, 'dom', 0, 0, axis_index_groups=groups, tiled=True)]
  transfers between devices with their start and end apart: 16 -> 16, of which waited for: 6 -> 7; matrix products, arithmetic and copies ran while one was open for 0% -> 0% of each run, Pallas kernels for 6% -> 6%
where the time goes in v4:
time: 100 us; the launch traced here: 99.6 us
  starting transfers between devices  74.4 us (74%)
  waiting for transfers between devices  12.3 us (12%)
  Pallas kernels  10.3 us (10%)
  local copies, waits for them, and re-layouts  1.67 us (2%)
    ppermute x8, starting transfers between devices, across(): lax.ppermute(x, 'dom', [(i, i ^ 1 << pair[i % 2]) for i in range(devices)])  28.8 us
    all_to_all x3, starting transfers between devices, exchange(): return lax.all_to_all(x, 'dom', 0, 0, axis_index_groups=groups, tiled=True)  24.8 us
    ppermute x5, starting transfers between devices, other_core(): return lax.ppermute(x, 'dom', [(i, i ^ 1) for i in range(devices)])  20.8 us
    pallas_call x15, Pallas kernels, call(): pl.pallas_call(lambda *refs: body(*refs[:reads], *refs[reads + waits:]),...  10.3 us
    all_to_all x3, waiting for transfers between devices, exchange(): return lax.all_to_all(x, 'dom', 0, 0, axis_index_groups=groups, tiled=True)  8.5 us
    ppermute x5, waiting for transfers between devices, other_core(): return lax.ppermute(x, 'dom', [(i, i ^ 1) for i in range(devices)])  2.67 us
  transfers between devices with their start and end apart: 16, of which 7 were waited for; matrix products, arithmetic and copies ran while one was open for 0% of the time, Pallas kernels for 6%

profile of v4, /device:TPU:1, one launch (start us, length us, event | category | flops | bytes accessed | tf_op | source)
XLA Modules:
  0.0 99.6 jit_solution(8650742017384732888)
XLA Ops:
  0.6 0.9 copy-done.1
  1.6 0.7 copy-done.6
  2.3 0.5 shard_map.94
  2.8 8.8 %collective-permute-start = (bf16[640,256]{1,0:T(8,128)(2,1)S(1)}, bf16[640,256]{1,0:T(8,128)(2,1)S(1)}, u32[]{:S(2)}, u32[]{:S(2)}) collective-permute-start(bf16[640,256]{1,0:T(8,128)(2,1)S(1)} %get-tuple-element.24), channel_id=1, source_target_pairs={{0,1},{1,0},{2,3},{3,2},{4,5},{5,4},{6,7},{7,6},{8,9},{9,8},{10,11... | collective-permute-start | bytes 983048 | tf_op jit(solution)/shard_map/ppermute | solution.py:266
  11.6 1.2 %collective-permute-done.refs_1_.refs_3_ = bf16[640,256]{1,0:T(8,128)(2,1)S(1)} collective-permute-done((bf16[640,256]{1,0:T(8,128)(2,1)S(1)}, bf16[640,256]{1,0:T(8,128)(2,1)S(1)}, u32[]{:S(2)}, u32[]{:S(2)}) %collective-permute-start) | collective-permute-done | bytes 327712 | tf_op jit(solution)/shard_map/ppermute | solution.py:266
  12.9 3.4 %collective-permute-start.1 = (bf16[256,256]{1,0:T(8,128)(2,1)S(1)}, bf16[256,256]{1,0:T(8,128)(2,1)S(1)}, u32[]{:S(2)}, u32[]{:S(2)}) collective-permute-start(bf16[256,256]{1,0:T(8,128)(2,1)S(1)} %get-tuple-element.26), channel_id=1, source_target_pairs={{0,256},{1,129},{2,258},{3,131},{4,260},{5,133},{6,262},{7,135},{8... | collective-permute-start | bytes 393224 | tf_op jit(solution)/shard_map/ppermute | solution.py:270
  16.3 4.9 %collective-permute-start.2 = (bf16[256,256]{1,0:T(8,128)(2,1)S(1)}, bf16[256,256]{1,0:T(8,128)(2,1)S(1)}, u32[]{:S(2)}, u32[]{:S(2)}) collective-permute-start(bf16[256,256]{1,0:T(8,128)(2,1)S(1)} %get-tuple-element.27), channel_id=1, source_target_pairs={{0,32},{1,65},{2,34},{3,67},{4,36},{5,69},{6,38},{7,71},{8,40},{9,... | collective-permute-start | bytes 393224 | tf_op jit(solution)/shard_map/ppermute | solution.py:270
  21.2 4.6 %collective-permute-start.3 = (bf16[256,256]{1,0:T(8,128)(2,1)S(1)}, bf16[256,256]{1,0:T(8,128)(2,1)S(1)}, u32[]{:S(2)}, u32[]{:S(2)}) collective-permute-start(bf16[256,256]{1,0:T(8,128)(2,1)S(1)} %get-tuple-element.28), channel_id=1, source_target_pairs={{0,8},{1,17},{2,10},{3,19},{4,12},{5,21},{6,14},{7,23},{8,0},{9,25... | collective-permute-start | bytes 393224 | tf_op jit(solution)/shard_map/ppermute | solution.py:270
  25.9 4.8 %collective-permute-start.4 = (bf16[256,256]{1,0:T(8,128)(2,1)S(1)}, bf16[256,256]{1,0:T(8,128)(2,1)S(1)}, u32[]{:S(2)}, u32[]{:S(2)}) collective-permute-start(bf16[256,256]{1,0:T(8,128)(2,1)S(1)} %get-tuple-element.25.refs_2_), channel_id=1, source_target_pairs={{0,2},{1,5},{2,0},{3,7},{4,6},{5,1},{6,4},{7,3},{8,10},{9,13},{10,... | collective-permute-start | bytes 393224 | tf_op jit(solution)/shard_map/ppermute | solution.py:270
  30.7 2.1 %shard_map.96.refs_0_.refs_4_ = bf16[1664,512]{1,0:T(8,128)(2,1)S(1)} custom-call(s32[10,512]{1,0:T(8,128)S(1)} %bitcast.6, s32[1,512]{1,0:T(1,128)S(1)} %bitcast.10, bf16[256,256]{1,0:T(8,128)(2,1)S(1)} %get-tuple-element.25.refs_2_), custom_call_target="tpu_custom_call" | custom-call | flops 2000000000 | bytes 2000000 | tf_op jit(solution)/shard_map/pallas_call | solution.py:24
  33.1 5.7 %collective-permute-start.5 = (bf16[512,256]{1,0:T(8,128)(2,1)S(1)}, bf16[512,256]{1,0:T(8,128)(2,1)S(1)}, u32[]{:S(2)}, u32[]{:S(2)}) collective-permute-start(bf16[512,256]{1,0:T(8,128)(2,1)S(1)} %shard_map.98), channel_id=1, source_target_pairs={{0,1},{1,0},{2,3},{3,2},{4,5},{5,4},{6,7},{7,6},{8,9},{9,8},{10,11... | collective-permute-start | bytes 786440 | tf_op jit(solution)/shard_map/ppermute | solution.py:266
  38.9 0.7 shard_map.97
  40.0 2.0 %shard_map.99 = (bf16[512,256]{1,0:T(8,128)(2,1)}, bf16[512,256]{1,0:T(8,128)(2,1)}, bf16[512,256]{1,0:T(8,128)(2,1)S(1)}, bf16[512,256]{1,0:T(8,128)(2,1)S(1)}) custom-call(bf16[1664,512]{1,0:T(8,128)(2,1)S(1)} %shard_map.96.refs_0_.refs_4_, f32[512,256]{1,0:T(8,128)S(1)} %get-tuple-element.29.refs_1_, f32[512,256]{1,0:T(8,128)S(1)} %get-tuple-element.30.refs_2_, ...), custom_call_target="tpu_custom_call" | custom-call | flops 2000000000 | bytes 5000000 | tf_op jit(solution)/shard_map/pallas_call | solution.py:24
  42.0 7.2 %all-to-all-start = ((bf16[32,16,256]{2,1,0:T(8,128)(2,1)}), bf16[32,16,256]{2,1,0:T(8,128)(2,1)S(1)}, u32[]{:S(2)}, u32[]{:S(2)}) async-start(bf16[32,16,256]{2,1,0:T(8,128)(2,1)} %bitcast.3), calls=%async_computation | async-start | bytes 524288 | tf_op jit(solution)/shard_map/all_to_all | solution.py:237
  49.2 0.7 shard_map.100
  49.9 2.1 %collective-permute-start.6 = (bf16[384,256]{1,0:T(8,128)(2,1)S(1)}, bf16[384,256]{1,0:T(8,128)(2,1)S(1)}, u32[]{:S(2)}, u32[]{:S(2)}) collective-permute-start(bf16[384,256]{1,0:T(8,128)(2,1)S(1)} %get-tuple-element.35), channel_id=1, source_target_pairs={{0,1},{1,0},{2,3},{3,2},{4,5},{5,4},{6,7},{7,6},{8,9},{9,8},{10,11... | collective-permute-start | bytes 589832 | tf_op jit(solution)/shard_map/ppermute | solution.py:266
  52.0 2.2 %collective-permute-start.7 = (bf16[256,256]{1,0:T(8,128)(2,1)S(1)}, bf16[256,256]{1,0:T(8,128)(2,1)S(1)}, u32[]{:S(2)}, u32[]{:S(2)}) collective-permute-start(bf16[256,256]{1,0:T(8,128)(2,1)S(1)} %get-tuple-element.37), channel_id=1, source_target_pairs={{0,1},{1,0},{2,3},{3,2},{4,5},{5,4},{6,7},{7,6},{8,9},{9,8},{10,11... | collective-permute-start | bytes 393224 | tf_op jit(solution)/shard_map/ppermute | solution.py:266
  54.2 1.1 %collective-permute-done.7.refs_1_ = bf16[256,256]{1,0:T(8,128)(2,1)S(1)} collective-permute-done((bf16[256,256]{1,0:T(8,128)(2,1)S(1)}, bf16[256,256]{1,0:T(8,128)(2,1)S(1)}, u32[]{:S(2)}, u32[]{:S(2)}) %collective-permute-start.7) | collective-permute-done | bytes 131104 | tf_op jit(solution)/shard_map/ppermute | solution.py:266
  55.3 2.9 %all-to-all-done.refs_0_ = bf16[32,16,256]{2,1,0:T(8,128)(2,1)S(1)} async-done(((bf16[32,16,256]{2,1,0:T(8,128)(2,1)}), bf16[32,16,256]{2,1,0:T(8,128)(2,1)S(1)}, u32[]{:S(2)}, u32[]{:S(2)}) %all-to-all-start) | async-done | bytes 262176 | tf_op jit(solution)/shard_map/all_to_all | solution.py:237
  58.2 0.7 shard_map.104
  58.9 11.6 %all-to-all-start.1 = ((bf16[16,16,256]{2,1,0:T(8,128)(2,1)}), bf16[16,16,256]{2,1,0:T(8,128)(2,1)S(1)}, u32[]{:S(2)}, u32[]{:S(2)}) async-start(bf16[16,16,256]{2,1,0:T(8,128)(2,1)} %shard_map.104), calls=%async_computation.1 | async-start | bytes 262144 | tf_op jit(solution)/shard_map/all_to_all | solution.py:237
  70.5 2.2 %collective-permute-start.8 = (bf16[256,256]{1,0:T(8,128)(2,1)S(1)}, bf16[256,256]{1,0:T(8,128)(2,1)S(1)}, u32[]{:S(2)}, u32[]{:S(2)}) collective-permute-start(bf16[256,256]{1,0:T(8,128)(2,1)S(1)} %get-tuple-element.38), channel_id=1, source_target_pairs={{0,256},{1,129},{2,258},{3,131},{4,260},{5,133},{6,262},{7,135},{8... | collective-permute-start | bytes 393224 | tf_op jit(solution)/shard_map/ppermute | solution.py:270
  72.7 2.2 %collective-permute-start.9 = (bf16[256,256]{1,0:T(8,128)(2,1)S(1)}, bf16[256,256]{1,0:T(8,128)(2,1)S(1)}, u32[]{:S(2)}, u32[]{:S(2)}) collective-permute-start(bf16[256,256]{1,0:T(8,128)(2,1)S(1)} %get-tuple-element.39), channel_id=1, source_target_pairs={{0,32},{1,65},{2,34},{3,67},{4,36},{5,69},{6,38},{7,71},{8,40},{9,... | collective-permute-start | bytes 393224 | tf_op jit(solution)/shard_map/ppermute | solution.py:270
  74.9 2.9 %collective-permute-start.10 = (bf16[256,256]{1,0:T(8,128)(2,1)S(1)}, bf16[256,256]{1,0:T(8,128)(2,1)S(1)}, u32[]{:S(2)}, u32[]{:S(2)}) collective-permute-start(bf16[256,256]{1,0:T(8,128)(2,1)S(1)} %get-tuple-element.40), channel_id=1, source_target_pairs={{0,8},{1,17},{2,10},{3,19},{4,12},{5,21},{6,14},{7,23},{8,0},{9,25... | collective-permute-start | bytes 393224 | tf_op jit(solution)/shard_map/ppermute | solution.py:270
  77.9 3.7 %collective-permute-start.11 = (bf16[256,256]{1,0:T(8,128)(2,1)S(1)}, bf16[256,256]{1,0:T(8,128)(2,1)S(1)}, u32[]{:S(2)}, u32[]{:S(2)}) collective-permute-start(bf16[256,256]{1,0:T(8,128)(2,1)S(1)} %get-tuple-element.41), channel_id=1, source_target_pairs={{0,2},{1,5},{2,0},{3,7},{4,6},{5,1},{6,4},{7,3},{8,10},{9,13},{10,... | collective-permute-start | bytes 393224 | tf_op jit(solution)/shard_map/ppermute | solution.py:270
  81.6 0.7 shard_map.105.refs_4_
  82.4 6.0 %all-to-all-start.2 = ((bf16[32,16,256]{2,1,0:T(8,128)(2,1)}), bf16[32,16,256]{2,1,0:T(8,128)(2,1)S(1)}, u32[]{:S(2)}, u32[]{:S(2)}) async-start(bf16[32,16,256]{2,1,0:T(8,128)(2,1)} %shard_map.105.refs_4_), calls=%async_computation.2 | async-start | bytes 524288 | tf_op jit(solution)/shard_map/all_to_all | solution.py:237
  88.4 0.9 collective-permute-done.8.refs_3_.refs_0_
  89.3 1.9 %collective-permute-start.12 = (bf16[512,256]{1,0:T(8,128)(2,1)S(1)}, bf16[512,256]{1,0:T(8,128)(2,1)S(1)}, u32[]{:S(2)}, u32[]{:S(2)}) collective-permute-start(bf16[512,256]{1,0:T(8,128)(2,1)S(1)} %shard_map.106), channel_id=1, source_target_pairs={{0,1},{1,0},{2,3},{3,2},{4,5},{5,4},{6,7},{7,6},{8,9},{9,8},{10,11... | collective-permute-start | bytes 786440 | tf_op jit(solution)/shard_map/ppermute | solution.py:266
  91.8 5.6 %all-to-all-done.2 = bf16[32,16,256]{2,1,0:T(8,128)(2,1)S(1)} async-done(((bf16[32,16,256]{2,1,0:T(8,128)(2,1)}), bf16[32,16,256]{2,1,0:T(8,128)(2,1)S(1)}, u32[]{:S(2)}, u32[]{:S(2)}) %all-to-all-start.2) | async-done | bytes 262176 | tf_op jit(solution)/shard_map/all_to_all | solution.py:237
  97.4 1.1 %shard_map.108 = f32[512,256]{1,0:T(8,128)} custom-call(bf16[512,256]{1,0:T(8,128)(2,1)S(1)} %bitcast.5), custom_call_target="tpu_custom_call" | custom-call | flops 100000000 | bytes 1000000 | tf_op jit(solution)/shard_map/pallas_call | solution.py:24
  98.4 1.1 %shard_map.107 = bf16[512,256]{1,0:T(8,128)(2,1)} custom-call(s32[9,1,128]{2,1,0:T(1,128)S(1)} %bitcast.9, f32[512,256]{1,0:T(8,128)S(1)} %shard_map.103.refs_1_, bf16[512,256]{1,0:T(8,128)(2,1)S(1)} %collective-permute-done.12.refs_2_), custom_call_target="tpu_custom_call" | custom-call | flops 1000000000 | bytes 1000000 | tf_op jit(solution)/shard_map/pallas_call | solution.py:24
  (33 shorter events, 1.2 us)
Async XLA Ops:
  0.6 1.0 copy-start.1
  1.6 0.7 copy-start.6
  2.3 28.4 %copy-start.5 = (s32[512,10]{0,1:T(8,128)S(1)}, s32[512,10]{0,1:T(8,128)}, u32[]{:S(2)}) copy-start(s32[512,10]{0,1:T(8,128)} %param.10) | copy-start | bytes 61444
  2.3 28.5 %copy-start.8 = (s32[512]{0:T(512)S(1)}, s32[512]{0:T(512)}, u32[]{:S(2)}) copy-start(s32[512]{0:T(512)} %param.11) | copy-start | bytes 6148
  2.8 10.0 %collective-permute-start = (bf16[640,256]{1,0:T(8,128)(2,1)S(1)}, bf16[640,256]{1,0:T(8,128)(2,1)S(1)}, u32[]{:S(2)}, u32[]{:S(2)}) collective-permute-start(bf16[640,256]{1,0:T(8,128)(2,1)S(1)} %get-tuple-element.24), channel_id=1, source_target_pairs={{0,1},{1,0},{2,3},{3,2},{4,5},{5,4},{6,7},{7,6},{8,9},{9,8},{10,11... | collective-permute-start | bytes 983048 | tf_op jit(solution)/shard_map/ppermute | solution.py:266
  12.9 20.0 %collective-permute-start.1 = (bf16[256,256]{1,0:T(8,128)(2,1)S(1)}, bf16[256,256]{1,0:T(8,128)(2,1)S(1)}, u32[]{:S(2)}, u32[]{:S(2)}) collective-permute-start(bf16[256,256]{1,0:T(8,128)(2,1)S(1)} %get-tuple-element.26), channel_id=1, source_target_pairs={{0,256},{1,129},{2,258},{3,131},{4,260},{5,133},{6,262},{7,135},{8... | collective-permute-start | bytes 393224 | tf_op jit(solution)/shard_map/ppermute | solution.py:270
  16.3 16.6 %collective-permute-start.2 = (bf16[256,256]{1,0:T(8,128)(2,1)S(1)}, bf16[256,256]{1,0:T(8,128)(2,1)S(1)}, u32[]{:S(2)}, u32[]{:S(2)}) collective-permute-start(bf16[256,256]{1,0:T(8,128)(2,1)S(1)} %get-tuple-element.27), channel_id=1, source_target_pairs={{0,32},{1,65},{2,34},{3,67},{4,36},{5,69},{6,38},{7,71},{8,40},{9,... | collective-permute-start | bytes 393224 | tf_op jit(solution)/shard_map/ppermute | solution.py:270
  21.2 11.7 %collective-permute-start.3 = (bf16[256,256]{1,0:T(8,128)(2,1)S(1)}, bf16[256,256]{1,0:T(8,128)(2,1)S(1)}, u32[]{:S(2)}, u32[]{:S(2)}) collective-permute-start(bf16[256,256]{1,0:T(8,128)(2,1)S(1)} %get-tuple-element.28), channel_id=1, source_target_pairs={{0,8},{1,17},{2,10},{3,19},{4,12},{5,21},{6,14},{7,23},{8,0},{9,25... | collective-permute-start | bytes 393224 | tf_op jit(solution)/shard_map/ppermute | solution.py:270
  25.9 7.2 %collective-permute-start.4 = (bf16[256,256]{1,0:T(8,128)(2,1)S(1)}, bf16[256,256]{1,0:T(8,128)(2,1)S(1)}, u32[]{:S(2)}, u32[]{:S(2)}) collective-permute-start(bf16[256,256]{1,0:T(8,128)(2,1)S(1)} %get-tuple-element.25.refs_2_), channel_id=1, source_target_pairs={{0,2},{1,5},{2,0},{3,7},{4,6},{5,1},{6,4},{7,3},{8,10},{9,13},{10,... | collective-permute-start | bytes 393224 | tf_op jit(solution)/shard_map/ppermute | solution.py:270
  32.8 6.0 %copy-start = (bf16[256,256]{1,0:T(8,128)(2,1)S(1)}, bf16[256,256]{1,0:T(8,128)(2,1)}, u32[]{:S(2)}) copy-start(bf16[256,256]{1,0:T(8,128)(2,1)} %refs_3_.1) | copy-start | bytes 393220
  32.9 6.0 %copy-start.2 = (bf16[512,256]{1,0:T(8,128)(2,1)S(1)}, bf16[512,256]{1,0:T(8,128)(2,1)}, u32[]{:S(2)}) copy-start(bf16[512,256]{1,0:T(8,128)(2,1)} %refs_4_.1) | copy-start | bytes 786436
  33.1 6.9 %copy-start.3 = (bf16[512,256]{1,0:T(8,128)(2,1)S(1)}, bf16[512,256]{1,0:T(8,128)(2,1)}, u32[]{:S(2)}) copy-start(bf16[512,256]{1,0:T(8,128)(2,1)} %refs_6_.1) | copy-start | bytes 786436
  33.1 6.9 %copy-start.4 = (bf16[256,256]{1,0:T(8,128)(2,1)S(1)}, bf16[256,256]{1,0:T(8,128)(2,1)}, u32[]{:S(2)}) copy-start(bf16[256,256]{1,0:T(8,128)(2,1)} %refs_7_.1) | copy-start | bytes 393220
  33.1 6.9 %collective-permute-start.5 = (bf16[512,256]{1,0:T(8,128)(2,1)S(1)}, bf16[512,256]{1,0:T(8,128)(2,1)S(1)}, u32[]{:S(2)}, u32[]{:S(2)}) collective-permute-start(bf16[512,256]{1,0:T(8,128)(2,1)S(1)} %shard_map.98), channel_id=1, source_target_pairs={{0,1},{1,0},{2,3},{3,2},{4,5},{5,4},{6,7},{7,6},{8,9},{9,8},{10,11... | collective-permute-start | bytes 786440 | tf_op jit(solution)/shard_map/ppermute | solution.py:266
  42.0 16.2 %all-to-all-start = ((bf16[32,16,256]{2,1,0:T(8,128)(2,1)}), bf16[32,16,256]{2,1,0:T(8,128)(2,1)S(1)}, u32[]{:S(2)}, u32[]{:S(2)}) async-start(bf16[32,16,256]{2,1,0:T(8,128)(2,1)} %bitcast.3), calls=%async_computation | async-start | bytes 524288 | tf_op jit(solution)/shard_map/all_to_all | solution.py:237
  49.9 5.4 %collective-permute-start.6 = (bf16[384,256]{1,0:T(8,128)(2,1)S(1)}, bf16[384,256]{1,0:T(8,128)(2,1)S(1)}, u32[]{:S(2)}, u32[]{:S(2)}) collective-permute-start(bf16[384,256]{1,0:T(8,128)(2,1)S(1)} %get-tuple-element.35), channel_id=1, source_target_pairs={{0,1},{1,0},{2,3},{3,2},{4,5},{5,4},{6,7},{7,6},{8,9},{9,8},{10,11... | collective-permute-start | bytes 589832 | tf_op jit(solution)/shard_map/ppermute | solution.py:266
  52.0 3.2 %collective-permute-start.7 = (bf16[256,256]{1,0:T(8,128)(2,1)S(1)}, bf16[256,256]{1,0:T(8,128)(2,1)S(1)}, u32[]{:S(2)}, u32[]{:S(2)}) collective-permute-start(bf16[256,256]{1,0:T(8,128)(2,1)S(1)} %get-tuple-element.37), channel_id=1, source_target_pairs={{0,1},{1,0},{2,3},{3,2},{4,5},{5,4},{6,7},{7,6},{8,9},{9,8},{10,11... | collective-permute-start | bytes 393224 | tf_op jit(solution)/shard_map/ppermute | solution.py:266
  58.9 32.4 %copy-start.7 = (s32[1,9,128]{2,0,1:T(1,128)S(1)}, s32[1,9,128]{2,0,1:T(1,128)}, u32[]{:S(2)}) copy-start(s32[1,9,128]{2,0,1:T(1,128)} %param.12) | copy-start | bytes 13828
  58.9 22.7 %all-to-all-start.1 = ((bf16[16,16,256]{2,1,0:T(8,128)(2,1)}), bf16[16,16,256]{2,1,0:T(8,128)(2,1)S(1)}, u32[]{:S(2)}, u32[]{:S(2)}) async-start(bf16[16,16,256]{2,1,0:T(8,128)(2,1)} %shard_map.104), calls=%async_computation.1 | async-start | bytes 262144 | tf_op jit(solution)/shard_map/all_to_all | solution.py:237
  70.5 18.8 %collective-permute-start.8 = (bf16[256,256]{1,0:T(8,128)(2,1)S(1)}, bf16[256,256]{1,0:T(8,128)(2,1)S(1)}, u32[]{:S(2)}, u32[]{:S(2)}) collective-permute-start(bf16[256,256]{1,0:T(8,128)(2,1)S(1)} %get-tuple-element.38), channel_id=1, source_target_pairs={{0,256},{1,129},{2,258},{3,131},{4,260},{5,133},{6,262},{7,135},{8... | collective-permute-start | bytes 393224 | tf_op jit(solution)/shard_map/ppermute | solution.py:270
  72.7 16.6 %collective-permute-start.9 = (bf16[256,256]{1,0:T(8,128)(2,1)S(1)}, bf16[256,256]{1,0:T(8,128)(2,1)S(1)}, u32[]{:S(2)}, u32[]{:S(2)}) collective-permute-start(bf16[256,256]{1,0:T(8,128)(2,1)S(1)} %get-tuple-element.39), channel_id=1, source_target_pairs={{0,32},{1,65},{2,34},{3,67},{4,36},{5,69},{6,38},{7,71},{8,40},{9,... | collective-permute-start | bytes 393224 | tf_op jit(solution)/shard_map/ppermute | solution.py:270
  74.9 14.3 %collective-permute-start.10 = (bf16[256,256]{1,0:T(8,128)(2,1)S(1)}, bf16[256,256]{1,0:T(8,128)(2,1)S(1)}, u32[]{:S(2)}, u32[]{:S(2)}) collective-permute-start(bf16[256,256]{1,0:T(8,128)(2,1)S(1)} %get-tuple-element.40), channel_id=1, source_target_pairs={{0,8},{1,17},{2,10},{3,19},{4,12},{5,21},{6,14},{7,23},{8,0},{9,25... | collective-permute-start | bytes 393224 | tf_op jit(solution)/shard_map/ppermute | solution.py:270
  77.9 11.4 %collective-permute-start.11 = (bf16[256,256]{1,0:T(8,128)(2,1)S(1)}, bf16[256,256]{1,0:T(8,128)(2,1)S(1)}, u32[]{:S(2)}, u32[]{:S(2)}) collective-permute-start(bf16[256,256]{1,0:T(8,128)(2,1)S(1)} %get-tuple-element.41), channel_id=1, source_target_pairs={{0,2},{1,5},{2,0},{3,7},{4,6},{5,1},{6,4},{7,3},{8,10},{9,13},{10,... | collective-permute-start | bytes 393224 | tf_op jit(solution)/shard_map/ppermute | solution.py:270
  82.4 15.0 %all-to-all-start.2 = ((bf16[32,16,256]{2,1,0:T(8,128)(2,1)}), bf16[32,16,256]{2,1,0:T(8,128)(2,1)S(1)}, u32[]{:S(2)}, u32[]{:S(2)}) async-start(bf16[32,16,256]{2,1,0:T(8,128)(2,1)} %shard_map.105.refs_4_), calls=%async_computation.2 | async-start | bytes 524288 | tf_op jit(solution)/shard_map/all_to_all | solution.py:237
  89.3 9.1 %collective-permute-start.12 = (bf16[512,256]{1,0:T(8,128)(2,1)S(1)}, bf16[512,256]{1,0:T(8,128)(2,1)S(1)}, u32[]{:S(2)}, u32[]{:S(2)}) collective-permute-start(bf16[512,256]{1,0:T(8,128)(2,1)S(1)} %shard_map.106), channel_id=1, source_target_pairs={{0,1},{1,0},{2,3},{3,2},{4,5},{5,4},{6,7},{7,6},{8,9},{9,8},{10,11... | collective-permute-start | bytes 786440 | tf_op jit(solution)/shard_map/ppermute | solution.py:266

commit v5 on v4

--- a/solution.py
+++ b/solution.py
@@ -9,6 +9,7 @@
 f32 = jnp.float32
 bf16 = jnp.bfloat16
 FAST_BITS = 5
+NEAR_FIRST = 20
 VMEM_LIMIT = 16 * 1024 * 1024
 TRANSPOSED_LHS = (((0,), (0,)), ((), ()))
 TRANSPOSED_RHS = (((1,), (1,)), ((), ()))
@@ -259,6 +260,7 @@
     near = bit_groups(devices, range(FAST_BITS))
     far = bit_groups(devices, range(FAST_BITS, levels))
     far = [group[len(group) // 2 :] + group[: len(group) // 2] for group in far]
+    near = [group[NEAR_FIRST:] + group[:NEAR_FIRST] for group in near]
     piece = 2 * width // len(near[0])
     small = (10**8, 10**6)
 

time: 100 us -> 96.4 us (0.964)
  waiting for transfers between devices: 12.3 us -> 4.23 us
  starting transfers between devices: 74.4 us -> 78.5 us
    all_to_all x3, waiting for transfers between devices: 8.5 us -> 1.22 us  [exchange(): return lax.all_to_all(x, 'dom', 0, 0, axis_index_groups=groups, tiled=True)]
    all_to_all x3, starting transfers between devices: 24.8 us -> 28.2 us  [exchange(): return lax.all_to_all(x, 'dom', 0, 0, axis_index_groups=groups, tiled=True)]
  transfers between devices with their start and end apart: 16 -> 16, of which waited for: 7 -> 5; matrix products, arithmetic and copies ran while one was open for 0% -> 0% of each run, Pallas kernels for 6% -> 6%
where the time goes in v5:
time: 96.4 us; the launch traced here: 95.6 us
  starting transfers between devices  78.5 us (81%)
  Pallas kernels  10.3 us (11%)
  waiting for transfers between devices  4.23 us (4%)
  local copies, waits for them, and re-layouts  1.67 us (2%)
    ppermute x8, starting transfers between devices, across(): lax.ppermute(x, 'dom', [(i, i ^ 1 << pair[i % 2]) for i in range(devices)])  29.2 us
    all_to_all x3, starting transfers between devices, exchange(): return lax.all_to_all(x, 'dom', 0, 0, axis_index_groups=groups, tiled=True)  28.2 us
    ppermute x5, starting transfers between devices, other_core(): return lax.ppermute(x, 'dom', [(i, i ^ 1) for i in range(devices)])  21.1 us
    pallas_call x15, Pallas kernels, call(): pl.pallas_call(lambda *refs: body(*refs[:reads], *refs[reads + waits:]),...  10.3 us
    ppermute x5, waiting for transfers between devices, other_core(): return lax.ppermute(x, 'dom', [(i, i ^ 1) for i in range(devices)])  2.8 us
  transfers between devices with their start and end apart: 16, of which 5 were waited for; matrix products, arithmetic and copies ran while one was open for 0% of the time, Pallas kernels for 6%

profile of v5, /device:TPU:1, one launch (start us, length us, event | category | flops | bytes accessed | tf_op | source)
XLA Modules:
  0.0 95.6 jit_solution(15078159770852071717)
XLA Ops:
  0.6 0.9 copy-done.1
  1.6 0.7 copy-done.6
  2.3 0.5 shard_map.94
  2.8 8.8 %collective-permute-start = (bf16[640,256]{1,0:T(8,128)(2,1)S(1)}, bf16[640,256]{1,0:T(8,128)(2,1)S(1)}, u32[]{:S(2)}, u32[]{:S(2)}) collective-permute-start(bf16[640,256]{1,0:T(8,128)(2,1)S(1)} %get-tuple-element.24), channel_id=1, source_target_pairs={{0,1},{1,0},{2,3},{3,2},{4,5},{5,4},{6,7},{7,6},{8,9},{9,8},{10,11... | collective-permute-start | bytes 983048 | tf_op jit(solution)/shard_map/ppermute | solution.py:268
  11.6 1.2 %collective-permute-done.refs_1_.refs_3_ = bf16[640,256]{1,0:T(8,128)(2,1)S(1)} collective-permute-done((bf16[640,256]{1,0:T(8,128)(2,1)S(1)}, bf16[640,256]{1,0:T(8,128)(2,1)S(1)}, u32[]{:S(2)}, u32[]{:S(2)}) %collective-permute-start) | collective-permute-done | bytes 327712 | tf_op jit(solution)/shard_map/ppermute | solution.py:268
  12.9 3.4 %collective-permute-start.1 = (bf16[256,256]{1,0:T(8,128)(2,1)S(1)}, bf16[256,256]{1,0:T(8,128)(2,1)S(1)}, u32[]{:S(2)}, u32[]{:S(2)}) collective-permute-start(bf16[256,256]{1,0:T(8,128)(2,1)S(1)} %get-tuple-element.26), channel_id=1, source_target_pairs={{0,256},{1,129},{2,258},{3,131},{4,260},{5,133},{6,262},{7,135},{8... | collective-permute-start | bytes 393224 | tf_op jit(solution)/shard_map/ppermute | solution.py:272
  16.3 4.9 %collective-permute-start.2 = (bf16[256,256]{1,0:T(8,128)(2,1)S(1)}, bf16[256,256]{1,0:T(8,128)(2,1)S(1)}, u32[]{:S(2)}, u32[]{:S(2)}) collective-permute-start(bf16[256,256]{1,0:T(8,128)(2,1)S(1)} %get-tuple-element.27), channel_id=1, source_target_pairs={{0,32},{1,65},{2,34},{3,67},{4,36},{5,69},{6,38},{7,71},{8,40},{9,... | collective-permute-start | bytes 393224 | tf_op jit(solution)/shard_map/ppermute | solution.py:272
  21.2 4.6 %collective-permute-start.3 = (bf16[256,256]{1,0:T(8,128)(2,1)S(1)}, bf16[256,256]{1,0:T(8,128)(2,1)S(1)}, u32[]{:S(2)}, u32[]{:S(2)}) collective-permute-start(bf16[256,256]{1,0:T(8,128)(2,1)S(1)} %get-tuple-element.28), channel_id=1, source_target_pairs={{0,8},{1,17},{2,10},{3,19},{4,12},{5,21},{6,14},{7,23},{8,0},{9,25... | collective-permute-start | bytes 393224 | tf_op jit(solution)/shard_map/ppermute | solution.py:272
  25.9 4.8 %collective-permute-start.4 = (bf16[256,256]{1,0:T(8,128)(2,1)S(1)}, bf16[256,256]{1,0:T(8,128)(2,1)S(1)}, u32[]{:S(2)}, u32[]{:S(2)}) collective-permute-start(bf16[256,256]{1,0:T(8,128)(2,1)S(1)} %get-tuple-element.25.refs_2_), channel_id=1, source_target_pairs={{0,2},{1,5},{2,0},{3,7},{4,6},{5,1},{6,4},{7,3},{8,10},{9,13},{10,... | collective-permute-start | bytes 393224 | tf_op jit(solution)/shard_map/ppermute | solution.py:272
  30.7 2.1 %shard_map.96.refs_0_.refs_4_ = bf16[1664,512]{1,0:T(8,128)(2,1)S(1)} custom-call(s32[10,512]{1,0:T(8,128)S(1)} %bitcast.6, s32[1,512]{1,0:T(1,128)S(1)} %bitcast.10, bf16[256,256]{1,0:T(8,128)(2,1)S(1)} %get-tuple-element.25.refs_2_), custom_call_target="tpu_custom_call" | custom-call | flops 2000000000 | bytes 2000000 | tf_op jit(solution)/shard_map/pallas_call | solution.py:25
  33.1 5.7 %collective-permute-start.5 = (bf16[512,256]{1,0:T(8,128)(2,1)S(1)}, bf16[512,256]{1,0:T(8,128)(2,1)S(1)}, u32[]{:S(2)}, u32[]{:S(2)}) collective-permute-start(bf16[512,256]{1,0:T(8,128)(2,1)S(1)} %shard_map.98), channel_id=1, source_target_pairs={{0,1},{1,0},{2,3},{3,2},{4,5},{5,4},{6,7},{7,6},{8,9},{9,8},{10,11... | collective-permute-start | bytes 786440 | tf_op jit(solution)/shard_map/ppermute | solution.py:268
  38.9 0.7 shard_map.97
  39.7 0.4 collective-permute-done.5.refs_3_
  40.0 2.0 %shard_map.99 = (bf16[512,256]{1,0:T(8,128)(2,1)}, bf16[512,256]{1,0:T(8,128)(2,1)}, bf16[512,256]{1,0:T(8,128)(2,1)S(1)}, bf16[512,256]{1,0:T(8,128)(2,1)S(1)}) custom-call(bf16[1664,512]{1,0:T(8,128)(2,1)S(1)} %shard_map.96.refs_0_.refs_4_, f32[512,256]{1,0:T(8,128)S(1)} %get-tuple-element.29.refs_1_, f32[512,256]{1,0:T(8,128)S(1)} %get-tuple-element.30.refs_2_, ...), custom_call_target="tpu_custom_call" | custom-call | flops 2000000000 | bytes 5000000 | tf_op jit(solution)/shard_map/pallas_call | solution.py:25
  42.0 9.0 %all-to-all-start = ((bf16[32,16,256]{2,1,0:T(8,128)(2,1)}), bf16[32,16,256]{2,1,0:T(8,128)(2,1)S(1)}, u32[]{:S(2)}, u32[]{:S(2)}) async-start(bf16[32,16,256]{2,1,0:T(8,128)(2,1)} %bitcast.3), calls=%async_computation | async-start | bytes 524288 | tf_op jit(solution)/shard_map/all_to_all | solution.py:238
  51.0 0.7 shard_map.100
  51.7 2.3 %collective-permute-start.6 = (bf16[384,256]{1,0:T(8,128)(2,1)S(1)}, bf16[384,256]{1,0:T(8,128)(2,1)S(1)}, u32[]{:S(2)}, u32[]{:S(2)}) collective-permute-start(bf16[384,256]{1,0:T(8,128)(2,1)S(1)} %get-tuple-element.35), channel_id=1, source_target_pairs={{0,1},{1,0},{2,3},{3,2},{4,5},{5,4},{6,7},{7,6},{8,9},{9,8},{10,11... | collective-permute-start | bytes 589832 | tf_op jit(solution)/shard_map/ppermute | solution.py:268
  54.0 2.1 %collective-permute-start.7 = (bf16[256,256]{1,0:T(8,128)(2,1)S(1)}, bf16[256,256]{1,0:T(8,128)(2,1)S(1)}, u32[]{:S(2)}, u32[]{:S(2)}) collective-permute-start(bf16[256,256]{1,0:T(8,128)(2,1)S(1)} %get-tuple-element.37), channel_id=1, source_target_pairs={{0,1},{1,0},{2,3},{3,2},{4,5},{5,4},{6,7},{7,6},{8,9},{9,8},{10,11... | collective-permute-start | bytes 393224 | tf_op jit(solution)/shard_map/ppermute | solution.py:268
  56.0 1.2 %collective-permute-done.7.refs_1_ = bf16[256,256]{1,0:T(8,128)(2,1)S(1)} collective-permute-done((bf16[256,256]{1,0:T(8,128)(2,1)S(1)}, bf16[256,256]{1,0:T(8,128)(2,1)S(1)}, u32[]{:S(2)}, u32[]{:S(2)}) %collective-permute-start.7) | collective-permute-done | bytes 131104 | tf_op jit(solution)/shard_map/ppermute | solution.py:268
  57.2 0.7 shard_map.104
  57.9 11.6 %all-to-all-start.1 = ((bf16[16,16,256]{2,1,0:T(8,128)(2,1)}), bf16[16,16,256]{2,1,0:T(8,128)(2,1)S(1)}, u32[]{:S(2)}, u32[]{:S(2)}) async-start(bf16[16,16,256]{2,1,0:T(8,128)(2,1)} %shard_map.104), calls=%async_computation.1 | async-start | bytes 262144 | tf_op jit(solution)/shard_map/all_to_all | solution.py:238
  69.6 2.2 %collective-permute-start.8 = (bf16[256,256]{1,0:T(8,128)(2,1)S(1)}, bf16[256,256]{1,0:T(8,128)(2,1)S(1)}, u32[]{:S(2)}, u32[]{:S(2)}) collective-permute-start(bf16[256,256]{1,0:T(8,128)(2,1)S(1)} %get-tuple-element.38), channel_id=1, source_target_pairs={{0,256},{1,129},{2,258},{3,131},{4,260},{5,133},{6,262},{7,135},{8... | collective-permute-start | bytes 393224 | tf_op jit(solution)/shard_map/ppermute | solution.py:272
  71.8 2.2 %collective-permute-start.9 = (bf16[256,256]{1,0:T(8,128)(2,1)S(1)}, bf16[256,256]{1,0:T(8,128)(2,1)S(1)}, u32[]{:S(2)}, u32[]{:S(2)}) collective-permute-start(bf16[256,256]{1,0:T(8,128)(2,1)S(1)} %get-tuple-element.39), channel_id=1, source_target_pairs={{0,32},{1,65},{2,34},{3,67},{4,36},{5,69},{6,38},{7,71},{8,40},{9,... | collective-permute-start | bytes 393224 | tf_op jit(solution)/shard_map/ppermute | solution.py:272
  74.0 2.4 %collective-permute-start.10 = (bf16[256,256]{1,0:T(8,128)(2,1)S(1)}, bf16[256,256]{1,0:T(8,128)(2,1)S(1)}, u32[]{:S(2)}, u32[]{:S(2)}) collective-permute-start(bf16[256,256]{1,0:T(8,128)(2,1)S(1)} %get-tuple-element.40), channel_id=1, source_target_pairs={{0,8},{1,17},{2,10},{3,19},{4,12},{5,21},{6,14},{7,23},{8,0},{9,25... | collective-permute-start | bytes 393224 | tf_op jit(solution)/shard_map/ppermute | solution.py:272
  76.4 4.7 %collective-permute-start.11 = (bf16[256,256]{1,0:T(8,128)(2,1)S(1)}, bf16[256,256]{1,0:T(8,128)(2,1)S(1)}, u32[]{:S(2)}, u32[]{:S(2)}) collective-permute-start(bf16[256,256]{1,0:T(8,128)(2,1)S(1)} %get-tuple-element.41), channel_id=1, source_target_pairs={{0,2},{1,5},{2,0},{3,7},{4,6},{5,1},{6,4},{7,3},{8,10},{9,13},{10,... | collective-permute-start | bytes 393224 | tf_op jit(solution)/shard_map/ppermute | solution.py:272
  81.0 0.7 shard_map.105.refs_4_
  81.8 7.6 %all-to-all-start.2 = ((bf16[32,16,256]{2,1,0:T(8,128)(2,1)}), bf16[32,16,256]{2,1,0:T(8,128)(2,1)S(1)}, u32[]{:S(2)}, u32[]{:S(2)}) async-start(bf16[32,16,256]{2,1,0:T(8,128)(2,1)} %shard_map.105.refs_4_), calls=%async_computation.2 | async-start | bytes 524288 | tf_op jit(solution)/shard_map/all_to_all | solution.py:238
  89.4 2.3 %collective-permute-start.12 = (bf16[512,256]{1,0:T(8,128)(2,1)S(1)}, bf16[512,256]{1,0:T(8,128)(2,1)S(1)}, u32[]{:S(2)}, u32[]{:S(2)}) collective-permute-start(bf16[512,256]{1,0:T(8,128)(2,1)S(1)} %shard_map.106), channel_id=1, source_target_pairs={{0,1},{1,0},{2,3},{3,2},{4,5},{5,4},{6,7},{7,6},{8,9},{9,8},{10,11... | collective-permute-start | bytes 786440 | tf_op jit(solution)/shard_map/ppermute | solution.py:268
  91.7 0.5 shard_map.103.refs_1_
  92.2 1.2 %all-to-all-done.2 = bf16[32,16,256]{2,1,0:T(8,128)(2,1)S(1)} async-done(((bf16[32,16,256]{2,1,0:T(8,128)(2,1)}), bf16[32,16,256]{2,1,0:T(8,128)(2,1)S(1)}, u32[]{:S(2)}, u32[]{:S(2)}) %all-to-all-start.2) | async-done | bytes 262176 | tf_op jit(solution)/shard_map/all_to_all | solution.py:238
  93.4 1.1 %shard_map.108 = f32[512,256]{1,0:T(8,128)} custom-call(bf16[512,256]{1,0:T(8,128)(2,1)S(1)} %bitcast.5), custom_call_target="tpu_custom_call" | custom-call | flops 100000000 | bytes 1000000 | tf_op jit(solution)/shard_map/pallas_call | solution.py:25
  94.5 1.1 %shard_map.107 = bf16[512,256]{1,0:T(8,128)(2,1)} custom-call(s32[9,1,128]{2,1,0:T(1,128)S(1)} %bitcast.9, f32[512,256]{1,0:T(8,128)S(1)} %shard_map.103.refs_1_, bf16[512,256]{1,0:T(8,128)(2,1)S(1)} %collective-permute-done.12.refs_2_), custom_call_target="tpu_custom_call" | custom-call | flops 1000000000 | bytes 1000000 | tf_op jit(solution)/shard_map/pallas_call | solution.py:25
  (33 shorter events, 0.4 us)
Async XLA Ops:
  0.6 1.0 copy-start.1
  1.6 0.7 copy-start.6
  2.3 28.4 %copy-start.5 = (s32[512,10]{0,1:T(8,128)S(1)}, s32[512,10]{0,1:T(8,128)}, u32[]{:S(2)}) copy-start(s32[512,10]{0,1:T(8,128)} %param.10) | copy-start | bytes 61444
  2.3 28.5 %copy-start.8 = (s32[512]{0:T(512)S(1)}, s32[512]{0:T(512)}, u32[]{:S(2)}) copy-start(s32[512]{0:T(512)} %param.11) | copy-start | bytes 6148
  2.8 10.0 %collective-permute-start = (bf16[640,256]{1,0:T(8,128)(2,1)S(1)}, bf16[640,256]{1,0:T(8,128)(2,1)S(1)}, u32[]{:S(2)}, u32[]{:S(2)}) collective-permute-start(bf16[640,256]{1,0:T(8,128)(2,1)S(1)} %get-tuple-element.24), channel_id=1, source_target_pairs={{0,1},{1,0},{2,3},{3,2},{4,5},{5,4},{6,7},{7,6},{8,9},{9,8},{10,11... | collective-permute-start | bytes 983048 | tf_op jit(solution)/shard_map/ppermute | solution.py:268
  12.9 20.0 %collective-permute-start.1 = (bf16[256,256]{1,0:T(8,128)(2,1)S(1)}, bf16[256,256]{1,0:T(8,128)(2,1)S(1)}, u32[]{:S(2)}, u32[]{:S(2)}) collective-permute-start(bf16[256,256]{1,0:T(8,128)(2,1)S(1)} %get-tuple-element.26), channel_id=1, source_target_pairs={{0,256},{1,129},{2,258},{3,131},{4,260},{5,133},{6,262},{7,135},{8... | collective-permute-start | bytes 393224 | tf_op jit(solution)/shard_map/ppermute | solution.py:272
  16.3 16.6 %collective-permute-start.2 = (bf16[256,256]{1,0:T(8,128)(2,1)S(1)}, bf16[256,256]{1,0:T(8,128)(2,1)S(1)}, u32[]{:S(2)}, u32[]{:S(2)}) collective-permute-start(bf16[256,256]{1,0:T(8,128)(2,1)S(1)} %get-tuple-element.27), channel_id=1, source_target_pairs={{0,32},{1,65},{2,34},{3,67},{4,36},{5,69},{6,38},{7,71},{8,40},{9,... | collective-permute-start | bytes 393224 | tf_op jit(solution)/shard_map/ppermute | solution.py:272
  21.2 11.7 %collective-permute-start.3 = (bf16[256,256]{1,0:T(8,128)(2,1)S(1)}, bf16[256,256]{1,0:T(8,128)(2,1)S(1)}, u32[]{:S(2)}, u32[]{:S(2)}) collective-permute-start(bf16[256,256]{1,0:T(8,128)(2,1)S(1)} %get-tuple-element.28), channel_id=1, source_target_pairs={{0,8},{1,17},{2,10},{3,19},{4,12},{5,21},{6,14},{7,23},{8,0},{9,25... | collective-permute-start | bytes 393224 | tf_op jit(solution)/shard_map/ppermute | solution.py:272
  25.9 7.2 %collective-permute-start.4 = (bf16[256,256]{1,0:T(8,128)(2,1)S(1)}, bf16[256,256]{1,0:T(8,128)(2,1)S(1)}, u32[]{:S(2)}, u32[]{:S(2)}) collective-permute-start(bf16[256,256]{1,0:T(8,128)(2,1)S(1)} %get-tuple-element.25.refs_2_), channel_id=1, source_target_pairs={{0,2},{1,5},{2,0},{3,7},{4,6},{5,1},{6,4},{7,3},{8,10},{9,13},{10,... | collective-permute-start | bytes 393224 | tf_op jit(solution)/shard_map/ppermute | solution.py:272
  32.8 6.0 %copy-start = (bf16[256,256]{1,0:T(8,128)(2,1)S(1)}, bf16[256,256]{1,0:T(8,128)(2,1)}, u32[]{:S(2)}) copy-start(bf16[256,256]{1,0:T(8,128)(2,1)} %refs_3_.1) | copy-start | bytes 393220
  32.9 6.0 %copy-start.2 = (bf16[512,256]{1,0:T(8,128)(2,1)S(1)}, bf16[512,256]{1,0:T(8,128)(2,1)}, u32[]{:S(2)}) copy-start(bf16[512,256]{1,0:T(8,128)(2,1)} %refs_4_.1) | copy-start | bytes 786436
  33.1 6.9 %copy-start.3 = (bf16[512,256]{1,0:T(8,128)(2,1)S(1)}, bf16[512,256]{1,0:T(8,128)(2,1)}, u32[]{:S(2)}) copy-start(bf16[512,256]{1,0:T(8,128)(2,1)} %refs_6_.1) | copy-start | bytes 786436
  33.1 6.9 %copy-start.4 = (bf16[256,256]{1,0:T(8,128)(2,1)S(1)}, bf16[256,256]{1,0:T(8,128)(2,1)}, u32[]{:S(2)}) copy-start(bf16[256,256]{1,0:T(8,128)(2,1)} %refs_7_.1) | copy-start | bytes 393220
  33.1 6.9 %collective-permute-start.5 = (bf16[512,256]{1,0:T(8,128)(2,1)S(1)}, bf16[512,256]{1,0:T(8,128)(2,1)S(1)}, u32[]{:S(2)}, u32[]{:S(2)}) collective-permute-start(bf16[512,256]{1,0:T(8,128)(2,1)S(1)} %shard_map.98), channel_id=1, source_target_pairs={{0,1},{1,0},{2,3},{3,2},{4,5},{5,4},{6,7},{7,6},{8,9},{9,8},{10,11... | collective-permute-start | bytes 786440 | tf_op jit(solution)/shard_map/ppermute | solution.py:268
  42.0 15.2 %all-to-all-start = ((bf16[32,16,256]{2,1,0:T(8,128)(2,1)}), bf16[32,16,256]{2,1,0:T(8,128)(2,1)S(1)}, u32[]{:S(2)}, u32[]{:S(2)}) async-start(bf16[32,16,256]{2,1,0:T(8,128)(2,1)} %bitcast.3), calls=%async_computation | async-start | bytes 524288 | tf_op jit(solution)/shard_map/all_to_all | solution.py:238
  51.7 5.5 %collective-permute-start.6 = (bf16[384,256]{1,0:T(8,128)(2,1)S(1)}, bf16[384,256]{1,0:T(8,128)(2,1)S(1)}, u32[]{:S(2)}, u32[]{:S(2)}) collective-permute-start(bf16[384,256]{1,0:T(8,128)(2,1)S(1)} %get-tuple-element.35), channel_id=1, source_target_pairs={{0,1},{1,0},{2,3},{3,2},{4,5},{5,4},{6,7},{7,6},{8,9},{9,8},{10,11... | collective-permute-start | bytes 589832 | tf_op jit(solution)/shard_map/ppermute | solution.py:268
  54.0 3.2 %collective-permute-start.7 = (bf16[256,256]{1,0:T(8,128)(2,1)S(1)}, bf16[256,256]{1,0:T(8,128)(2,1)S(1)}, u32[]{:S(2)}, u32[]{:S(2)}) collective-permute-start(bf16[256,256]{1,0:T(8,128)(2,1)S(1)} %get-tuple-element.37), channel_id=1, source_target_pairs={{0,1},{1,0},{2,3},{3,2},{4,5},{5,4},{6,7},{7,6},{8,9},{9,8},{10,11... | collective-permute-start | bytes 393224 | tf_op jit(solution)/shard_map/ppermute | solution.py:268
  57.9 33.8 %copy-start.7 = (s32[1,9,128]{2,0,1:T(1,128)S(1)}, s32[1,9,128]{2,0,1:T(1,128)}, u32[]{:S(2)}) copy-start(s32[1,9,128]{2,0,1:T(1,128)} %param.12) | copy-start | bytes 13828
  57.9 23.1 %all-to-all-start.1 = ((bf16[16,16,256]{2,1,0:T(8,128)(2,1)}), bf16[16,16,256]{2,1,0:T(8,128)(2,1)S(1)}, u32[]{:S(2)}, u32[]{:S(2)}) async-start(bf16[16,16,256]{2,1,0:T(8,128)(2,1)} %shard_map.104), calls=%async_computation.1 | async-start | bytes 262144 | tf_op jit(solution)/shard_map/all_to_all | solution.py:238
  69.6 19.8 %collective-permute-start.8 = (bf16[256,256]{1,0:T(8,128)(2,1)S(1)}, bf16[256,256]{1,0:T(8,128)(2,1)S(1)}, u32[]{:S(2)}, u32[]{:S(2)}) collective-permute-start(bf16[256,256]{1,0:T(8,128)(2,1)S(1)} %get-tuple-element.38), channel_id=1, source_target_pairs={{0,256},{1,129},{2,258},{3,131},{4,260},{5,133},{6,262},{7,135},{8... | collective-permute-start | bytes 393224 | tf_op jit(solution)/shard_map/ppermute | solution.py:272
  71.8 17.6 %collective-permute-start.9 = (bf16[256,256]{1,0:T(8,128)(2,1)S(1)}, bf16[256,256]{1,0:T(8,128)(2,1)S(1)}, u32[]{:S(2)}, u32[]{:S(2)}) collective-permute-start(bf16[256,256]{1,0:T(8,128)(2,1)S(1)} %get-tuple-element.39), channel_id=1, source_target_pairs={{0,32},{1,65},{2,34},{3,67},{4,36},{5,69},{6,38},{7,71},{8,40},{9,... | collective-permute-start | bytes 393224 | tf_op jit(solution)/shard_map/ppermute | solution.py:272
  74.0 15.4 %collective-permute-start.10 = (bf16[256,256]{1,0:T(8,128)(2,1)S(1)}, bf16[256,256]{1,0:T(8,128)(2,1)S(1)}, u32[]{:S(2)}, u32[]{:S(2)}) collective-permute-start(bf16[256,256]{1,0:T(8,128)(2,1)S(1)} %get-tuple-element.40), channel_id=1, source_target_pairs={{0,8},{1,17},{2,10},{3,19},{4,12},{5,21},{6,14},{7,23},{8,0},{9,25... | collective-permute-start | bytes 393224 | tf_op jit(solution)/shard_map/ppermute | solution.py:272
  76.4 13.0 %collective-permute-start.11 = (bf16[256,256]{1,0:T(8,128)(2,1)S(1)}, bf16[256,256]{1,0:T(8,128)(2,1)S(1)}, u32[]{:S(2)}, u32[]{:S(2)}) collective-permute-start(bf16[256,256]{1,0:T(8,128)(2,1)S(1)} %get-tuple-element.41), channel_id=1, source_target_pairs={{0,2},{1,5},{2,0},{3,7},{4,6},{5,1},{6,4},{7,3},{8,10},{9,13},{10,... | collective-permute-start | bytes 393224 | tf_op jit(solution)/shard_map/ppermute | solution.py:272
  81.8 11.6 %all-to-all-start.2 = ((bf16[32,16,256]{2,1,0:T(8,128)(2,1)}), bf16[32,16,256]{2,1,0:T(8,128)(2,1)S(1)}, u32[]{:S(2)}, u32[]{:S(2)}) async-start(bf16[32,16,256]{2,1,0:T(8,128)(2,1)} %shard_map.105.refs_4_), calls=%async_computation.2 | async-start | bytes 524288 | tf_op jit(solution)/shard_map/all_to_all | solution.py:238
  89.4 5.1 %collective-permute-start.12 = (bf16[512,256]{1,0:T(8,128)(2,1)S(1)}, bf16[512,256]{1,0:T(8,128)(2,1)S(1)}, u32[]{:S(2)}, u32[]{:S(2)}) collective-permute-start(bf16[512,256]{1,0:T(8,128)(2,1)S(1)} %shard_map.106), channel_id=1, source_target_pairs={{0,1},{1,0},{2,3},{3,2},{4,5},{5,4},{6,7},{7,6},{8,9},{9,8},{10,11... | collective-permute-start | bytes 786440 | tf_op jit(solution)/shard_map/ppermute | solution.py:268

commit v6 on v5

--- a/solution.py
+++ b/solution.py
@@ -9,7 +9,7 @@
 f32 = jnp.float32
 bf16 = jnp.bfloat16
 FAST_BITS = 5
-NEAR_FIRST = 20
+NEAR_FIRST = 21
 VMEM_LIMIT = 16 * 1024 * 1024
 TRANSPOSED_LHS = (((0,), (0,)), ((), ()))
 TRANSPOSED_RHS = (((1,), (1,)), ((), ()))

time: 96.4 us -> 95.4 us (0.990)
  starting transfers between devices: 78.5 us -> 77.5 us
    all_to_all x3, starting transfers between devices: 28.2 us -> 27.2 us  [exchange(): return lax.all_to_all(x, 'dom', 0, 0, axis_index_groups=groups, tiled=True)]
where the time goes in v6:
time: 95.4 us; the launch traced here: 94.6 us
  starting transfers between devices  77.5 us (81%)
  Pallas kernels  10.3 us (11%)
  waiting for transfers between devices  4.21 us (4%)
  local copies, waits for them, and re-layouts  1.67 us (2%)
  between operations  0.96 us (1%)
    ppermute x8, starting transfers between devices, across(): lax.ppermute(x, 'dom', [(i, i ^ 1 << pair[i % 2]) for i in range(devices)])  29.2 us
    all_to_all x3, starting transfers between devices, exchange(): return lax.all_to_all(x, 'dom', 0, 0, axis_index_groups=groups, tiled=True)  27.2 us
    ppermute x5, starting transfers between devices, other_core(): return lax.ppermute(x, 'dom', [(i, i ^ 1) for i in range(devices)])  21.1 us
    pallas_call x15, Pallas kernels, call(): pl.pallas_call(lambda *refs: body(*refs[:reads], *refs[reads + waits:]),...  10.3 us
    ppermute x5, waiting for transfers between devices, other_core(): return lax.ppermute(x, 'dom', [(i, i ^ 1) for i in range(devices)])  2.8 us
  transfers between devices with their start and end apart: 16, of which 5 were waited for; matrix products, arithmetic and copies ran while one was open for 0% of the time, Pallas kernels for 6%

profile of v6, /device:TPU:1, one launch (start us, length us, event | category | flops | bytes accessed | tf_op | source)
XLA Modules:
  0.0 94.6 jit_solution(9429236721293491864)
XLA Ops:
  0.6 0.9 copy-done.1
  1.6 0.7 copy-done.6
  2.3 0.5 shard_map.94
  2.8 8.8 %collective-permute-start = (bf16[640,256]{1,0:T(8,128)(2,1)S(1)}, bf16[640,256]{1,0:T(8,128)(2,1)S(1)}, u32[]{:S(2)}, u32[]{:S(2)}) collective-permute-start(bf16[640,256]{1,0:T(8,128)(2,1)S(1)} %get-tuple-element.24), channel_id=1, source_target_pairs={{0,1},{1,0},{2,3},{3,2},{4,5},{5,4},{6,7},{7,6},{8,9},{9,8},{10,11... | collective-permute-start | bytes 983048 | tf_op jit(solution)/shard_map/ppermute | solution.py:268
  11.6 1.2 %collective-permute-done.refs_1_.refs_3_ = bf16[640,256]{1,0:T(8,128)(2,1)S(1)} collective-permute-done((bf16[640,256]{1,0:T(8,128)(2,1)S(1)}, bf16[640,256]{1,0:T(8,128)(2,1)S(1)}, u32[]{:S(2)}, u32[]{:S(2)}) %collective-permute-start) | collective-permute-done | bytes 327712 | tf_op jit(solution)/shard_map/ppermute | solution.py:268
  12.9 3.4 %collective-permute-start.1 = (bf16[256,256]{1,0:T(8,128)(2,1)S(1)}, bf16[256,256]{1,0:T(8,128)(2,1)S(1)}, u32[]{:S(2)}, u32[]{:S(2)}) collective-permute-start(bf16[256,256]{1,0:T(8,128)(2,1)S(1)} %get-tuple-element.26), channel_id=1, source_target_pairs={{0,256},{1,129},{2,258},{3,131},{4,260},{5,133},{6,262},{7,135},{8... | collective-permute-start | bytes 393224 | tf_op jit(solution)/shard_map/ppermute | solution.py:272
  16.3 4.9 %collective-permute-start.2 = (bf16[256,256]{1,0:T(8,128)(2,1)S(1)}, bf16[256,256]{1,0:T(8,128)(2,1)S(1)}, u32[]{:S(2)}, u32[]{:S(2)}) collective-permute-start(bf16[256,256]{1,0:T(8,128)(2,1)S(1)} %get-tuple-element.27), channel_id=1, source_target_pairs={{0,32},{1,65},{2,34},{3,67},{4,36},{5,69},{6,38},{7,71},{8,40},{9,... | collective-permute-start | bytes 393224 | tf_op jit(solution)/shard_map/ppermute | solution.py:272
  21.2 4.6 %collective-permute-start.3 = (bf16[256,256]{1,0:T(8,128)(2,1)S(1)}, bf16[256,256]{1,0:T(8,128)(2,1)S(1)}, u32[]{:S(2)}, u32[]{:S(2)}) collective-permute-start(bf16[256,256]{1,0:T(8,128)(2,1)S(1)} %get-tuple-element.28), channel_id=1, source_target_pairs={{0,8},{1,17},{2,10},{3,19},{4,12},{5,21},{6,14},{7,23},{8,0},{9,25... | collective-permute-start | bytes 393224 | tf_op jit(solution)/shard_map/ppermute | solution.py:272
  25.9 4.8 %collective-permute-start.4 = (bf16[256,256]{1,0:T(8,128)(2,1)S(1)}, bf16[256,256]{1,0:T(8,128)(2,1)S(1)}, u32[]{:S(2)}, u32[]{:S(2)}) collective-permute-start(bf16[256,256]{1,0:T(8,128)(2,1)S(1)} %get-tuple-element.25.refs_2_), channel_id=1, source_target_pairs={{0,2},{1,5},{2,0},{3,7},{4,6},{5,1},{6,4},{7,3},{8,10},{9,13},{10,... | collective-permute-start | bytes 393224 | tf_op jit(solution)/shard_map/ppermute | solution.py:272
  30.7 2.1 %shard_map.96.refs_0_.refs_4_ = bf16[1664,512]{1,0:T(8,128)(2,1)S(1)} custom-call(s32[10,512]{1,0:T(8,128)S(1)} %bitcast.6, s32[1,512]{1,0:T(1,128)S(1)} %bitcast.10, bf16[256,256]{1,0:T(8,128)(2,1)S(1)} %get-tuple-element.25.refs_2_), custom_call_target="tpu_custom_call" | custom-call | flops 2000000000 | bytes 2000000 | tf_op jit(solution)/shard_map/pallas_call | solution.py:25
  33.1 5.7 %collective-permute-start.5 = (bf16[512,256]{1,0:T(8,128)(2,1)S(1)}, bf16[512,256]{1,0:T(8,128)(2,1)S(1)}, u32[]{:S(2)}, u32[]{:S(2)}) collective-permute-start(bf16[512,256]{1,0:T(8,128)(2,1)S(1)} %shard_map.98), channel_id=1, source_target_pairs={{0,1},{1,0},{2,3},{3,2},{4,5},{5,4},{6,7},{7,6},{8,9},{9,8},{10,11... | collective-permute-start | bytes 786440 | tf_op jit(solution)/shard_map/ppermute | solution.py:268
  38.9 0.7 shard_map.97
  39.7 0.4 collective-permute-done.5.refs_3_
  40.0 2.0 %shard_map.99 = (bf16[512,256]{1,0:T(8,128)(2,1)}, bf16[512,256]{1,0:T(8,128)(2,1)}, bf16[512,256]{1,0:T(8,128)(2,1)S(1)}, bf16[512,256]{1,0:T(8,128)(2,1)S(1)}) custom-call(bf16[1664,512]{1,0:T(8,128)(2,1)S(1)} %shard_map.96.refs_0_.refs_4_, f32[512,256]{1,0:T(8,128)S(1)} %get-tuple-element.29.refs_1_, f32[512,256]{1,0:T(8,128)S(1)} %get-tuple-element.30.refs_2_, ...), custom_call_target="tpu_custom_call" | custom-call | flops 2000000000 | bytes 5000000 | tf_op jit(solution)/shard_map/pallas_call | solution.py:25
  42.0 8.7 %all-to-all-start = ((bf16[32,16,256]{2,1,0:T(8,128)(2,1)}), bf16[32,16,256]{2,1,0:T(8,128)(2,1)S(1)}, u32[]{:S(2)}, u32[]{:S(2)}) async-start(bf16[32,16,256]{2,1,0:T(8,128)(2,1)} %bitcast.3), calls=%async_computation | async-start | bytes 524288 | tf_op jit(solution)/shard_map/all_to_all | solution.py:238
  50.7 0.7 shard_map.100
  51.4 2.3 %collective-permute-start.6 = (bf16[384,256]{1,0:T(8,128)(2,1)S(1)}, bf16[384,256]{1,0:T(8,128)(2,1)S(1)}, u32[]{:S(2)}, u32[]{:S(2)}) collective-permute-start(bf16[384,256]{1,0:T(8,128)(2,1)S(1)} %get-tuple-element.35), channel_id=1, source_target_pairs={{0,1},{1,0},{2,3},{3,2},{4,5},{5,4},{6,7},{7,6},{8,9},{9,8},{10,11... | collective-permute-start | bytes 589832 | tf_op jit(solution)/shard_map/ppermute | solution.py:268
  53.7 2.1 %collective-permute-start.7 = (bf16[256,256]{1,0:T(8,128)(2,1)S(1)}, bf16[256,256]{1,0:T(8,128)(2,1)S(1)}, u32[]{:S(2)}, u32[]{:S(2)}) collective-permute-start(bf16[256,256]{1,0:T(8,128)(2,1)S(1)} %get-tuple-element.37), channel_id=1, source_target_pairs={{0,1},{1,0},{2,3},{3,2},{4,5},{5,4},{6,7},{7,6},{8,9},{9,8},{10,11... | collective-permute-start | bytes 393224 | tf_op jit(solution)/shard_map/ppermute | solution.py:268
  55.8 1.2 %collective-permute-done.7.refs_1_ = bf16[256,256]{1,0:T(8,128)(2,1)S(1)} collective-permute-done((bf16[256,256]{1,0:T(8,128)(2,1)S(1)}, bf16[256,256]{1,0:T(8,128)(2,1)S(1)}, u32[]{:S(2)}, u32[]{:S(2)}) %collective-permute-start.7) | collective-permute-done | bytes 131104 | tf_op jit(solution)/shard_map/ppermute | solution.py:268
  57.0 0.7 shard_map.104
  57.7 11.6 %all-to-all-start.1 = ((bf16[16,16,256]{2,1,0:T(8,128)(2,1)}), bf16[16,16,256]{2,1,0:T(8,128)(2,1)S(1)}, u32[]{:S(2)}, u32[]{:S(2)}) async-start(bf16[16,16,256]{2,1,0:T(8,128)(2,1)} %shard_map.104), calls=%async_computation.1 | async-start | bytes 262144 | tf_op jit(solution)/shard_map/all_to_all | solution.py:238
  69.3 2.2 %collective-permute-start.8 = (bf16[256,256]{1,0:T(8,128)(2,1)S(1)}, bf16[256,256]{1,0:T(8,128)(2,1)S(1)}, u32[]{:S(2)}, u32[]{:S(2)}) collective-permute-start(bf16[256,256]{1,0:T(8,128)(2,1)S(1)} %get-tuple-element.38), channel_id=1, source_target_pairs={{0,256},{1,129},{2,258},{3,131},{4,260},{5,133},{6,262},{7,135},{8... | collective-permute-start | bytes 393224 | tf_op jit(solution)/shard_map/ppermute | solution.py:272
  71.5 2.2 %collective-permute-start.9 = (bf16[256,256]{1,0:T(8,128)(2,1)S(1)}, bf16[256,256]{1,0:T(8,128)(2,1)S(1)}, u32[]{:S(2)}, u32[]{:S(2)}) collective-permute-start(bf16[256,256]{1,0:T(8,128)(2,1)S(1)} %get-tuple-element.39), channel_id=1, source_target_pairs={{0,32},{1,65},{2,34},{3,67},{4,36},{5,69},{6,38},{7,71},{8,40},{9,... | collective-permute-start | bytes 393224 | tf_op jit(solution)/shard_map/ppermute | solution.py:272
  73.7 2.4 %collective-permute-start.10 = (bf16[256,256]{1,0:T(8,128)(2,1)S(1)}, bf16[256,256]{1,0:T(8,128)(2,1)S(1)}, u32[]{:S(2)}, u32[]{:S(2)}) collective-permute-start(bf16[256,256]{1,0:T(8,128)(2,1)S(1)} %get-tuple-element.40), channel_id=1, source_target_pairs={{0,8},{1,17},{2,10},{3,19},{4,12},{5,21},{6,14},{7,23},{8,0},{9,25... | collective-permute-start | bytes 393224 | tf_op jit(solution)/shard_map/ppermute | solution.py:272
  76.1 4.7 %collective-permute-start.11 = (bf16[256,256]{1,0:T(8,128)(2,1)S(1)}, bf16[256,256]{1,0:T(8,128)(2,1)S(1)}, u32[]{:S(2)}, u32[]{:S(2)}) collective-permute-start(bf16[256,256]{1,0:T(8,128)(2,1)S(1)} %get-tuple-element.41), channel_id=1, source_target_pairs={{0,2},{1,5},{2,0},{3,7},{4,6},{5,1},{6,4},{7,3},{8,10},{9,13},{10,... | collective-permute-start | bytes 393224 | tf_op jit(solution)/shard_map/ppermute | solution.py:272
  80.8 0.7 shard_map.105.refs_4_
  81.5 6.8 %all-to-all-start.2 = ((bf16[32,16,256]{2,1,0:T(8,128)(2,1)}), bf16[32,16,256]{2,1,0:T(8,128)(2,1)S(1)}, u32[]{:S(2)}, u32[]{:S(2)}) async-start(bf16[32,16,256]{2,1,0:T(8,128)(2,1)} %shard_map.105.refs_4_), calls=%async_computation.2 | async-start | bytes 524288 | tf_op jit(solution)/shard_map/all_to_all | solution.py:238
  88.4 2.3 %collective-permute-start.12 = (bf16[512,256]{1,0:T(8,128)(2,1)S(1)}, bf16[512,256]{1,0:T(8,128)(2,1)S(1)}, u32[]{:S(2)}, u32[]{:S(2)}) collective-permute-start(bf16[512,256]{1,0:T(8,128)(2,1)S(1)} %shard_map.106), channel_id=1, source_target_pairs={{0,1},{1,0},{2,3},{3,2},{4,5},{5,4},{6,7},{7,6},{8,9},{9,8},{10,11... | collective-permute-start | bytes 786440 | tf_op jit(solution)/shard_map/ppermute | solution.py:268
  90.7 0.5 shard_map.103.refs_1_
  91.2 1.2 %all-to-all-done.2 = bf16[32,16,256]{2,1,0:T(8,128)(2,1)S(1)} async-done(((bf16[32,16,256]{2,1,0:T(8,128)(2,1)}), bf16[32,16,256]{2,1,0:T(8,128)(2,1)S(1)}, u32[]{:S(2)}, u32[]{:S(2)}) %all-to-all-start.2) | async-done | bytes 262176 | tf_op jit(solution)/shard_map/all_to_all | solution.py:238
  92.4 1.1 %shard_map.108 = f32[512,256]{1,0:T(8,128)} custom-call(bf16[512,256]{1,0:T(8,128)(2,1)S(1)} %bitcast.5), custom_call_target="tpu_custom_call" | custom-call | flops 100000000 | bytes 1000000 | tf_op jit(solution)/shard_map/pallas_call | solution.py:25
  93.5 1.1 %shard_map.107 = bf16[512,256]{1,0:T(8,128)(2,1)} custom-call(s32[9,1,128]{2,1,0:T(1,128)S(1)} %bitcast.9, f32[512,256]{1,0:T(8,128)S(1)} %shard_map.103.refs_1_, bf16[512,256]{1,0:T(8,128)(2,1)S(1)} %collective-permute-done.12.refs_2_), custom_call_target="tpu_custom_call" | custom-call | flops 1000000000 | bytes 1000000 | tf_op jit(solution)/shard_map/pallas_call | solution.py:25
  (33 shorter events, 0.4 us)
Async XLA Ops:
  0.6 1.0 %copy-start.1 = (bf16[512,256]{1,0:T(8,128)(2,1)S(1)}, bf16[512,256]{1,0:T(8,128)(2,1)}, u32[]{:S(2)}) copy-start(bf16[512,256]{1,0:T(8,128)(2,1)} %refs_4_.1) | copy-start | bytes 786436
  1.6 0.7 copy-start.6
  2.3 28.4 %copy-start.5 = (s32[512,10]{0,1:T(8,128)S(1)}, s32[512,10]{0,1:T(8,128)}, u32[]{:S(2)}) copy-start(s32[512,10]{0,1:T(8,128)} %param.10) | copy-start | bytes 61444
  2.3 28.5 %copy-start.8 = (s32[512]{0:T(512)S(1)}, s32[512]{0:T(512)}, u32[]{:S(2)}) copy-start(s32[512]{0:T(512)} %param.11) | copy-start | bytes 6148
  2.8 10.0 %collective-permute-start = (bf16[640,256]{1,0:T(8,128)(2,1)S(1)}, bf16[640,256]{1,0:T(8,128)(2,1)S(1)}, u32[]{:S(2)}, u32[]{:S(2)}) collective-permute-start(bf16[640,256]{1,0:T(8,128)(2,1)S(1)} %get-tuple-element.24), channel_id=1, source_target_pairs={{0,1},{1,0},{2,3},{3,2},{4,5},{5,4},{6,7},{7,6},{8,9},{9,8},{10,11... | collective-permute-start | bytes 983048 | tf_op jit(solution)/shard_map/ppermute | solution.py:268
  12.9 20.0 %collective-permute-start.1 = (bf16[256,256]{1,0:T(8,128)(2,1)S(1)}, bf16[256,256]{1,0:T(8,128)(2,1)S(1)}, u32[]{:S(2)}, u32[]{:S(2)}) collective-permute-start(bf16[256,256]{1,0:T(8,128)(2,1)S(1)} %get-tuple-element.26), channel_id=1, source_target_pairs={{0,256},{1,129},{2,258},{3,131},{4,260},{5,133},{6,262},{7,135},{8... | collective-permute-start | bytes 393224 | tf_op jit(solution)/shard_map/ppermute | solution.py:272
  16.3 16.6 %collective-permute-start.2 = (bf16[256,256]{1,0:T(8,128)(2,1)S(1)}, bf16[256,256]{1,0:T(8,128)(2,1)S(1)}, u32[]{:S(2)}, u32[]{:S(2)}) collective-permute-start(bf16[256,256]{1,0:T(8,128)(2,1)S(1)} %get-tuple-element.27), channel_id=1, source_target_pairs={{0,32},{1,65},{2,34},{3,67},{4,36},{5,69},{6,38},{7,71},{8,40},{9,... | collective-permute-start | bytes 393224 | tf_op jit(solution)/shard_map/ppermute | solution.py:272
  21.2 11.7 %collective-permute-start.3 = (bf16[256,256]{1,0:T(8,128)(2,1)S(1)}, bf16[256,256]{1,0:T(8,128)(2,1)S(1)}, u32[]{:S(2)}, u32[]{:S(2)}) collective-permute-start(bf16[256,256]{1,0:T(8,128)(2,1)S(1)} %get-tuple-element.28), channel_id=1, source_target_pairs={{0,8},{1,17},{2,10},{3,19},{4,12},{5,21},{6,14},{7,23},{8,0},{9,25... | collective-permute-start | bytes 393224 | tf_op jit(solution)/shard_map/ppermute | solution.py:272
  25.9 7.2 %collective-permute-start.4 = (bf16[256,256]{1,0:T(8,128)(2,1)S(1)}, bf16[256,256]{1,0:T(8,128)(2,1)S(1)}, u32[]{:S(2)}, u32[]{:S(2)}) collective-permute-start(bf16[256,256]{1,0:T(8,128)(2,1)S(1)} %get-tuple-element.25.refs_2_), channel_id=1, source_target_pairs={{0,2},{1,5},{2,0},{3,7},{4,6},{5,1},{6,4},{7,3},{8,10},{9,13},{10,... | collective-permute-start | bytes 393224 | tf_op jit(solution)/shard_map/ppermute | solution.py:272
  32.8 6.0 %copy-start = (bf16[256,256]{1,0:T(8,128)(2,1)S(1)}, bf16[256,256]{1,0:T(8,128)(2,1)}, u32[]{:S(2)}) copy-start(bf16[256,256]{1,0:T(8,128)(2,1)} %refs_3_.1) | copy-start | bytes 393220
  32.9 6.0 %copy-start.2 = (bf16[512,256]{1,0:T(8,128)(2,1)S(1)}, bf16[512,256]{1,0:T(8,128)(2,1)}, u32[]{:S(2)}) copy-start(bf16[512,256]{1,0:T(8,128)(2,1)} %refs_4_.1) | copy-start | bytes 786436
  33.1 6.9 %copy-start.3 = (bf16[512,256]{1,0:T(8,128)(2,1)S(1)}, bf16[512,256]{1,0:T(8,128)(2,1)}, u32[]{:S(2)}) copy-start(bf16[512,256]{1,0:T(8,128)(2,1)} %refs_6_.1) | copy-start | bytes 786436
  33.1 6.9 %copy-start.4 = (bf16[256,256]{1,0:T(8,128)(2,1)S(1)}, bf16[256,256]{1,0:T(8,128)(2,1)}, u32[]{:S(2)}) copy-start(bf16[256,256]{1,0:T(8,128)(2,1)} %refs_7_.1) | copy-start | bytes 393220
  33.1 6.9 %collective-permute-start.5 = (bf16[512,256]{1,0:T(8,128)(2,1)S(1)}, bf16[512,256]{1,0:T(8,128)(2,1)S(1)}, u32[]{:S(2)}, u32[]{:S(2)}) collective-permute-start(bf16[512,256]{1,0:T(8,128)(2,1)S(1)} %shard_map.98), channel_id=1, source_target_pairs={{0,1},{1,0},{2,3},{3,2},{4,5},{5,4},{6,7},{7,6},{8,9},{9,8},{10,11... | collective-permute-start | bytes 786440 | tf_op jit(solution)/shard_map/ppermute | solution.py:268
  42.0 14.9 %all-to-all-start = ((bf16[32,16,256]{2,1,0:T(8,128)(2,1)}), bf16[32,16,256]{2,1,0:T(8,128)(2,1)S(1)}, u32[]{:S(2)}, u32[]{:S(2)}) async-start(bf16[32,16,256]{2,1,0:T(8,128)(2,1)} %bitcast.3), calls=%async_computation | async-start | bytes 524288 | tf_op jit(solution)/shard_map/all_to_all | solution.py:238
  51.4 5.5 %collective-permute-start.6 = (bf16[384,256]{1,0:T(8,128)(2,1)S(1)}, bf16[384,256]{1,0:T(8,128)(2,1)S(1)}, u32[]{:S(2)}, u32[]{:S(2)}) collective-permute-start(bf16[384,256]{1,0:T(8,128)(2,1)S(1)} %get-tuple-element.35), channel_id=1, source_target_pairs={{0,1},{1,0},{2,3},{3,2},{4,5},{5,4},{6,7},{7,6},{8,9},{9,8},{10,11... | collective-permute-start | bytes 589832 | tf_op jit(solution)/shard_map/ppermute | solution.py:268
  53.7 3.2 %collective-permute-start.7 = (bf16[256,256]{1,0:T(8,128)(2,1)S(1)}, bf16[256,256]{1,0:T(8,128)(2,1)S(1)}, u32[]{:S(2)}, u32[]{:S(2)}) collective-permute-start(bf16[256,256]{1,0:T(8,128)(2,1)S(1)} %get-tuple-element.37), channel_id=1, source_target_pairs={{0,1},{1,0},{2,3},{3,2},{4,5},{5,4},{6,7},{7,6},{8,9},{9,8},{10,11... | collective-permute-start | bytes 393224 | tf_op jit(solution)/shard_map/ppermute | solution.py:268
  57.7 33.0 %copy-start.7 = (s32[1,9,128]{2,0,1:T(1,128)S(1)}, s32[1,9,128]{2,0,1:T(1,128)}, u32[]{:S(2)}) copy-start(s32[1,9,128]{2,0,1:T(1,128)} %param.12) | copy-start | bytes 13828
  57.7 23.1 %all-to-all-start.1 = ((bf16[16,16,256]{2,1,0:T(8,128)(2,1)}), bf16[16,16,256]{2,1,0:T(8,128)(2,1)S(1)}, u32[]{:S(2)}, u32[]{:S(2)}) async-start(bf16[16,16,256]{2,1,0:T(8,128)(2,1)} %shard_map.104), calls=%async_computation.1 | async-start | bytes 262144 | tf_op jit(solution)/shard_map/all_to_all | solution.py:238
  69.3 19.1 %collective-permute-start.8 = (bf16[256,256]{1,0:T(8,128)(2,1)S(1)}, bf16[256,256]{1,0:T(8,128)(2,1)S(1)}, u32[]{:S(2)}, u32[]{:S(2)}) collective-permute-start(bf16[256,256]{1,0:T(8,128)(2,1)S(1)} %get-tuple-element.38), channel_id=1, source_target_pairs={{0,256},{1,129},{2,258},{3,131},{4,260},{5,133},{6,262},{7,135},{8... | collective-permute-start | bytes 393224 | tf_op jit(solution)/shard_map/ppermute | solution.py:272
  71.5 16.9 %collective-permute-start.9 = (bf16[256,256]{1,0:T(8,128)(2,1)S(1)}, bf16[256,256]{1,0:T(8,128)(2,1)S(1)}, u32[]{:S(2)}, u32[]{:S(2)}) collective-permute-start(bf16[256,256]{1,0:T(8,128)(2,1)S(1)} %get-tuple-element.39), channel_id=1, source_target_pairs={{0,32},{1,65},{2,34},{3,67},{4,36},{5,69},{6,38},{7,71},{8,40},{9,... | collective-permute-start | bytes 393224 | tf_op jit(solution)/shard_map/ppermute | solution.py:272
  73.7 14.7 %collective-permute-start.10 = (bf16[256,256]{1,0:T(8,128)(2,1)S(1)}, bf16[256,256]{1,0:T(8,128)(2,1)S(1)}, u32[]{:S(2)}, u32[]{:S(2)}) collective-permute-start(bf16[256,256]{1,0:T(8,128)(2,1)S(1)} %get-tuple-element.40), channel_id=1, source_target_pairs={{0,8},{1,17},{2,10},{3,19},{4,12},{5,21},{6,14},{7,23},{8,0},{9,25... | collective-permute-start | bytes 393224 | tf_op jit(solution)/shard_map/ppermute | solution.py:272
  76.1 12.3 %collective-permute-start.11 = (bf16[256,256]{1,0:T(8,128)(2,1)S(1)}, bf16[256,256]{1,0:T(8,128)(2,1)S(1)}, u32[]{:S(2)}, u32[]{:S(2)}) collective-permute-start(bf16[256,256]{1,0:T(8,128)(2,1)S(1)} %get-tuple-element.41), channel_id=1, source_target_pairs={{0,2},{1,5},{2,0},{3,7},{4,6},{5,1},{6,4},{7,3},{8,10},{9,13},{10,... | collective-permute-start | bytes 393224 | tf_op jit(solution)/shard_map/ppermute | solution.py:272
  81.5 10.9 %all-to-all-start.2 = ((bf16[32,16,256]{2,1,0:T(8,128)(2,1)}), bf16[32,16,256]{2,1,0:T(8,128)(2,1)S(1)}, u32[]{:S(2)}, u32[]{:S(2)}) async-start(bf16[32,16,256]{2,1,0:T(8,128)(2,1)} %shard_map.105.refs_4_), calls=%async_computation.2 | async-start | bytes 524288 | tf_op jit(solution)/shard_map/all_to_all | solution.py:238
  88.4 5.1 %collective-permute-start.12 = (bf16[512,256]{1,0:T(8,128)(2,1)S(1)}, bf16[512,256]{1,0:T(8,128)(2,1)S(1)}, u32[]{:S(2)}, u32[]{:S(2)}) collective-permute-start(bf16[512,256]{1,0:T(8,128)(2,1)S(1)} %shard_map.106), channel_id=1, source_target_pairs={{0,1},{1,0},{2,3},{3,2},{4,5},{5,4},{6,7},{7,6},{8,9},{9,8},{10,11... | collective-permute-start | bytes 786440 | tf_op jit(solution)/shard_map/ppermute | solution.py:268

commit v7 on v6

--- a/solution.py
+++ b/solution.py
@@ -242,7 +242,7 @@
     pairs = []
     for top in range(levels - 1, 1, -2):
         pairs.append((top, top - 1) if not pairs else (top - 1, top))
-    return pairs
+    return pairs[: len(pairs) // 2] + pairs[len(pairs) // 2 :][::-1]
 
 
 def per_device(features, w_self, w_neigh, neighbors, degree, boundary, upstream):

time: 95.4 us -> 95.5 us (level)
  no operation moved by 1% of the time
where the time goes in v7:
time: 95.5 us; the launch traced here: 94.7 us
  starting transfers between devices  77.4 us (81%)
  Pallas kernels  10.3 us (11%)
  waiting for transfers between devices  4.39 us (5%)
  local copies, waits for them, and re-layouts  1.67 us (2%)
  between operations  0.96 us (1%)
    ppermute x8, starting transfers between devices, across(): lax.ppermute(x, 'dom', [(i, i ^ 1 << pair[i % 2]) for i in range(devices)])  29.2 us
    all_to_all x3, starting transfers between devices, exchange(): return lax.all_to_all(x, 'dom', 0, 0, axis_index_groups=groups, tiled=True)  27.1 us
    ppermute x5, starting transfers between devices, other_core(): return lax.ppermute(x, 'dom', [(i, i ^ 1) for i in range(devices)])  21 us
    pallas_call x15, Pallas kernels, call(): pl.pallas_call(lambda *refs: body(*refs[:reads], *refs[reads + waits:]),...  10.3 us
    ppermute x5, waiting for transfers between devices, other_core(): return lax.ppermute(x, 'dom', [(i, i ^ 1) for i in range(devices)])  2.8 us
  transfers between devices with their start and end apart: 16, of which 5 were waited for; matrix products, arithmetic and copies ran while one was open for 0% of the time, Pallas kernels for 6%

profile of v7, /device:TPU:1, one launch (start us, length us, event | category | flops | bytes accessed | tf_op | source)
XLA Modules:
  0.0 94.7 jit_solution(12804564927358779198)
XLA Ops:
  0.6 0.9 copy-done.1
  1.6 0.7 copy-done.6
  2.3 0.5 shard_map.94
  2.8 8.8 %collective-permute-start = (bf16[640,256]{1,0:T(8,128)(2,1)S(1)}, bf16[640,256]{1,0:T(8,128)(2,1)S(1)}, u32[]{:S(2)}, u32[]{:S(2)}) collective-permute-start(bf16[640,256]{1,0:T(8,128)(2,1)S(1)} %get-tuple-element.24), channel_id=1, source_target_pairs={{0,1},{1,0},{2,3},{3,2},{4,5},{5,4},{6,7},{7,6},{8,9},{9,8},{10,11... | collective-permute-start | bytes 983048 | tf_op jit(solution)/shard_map/ppermute | solution.py:268
  11.6 1.2 %collective-permute-done.refs_1_.refs_3_ = bf16[640,256]{1,0:T(8,128)(2,1)S(1)} collective-permute-done((bf16[640,256]{1,0:T(8,128)(2,1)S(1)}, bf16[640,256]{1,0:T(8,128)(2,1)S(1)}, u32[]{:S(2)}, u32[]{:S(2)}) %collective-permute-start) | collective-permute-done | bytes 327712 | tf_op jit(solution)/shard_map/ppermute | solution.py:268
  12.9 3.4 %collective-permute-start.1 = (bf16[256,256]{1,0:T(8,128)(2,1)S(1)}, bf16[256,256]{1,0:T(8,128)(2,1)S(1)}, u32[]{:S(2)}, u32[]{:S(2)}) collective-permute-start(bf16[256,256]{1,0:T(8,128)(2,1)S(1)} %get-tuple-element.26), channel_id=1, source_target_pairs={{0,256},{1,129},{2,258},{3,131},{4,260},{5,133},{6,262},{7,135},{8... | collective-permute-start | bytes 393224 | tf_op jit(solution)/shard_map/ppermute | solution.py:272
  16.3 4.9 %collective-permute-start.2 = (bf16[256,256]{1,0:T(8,128)(2,1)S(1)}, bf16[256,256]{1,0:T(8,128)(2,1)S(1)}, u32[]{:S(2)}, u32[]{:S(2)}) collective-permute-start(bf16[256,256]{1,0:T(8,128)(2,1)S(1)} %get-tuple-element.27), channel_id=1, source_target_pairs={{0,32},{1,65},{2,34},{3,67},{4,36},{5,69},{6,38},{7,71},{8,40},{9,... | collective-permute-start | bytes 393224 | tf_op jit(solution)/shard_map/ppermute | solution.py:272
  21.2 4.8 %collective-permute-start.3 = (bf16[256,256]{1,0:T(8,128)(2,1)S(1)}, bf16[256,256]{1,0:T(8,128)(2,1)S(1)}, u32[]{:S(2)}, u32[]{:S(2)}) collective-permute-start(bf16[256,256]{1,0:T(8,128)(2,1)S(1)} %get-tuple-element.28), channel_id=1, source_target_pairs={{0,2},{1,5},{2,0},{3,7},{4,6},{5,1},{6,4},{7,3},{8,10},{9,13},{10,... | collective-permute-start | bytes 393224 | tf_op jit(solution)/shard_map/ppermute | solution.py:272
  26.1 4.6 %collective-permute-start.4 = (bf16[256,256]{1,0:T(8,128)(2,1)S(1)}, bf16[256,256]{1,0:T(8,128)(2,1)S(1)}, u32[]{:S(2)}, u32[]{:S(2)}) collective-permute-start(bf16[256,256]{1,0:T(8,128)(2,1)S(1)} %get-tuple-element.25.refs_2_), channel_id=1, source_target_pairs={{0,8},{1,17},{2,10},{3,19},{4,12},{5,21},{6,14},{7,23},{8,0},{9,25... | collective-permute-start | bytes 393224 | tf_op jit(solution)/shard_map/ppermute | solution.py:272
  30.7 2.1 %shard_map.96.refs_0_.refs_4_ = bf16[1664,512]{1,0:T(8,128)(2,1)S(1)} custom-call(s32[10,512]{1,0:T(8,128)S(1)} %bitcast.6, s32[1,512]{1,0:T(1,128)S(1)} %bitcast.10, bf16[256,256]{1,0:T(8,128)(2,1)S(1)} %get-tuple-element.25.refs_2_), custom_call_target="tpu_custom_call" | custom-call | flops 2000000000 | bytes 2000000 | tf_op jit(solution)/shard_map/pallas_call | solution.py:25
  33.3 5.7 %collective-permute-start.5 = (bf16[512,256]{1,0:T(8,128)(2,1)S(1)}, bf16[512,256]{1,0:T(8,128)(2,1)S(1)}, u32[]{:S(2)}, u32[]{:S(2)}) collective-permute-start(bf16[512,256]{1,0:T(8,128)(2,1)S(1)} %shard_map.98), channel_id=1, source_target_pairs={{0,1},{1,0},{2,3},{3,2},{4,5},{5,4},{6,7},{7,6},{8,9},{9,8},{10,11... | collective-permute-start | bytes 786440 | tf_op jit(solution)/shard_map/ppermute | solution.py:268
  39.0 0.7 shard_map.97
  39.7 0.4 collective-permute-done.5.refs_3_
  40.1 2.0 %shard_map.99 = (bf16[512,256]{1,0:T(8,128)(2,1)}, bf16[512,256]{1,0:T(8,128)(2,1)}, bf16[512,256]{1,0:T(8,128)(2,1)S(1)}, bf16[512,256]{1,0:T(8,128)(2,1)S(1)}) custom-call(bf16[1664,512]{1,0:T(8,128)(2,1)S(1)} %shard_map.96.refs_0_.refs_4_, f32[512,256]{1,0:T(8,128)S(1)} %get-tuple-element.29.refs_1_, f32[512,256]{1,0:T(8,128)S(1)} %get-tuple-element.30.refs_2_, ...), custom_call_target="tpu_custom_call" | custom-call | flops 2000000000 | bytes 5000000 | tf_op jit(solution)/shard_map/pallas_call | solution.py:25
  42.1 8.7 %all-to-all-start = ((bf16[32,16,256]{2,1,0:T(8,128)(2,1)}), bf16[32,16,256]{2,1,0:T(8,128)(2,1)S(1)}, u32[]{:S(2)}, u32[]{:S(2)}) async-start(bf16[32,16,256]{2,1,0:T(8,128)(2,1)} %bitcast.3), calls=%async_computation | async-start | bytes 524288 | tf_op jit(solution)/shard_map/all_to_all | solution.py:238
  50.8 0.7 shard_map.100
  51.5 2.3 %collective-permute-start.6 = (bf16[384,256]{1,0:T(8,128)(2,1)S(1)}, bf16[384,256]{1,0:T(8,128)(2,1)S(1)}, u32[]{:S(2)}, u32[]{:S(2)}) collective-permute-start(bf16[384,256]{1,0:T(8,128)(2,1)S(1)} %get-tuple-element.35), channel_id=1, source_target_pairs={{0,1},{1,0},{2,3},{3,2},{4,5},{5,4},{6,7},{7,6},{8,9},{9,8},{10,11... | collective-permute-start | bytes 589832 | tf_op jit(solution)/shard_map/ppermute | solution.py:268
  53.8 2.1 %collective-permute-start.7 = (bf16[256,256]{1,0:T(8,128)(2,1)S(1)}, bf16[256,256]{1,0:T(8,128)(2,1)S(1)}, u32[]{:S(2)}, u32[]{:S(2)}) collective-permute-start(bf16[256,256]{1,0:T(8,128)(2,1)S(1)} %get-tuple-element.37), channel_id=1, source_target_pairs={{0,1},{1,0},{2,3},{3,2},{4,5},{5,4},{6,7},{7,6},{8,9},{9,8},{10,11... | collective-permute-start | bytes 393224 | tf_op jit(solution)/shard_map/ppermute | solution.py:268
  55.8 1.2 %collective-permute-done.7.refs_1_ = bf16[256,256]{1,0:T(8,128)(2,1)S(1)} collective-permute-done((bf16[256,256]{1,0:T(8,128)(2,1)S(1)}, bf16[256,256]{1,0:T(8,128)(2,1)S(1)}, u32[]{:S(2)}, u32[]{:S(2)}) %collective-permute-start.7) | collective-permute-done | bytes 131104 | tf_op jit(solution)/shard_map/ppermute | solution.py:268
  57.0 0.7 shard_map.104
  57.7 11.6 %all-to-all-start.1 = ((bf16[16,16,256]{2,1,0:T(8,128)(2,1)}), bf16[16,16,256]{2,1,0:T(8,128)(2,1)S(1)}, u32[]{:S(2)}, u32[]{:S(2)}) async-start(bf16[16,16,256]{2,1,0:T(8,128)(2,1)} %shard_map.104), calls=%async_computation.1 | async-start | bytes 262144 | tf_op jit(solution)/shard_map/all_to_all | solution.py:238
  69.4 2.2 %collective-permute-start.8 = (bf16[256,256]{1,0:T(8,128)(2,1)S(1)}, bf16[256,256]{1,0:T(8,128)(2,1)S(1)}, u32[]{:S(2)}, u32[]{:S(2)}) collective-permute-start(bf16[256,256]{1,0:T(8,128)(2,1)S(1)} %get-tuple-element.38), channel_id=1, source_target_pairs={{0,256},{1,129},{2,258},{3,131},{4,260},{5,133},{6,262},{7,135},{8... | collective-permute-start | bytes 393224 | tf_op jit(solution)/shard_map/ppermute | solution.py:272
  71.6 2.2 %collective-permute-start.9 = (bf16[256,256]{1,0:T(8,128)(2,1)S(1)}, bf16[256,256]{1,0:T(8,128)(2,1)S(1)}, u32[]{:S(2)}, u32[]{:S(2)}) collective-permute-start(bf16[256,256]{1,0:T(8,128)(2,1)S(1)} %get-tuple-element.39), channel_id=1, source_target_pairs={{0,32},{1,65},{2,34},{3,67},{4,36},{5,69},{6,38},{7,71},{8,40},{9,... | collective-permute-start | bytes 393224 | tf_op jit(solution)/shard_map/ppermute | solution.py:272
  73.8 2.5 %collective-permute-start.10 = (bf16[256,256]{1,0:T(8,128)(2,1)S(1)}, bf16[256,256]{1,0:T(8,128)(2,1)S(1)}, u32[]{:S(2)}, u32[]{:S(2)}) collective-permute-start(bf16[256,256]{1,0:T(8,128)(2,1)S(1)} %get-tuple-element.40), channel_id=1, source_target_pairs={{0,2},{1,5},{2,0},{3,7},{4,6},{5,1},{6,4},{7,3},{8,10},{9,13},{10,... | collective-permute-start | bytes 393224 | tf_op jit(solution)/shard_map/ppermute | solution.py:272
  76.3 4.5 %collective-permute-start.11 = (bf16[256,256]{1,0:T(8,128)(2,1)S(1)}, bf16[256,256]{1,0:T(8,128)(2,1)S(1)}, u32[]{:S(2)}, u32[]{:S(2)}) collective-permute-start(bf16[256,256]{1,0:T(8,128)(2,1)S(1)} %get-tuple-element.41), channel_id=1, source_target_pairs={{0,8},{1,17},{2,10},{3,19},{4,12},{5,21},{6,14},{7,23},{8,0},{9,25... | collective-permute-start | bytes 393224 | tf_op jit(solution)/shard_map/ppermute | solution.py:272
  80.8 0.7 shard_map.105.refs_4_
  81.6 6.8 %all-to-all-start.2 = ((bf16[32,16,256]{2,1,0:T(8,128)(2,1)}), bf16[32,16,256]{2,1,0:T(8,128)(2,1)S(1)}, u32[]{:S(2)}, u32[]{:S(2)}) async-start(bf16[32,16,256]{2,1,0:T(8,128)(2,1)} %shard_map.105.refs_4_), calls=%async_computation.2 | async-start | bytes 524288 | tf_op jit(solution)/shard_map/all_to_all | solution.py:238
  88.5 2.3 %collective-permute-start.12 = (bf16[512,256]{1,0:T(8,128)(2,1)S(1)}, bf16[512,256]{1,0:T(8,128)(2,1)S(1)}, u32[]{:S(2)}, u32[]{:S(2)}) collective-permute-start(bf16[512,256]{1,0:T(8,128)(2,1)S(1)} %shard_map.106), channel_id=1, source_target_pairs={{0,1},{1,0},{2,3},{3,2},{4,5},{5,4},{6,7},{7,6},{8,9},{9,8},{10,11... | collective-permute-start | bytes 786440 | tf_op jit(solution)/shard_map/ppermute | solution.py:268
  90.8 0.5 shard_map.103.refs_1_
  91.3 1.2 %all-to-all-done.2 = bf16[32,16,256]{2,1,0:T(8,128)(2,1)S(1)} async-done(((bf16[32,16,256]{2,1,0:T(8,128)(2,1)}), bf16[32,16,256]{2,1,0:T(8,128)(2,1)S(1)}, u32[]{:S(2)}, u32[]{:S(2)}) %all-to-all-start.2) | async-done | bytes 262176 | tf_op jit(solution)/shard_map/all_to_all | solution.py:238
  92.5 1.1 %shard_map.108 = f32[512,256]{1,0:T(8,128)} custom-call(bf16[512,256]{1,0:T(8,128)(2,1)S(1)} %bitcast.5), custom_call_target="tpu_custom_call" | custom-call | flops 100000000 | bytes 1000000 | tf_op jit(solution)/shard_map/pallas_call | solution.py:25
  93.6 1.1 %shard_map.107 = bf16[512,256]{1,0:T(8,128)(2,1)} custom-call(s32[9,1,128]{2,1,0:T(1,128)S(1)} %bitcast.9, f32[512,256]{1,0:T(8,128)S(1)} %shard_map.103.refs_1_, bf16[512,256]{1,0:T(8,128)(2,1)S(1)} %collective-permute-done.12.refs_2_), custom_call_target="tpu_custom_call" | custom-call | flops 1000000000 | bytes 1000000 | tf_op jit(solution)/shard_map/pallas_call | solution.py:25
  (33 shorter events, 0.6 us)
Async XLA Ops:
  0.6 1.0 %copy-start.1 = (bf16[512,256]{1,0:T(8,128)(2,1)S(1)}, bf16[512,256]{1,0:T(8,128)(2,1)}, u32[]{:S(2)}) copy-start(bf16[512,256]{1,0:T(8,128)(2,1)} %refs_4_.1) | copy-start | bytes 786436
  1.6 0.7 copy-start.6
  2.3 28.4 %copy-start.5 = (s32[512,10]{0,1:T(8,128)S(1)}, s32[512,10]{0,1:T(8,128)}, u32[]{:S(2)}) copy-start(s32[512,10]{0,1:T(8,128)} %param.10) | copy-start | bytes 61444
  2.3 28.5 %copy-start.8 = (s32[512]{0:T(512)S(1)}, s32[512]{0:T(512)}, u32[]{:S(2)}) copy-start(s32[512]{0:T(512)} %param.11) | copy-start | bytes 6148
  2.8 10.0 %collective-permute-start = (bf16[640,256]{1,0:T(8,128)(2,1)S(1)}, bf16[640,256]{1,0:T(8,128)(2,1)S(1)}, u32[]{:S(2)}, u32[]{:S(2)}) collective-permute-start(bf16[640,256]{1,0:T(8,128)(2,1)S(1)} %get-tuple-element.24), channel_id=1, source_target_pairs={{0,1},{1,0},{2,3},{3,2},{4,5},{5,4},{6,7},{7,6},{8,9},{9,8},{10,11... | collective-permute-start | bytes 983048 | tf_op jit(solution)/shard_map/ppermute | solution.py:268
  12.9 20.0 %collective-permute-start.1 = (bf16[256,256]{1,0:T(8,128)(2,1)S(1)}, bf16[256,256]{1,0:T(8,128)(2,1)S(1)}, u32[]{:S(2)}, u32[]{:S(2)}) collective-permute-start(bf16[256,256]{1,0:T(8,128)(2,1)S(1)} %get-tuple-element.26), channel_id=1, source_target_pairs={{0,256},{1,129},{2,258},{3,131},{4,260},{5,133},{6,262},{7,135},{8... | collective-permute-start | bytes 393224 | tf_op jit(solution)/shard_map/ppermute | solution.py:272
  16.3 16.6 %collective-permute-start.2 = (bf16[256,256]{1,0:T(8,128)(2,1)S(1)}, bf16[256,256]{1,0:T(8,128)(2,1)S(1)}, u32[]{:S(2)}, u32[]{:S(2)}) collective-permute-start(bf16[256,256]{1,0:T(8,128)(2,1)S(1)} %get-tuple-element.27), channel_id=1, source_target_pairs={{0,32},{1,65},{2,34},{3,67},{4,36},{5,69},{6,38},{7,71},{8,40},{9,... | collective-permute-start | bytes 393224 | tf_op jit(solution)/shard_map/ppermute | solution.py:272
  21.2 11.7 %collective-permute-start.3 = (bf16[256,256]{1,0:T(8,128)(2,1)S(1)}, bf16[256,256]{1,0:T(8,128)(2,1)S(1)}, u32[]{:S(2)}, u32[]{:S(2)}) collective-permute-start(bf16[256,256]{1,0:T(8,128)(2,1)S(1)} %get-tuple-element.28), channel_id=1, source_target_pairs={{0,2},{1,5},{2,0},{3,7},{4,6},{5,1},{6,4},{7,3},{8,10},{9,13},{10,... | collective-permute-start | bytes 393224 | tf_op jit(solution)/shard_map/ppermute | solution.py:272
  26.1 7.2 %collective-permute-start.4 = (bf16[256,256]{1,0:T(8,128)(2,1)S(1)}, bf16[256,256]{1,0:T(8,128)(2,1)S(1)}, u32[]{:S(2)}, u32[]{:S(2)}) collective-permute-start(bf16[256,256]{1,0:T(8,128)(2,1)S(1)} %get-tuple-element.25.refs_2_), channel_id=1, source_target_pairs={{0,8},{1,17},{2,10},{3,19},{4,12},{5,21},{6,14},{7,23},{8,0},{9,25... | collective-permute-start | bytes 393224 | tf_op jit(solution)/shard_map/ppermute | solution.py:272
  32.8 6.1 %copy-start = (bf16[256,256]{1,0:T(8,128)(2,1)S(1)}, bf16[256,256]{1,0:T(8,128)(2,1)}, u32[]{:S(2)}) copy-start(bf16[256,256]{1,0:T(8,128)(2,1)} %refs_3_.1) | copy-start | bytes 393220
  32.9 6.1 %copy-start.2 = (bf16[512,256]{1,0:T(8,128)(2,1)S(1)}, bf16[512,256]{1,0:T(8,128)(2,1)}, u32[]{:S(2)}) copy-start(bf16[512,256]{1,0:T(8,128)(2,1)} %refs_4_.1) | copy-start | bytes 786436
  33.3 6.8 %copy-start.3 = (bf16[512,256]{1,0:T(8,128)(2,1)S(1)}, bf16[512,256]{1,0:T(8,128)(2,1)}, u32[]{:S(2)}) copy-start(bf16[512,256]{1,0:T(8,128)(2,1)} %refs_6_.1) | copy-start | bytes 786436
  33.3 6.8 %copy-start.4 = (bf16[256,256]{1,0:T(8,128)(2,1)S(1)}, bf16[256,256]{1,0:T(8,128)(2,1)}, u32[]{:S(2)}) copy-start(bf16[256,256]{1,0:T(8,128)(2,1)} %refs_7_.1) | copy-start | bytes 393220
  33.3 6.8 %collective-permute-start.5 = (bf16[512,256]{1,0:T(8,128)(2,1)S(1)}, bf16[512,256]{1,0:T(8,128)(2,1)S(1)}, u32[]{:S(2)}, u32[]{:S(2)}) collective-permute-start(bf16[512,256]{1,0:T(8,128)(2,1)S(1)} %shard_map.98), channel_id=1, source_target_pairs={{0,1},{1,0},{2,3},{3,2},{4,5},{5,4},{6,7},{7,6},{8,9},{9,8},{10,11... | collective-permute-start | bytes 786440 | tf_op jit(solution)/shard_map/ppermute | solution.py:268
  42.1 14.9 %all-to-all-start = ((bf16[32,16,256]{2,1,0:T(8,128)(2,1)}), bf16[32,16,256]{2,1,0:T(8,128)(2,1)S(1)}, u32[]{:S(2)}, u32[]{:S(2)}) async-start(bf16[32,16,256]{2,1,0:T(8,128)(2,1)} %bitcast.3), calls=%async_computation | async-start | bytes 524288 | tf_op jit(solution)/shard_map/all_to_all | solution.py:238
  51.5 5.5 %collective-permute-start.6 = (bf16[384,256]{1,0:T(8,128)(2,1)S(1)}, bf16[384,256]{1,0:T(8,128)(2,1)S(1)}, u32[]{:S(2)}, u32[]{:S(2)}) collective-permute-start(bf16[384,256]{1,0:T(8,128)(2,1)S(1)} %get-tuple-element.35), channel_id=1, source_target_pairs={{0,1},{1,0},{2,3},{3,2},{4,5},{5,4},{6,7},{7,6},{8,9},{9,8},{10,11... | collective-permute-start | bytes 589832 | tf_op jit(solution)/shard_map/ppermute | solution.py:268
  53.8 3.2 %collective-permute-start.7 = (bf16[256,256]{1,0:T(8,128)(2,1)S(1)}, bf16[256,256]{1,0:T(8,128)(2,1)S(1)}, u32[]{:S(2)}, u32[]{:S(2)}) collective-permute-start(bf16[256,256]{1,0:T(8,128)(2,1)S(1)} %get-tuple-element.37), channel_id=1, source_target_pairs={{0,1},{1,0},{2,3},{3,2},{4,5},{5,4},{6,7},{7,6},{8,9},{9,8},{10,11... | collective-permute-start | bytes 393224 | tf_op jit(solution)/shard_map/ppermute | solution.py:268
  57.7 33.0 %copy-start.7 = (s32[1,9,128]{2,0,1:T(1,128)S(1)}, s32[1,9,128]{2,0,1:T(1,128)}, u32[]{:S(2)}) copy-start(s32[1,9,128]{2,0,1:T(1,128)} %param.12) | copy-start | bytes 13828
  57.7 23.1 %all-to-all-start.1 = ((bf16[16,16,256]{2,1,0:T(8,128)(2,1)}), bf16[16,16,256]{2,1,0:T(8,128)(2,1)S(1)}, u32[]{:S(2)}, u32[]{:S(2)}) async-start(bf16[16,16,256]{2,1,0:T(8,128)(2,1)} %shard_map.104), calls=%async_computation.1 | async-start | bytes 262144 | tf_op jit(solution)/shard_map/all_to_all | solution.py:238
  69.4 19.1 %collective-permute-start.8 = (bf16[256,256]{1,0:T(8,128)(2,1)S(1)}, bf16[256,256]{1,0:T(8,128)(2,1)S(1)}, u32[]{:S(2)}, u32[]{:S(2)}) collective-permute-start(bf16[256,256]{1,0:T(8,128)(2,1)S(1)} %get-tuple-element.38), channel_id=1, source_target_pairs={{0,256},{1,129},{2,258},{3,131},{4,260},{5,133},{6,262},{7,135},{8... | collective-permute-start | bytes 393224 | tf_op jit(solution)/shard_map/ppermute | solution.py:272
  71.6 16.9 %collective-permute-start.9 = (bf16[256,256]{1,0:T(8,128)(2,1)S(1)}, bf16[256,256]{1,0:T(8,128)(2,1)S(1)}, u32[]{:S(2)}, u32[]{:S(2)}) collective-permute-start(bf16[256,256]{1,0:T(8,128)(2,1)S(1)} %get-tuple-element.39), channel_id=1, source_target_pairs={{0,32},{1,65},{2,34},{3,67},{4,36},{5,69},{6,38},{7,71},{8,40},{9,... | collective-permute-start | bytes 393224 | tf_op jit(solution)/shard_map/ppermute | solution.py:272
  73.8 14.7 %collective-permute-start.10 = (bf16[256,256]{1,0:T(8,128)(2,1)S(1)}, bf16[256,256]{1,0:T(8,128)(2,1)S(1)}, u32[]{:S(2)}, u32[]{:S(2)}) collective-permute-start(bf16[256,256]{1,0:T(8,128)(2,1)S(1)} %get-tuple-element.40), channel_id=1, source_target_pairs={{0,2},{1,5},{2,0},{3,7},{4,6},{5,1},{6,4},{7,3},{8,10},{9,13},{10,... | collective-permute-start | bytes 393224 | tf_op jit(solution)/shard_map/ppermute | solution.py:272
  76.3 12.1 %collective-permute-start.11 = (bf16[256,256]{1,0:T(8,128)(2,1)S(1)}, bf16[256,256]{1,0:T(8,128)(2,1)S(1)}, u32[]{:S(2)}, u32[]{:S(2)}) collective-permute-start(bf16[256,256]{1,0:T(8,128)(2,1)S(1)} %get-tuple-element.41), channel_id=1, source_target_pairs={{0,8},{1,17},{2,10},{3,19},{4,12},{5,21},{6,14},{7,23},{8,0},{9,25... | collective-permute-start | bytes 393224 | tf_op jit(solution)/shard_map/ppermute | solution.py:272
  81.6 10.9 %all-to-all-start.2 = ((bf16[32,16,256]{2,1,0:T(8,128)(2,1)}), bf16[32,16,256]{2,1,0:T(8,128)(2,1)S(1)}, u32[]{:S(2)}, u32[]{:S(2)}) async-start(bf16[32,16,256]{2,1,0:T(8,128)(2,1)} %shard_map.105.refs_4_), calls=%async_computation.2 | async-start | bytes 524288 | tf_op jit(solution)/shard_map/all_to_all | solution.py:238
  88.5 5.1 %collective-permute-start.12 = (bf16[512,256]{1,0:T(8,128)(2,1)S(1)}, bf16[512,256]{1,0:T(8,128)(2,1)S(1)}, u32[]{:S(2)}, u32[]{:S(2)}) collective-permute-start(bf16[512,256]{1,0:T(8,128)(2,1)S(1)} %shard_map.106), channel_id=1, source_target_pairs={{0,1},{1,0},{2,3},{3,2},{4,5},{5,4},{6,7},{7,6},{8,9},{9,8},{10,11... | collective-permute-start | bytes 786440 | tf_op jit(solution)/shard_map/ppermute | solution.py:268

commit v8 on v6

--- a/solution.py
+++ b/solution.py
@@ -10,6 +10,7 @@
 bf16 = jnp.bfloat16
 FAST_BITS = 5
 NEAR_FIRST = 21
+FAR_FIRST = 9
 VMEM_LIMIT = 16 * 1024 * 1024
 TRANSPOSED_LHS = (((0,), (0,)), ((), ()))
 TRANSPOSED_RHS = (((1,), (1,)), ((), ()))
@@ -259,7 +260,7 @@
     load_shape = shape((2 * bnd, width), bf16)
     near = bit_groups(devices, range(FAST_BITS))
     far = bit_groups(devices, range(FAST_BITS, levels))
-    far = [group[len(group) // 2 :] + group[: len(group) // 2] for group in far]
+    far = [group[FAR_FIRST:] + group[:FAR_FIRST] for group in far]
     near = [group[NEAR_FIRST:] + group[:NEAR_FIRST] for group in near]
     piece = 2 * width // len(near[0])
     small = (10**8, 10**6)

time: 95.4 us -> 95.8 us (level)
  no operation moved by 1% of the time
where the time goes in v8:
time: 95.8 us; the launch traced here: 95 us
  starting transfers between devices  77.9 us (81%)
  Pallas kernels  10.3 us (11%)
  waiting for transfers between devices  4.21 us (4%)
  local copies, waits for them, and re-layouts  1.67 us (2%)
  between operations  0.96 us (1%)
    ppermute x8, starting transfers between devices, across(): lax.ppermute(x, 'dom', [(i, i ^ 1 << pair[i % 2]) for i in range(devices)])  30.1 us
    all_to_all x3, starting transfers between devices, exchange(): return lax.all_to_all(x, 'dom', 0, 0, axis_index_groups=groups, tiled=True)  26.7 us
    ppermute x5, starting transfers between devices, other_core(): return lax.ppermute(x, 'dom', [(i, i ^ 1) for i in range(devices)])  21.1 us
    pallas_call x15, Pallas kernels, call(): pl.pallas_call(lambda *refs: body(*refs[:reads], *refs[reads + waits:]),...  10.3 us
    ppermute x5, waiting for transfers between devices, other_core(): return lax.ppermute(x, 'dom', [(i, i ^ 1) for i in range(devices)])  2.8 us
  transfers between devices with their start and end apart: 16, of which 5 were waited for; matrix products, arithmetic and copies ran while one was open for 0% of the time, Pallas kernels for 6%

profile of v8, /device:TPU:1, one launch (start us, length us, event | category | flops | bytes accessed | tf_op | source)
XLA Modules:
  0.0 95.0 jit_solution(1652291269244531539)
XLA Ops:
  0.6 0.9 copy-done.1
  1.6 0.7 copy-done.6
  2.3 0.5 shard_map.94
  2.8 8.8 %collective-permute-start = (bf16[640,256]{1,0:T(8,128)(2,1)S(1)}, bf16[640,256]{1,0:T(8,128)(2,1)S(1)}, u32[]{:S(2)}, u32[]{:S(2)}) collective-permute-start(bf16[640,256]{1,0:T(8,128)(2,1)S(1)} %get-tuple-element.24), channel_id=1, source_target_pairs={{0,1},{1,0},{2,3},{3,2},{4,5},{5,4},{6,7},{7,6},{8,9},{9,8},{10,11... | collective-permute-start | bytes 983048 | tf_op jit(solution)/shard_map/ppermute | solution.py:269
  11.6 1.2 %collective-permute-done.refs_1_.refs_3_ = bf16[640,256]{1,0:T(8,128)(2,1)S(1)} collective-permute-done((bf16[640,256]{1,0:T(8,128)(2,1)S(1)}, bf16[640,256]{1,0:T(8,128)(2,1)S(1)}, u32[]{:S(2)}, u32[]{:S(2)}) %collective-permute-start) | collective-permute-done | bytes 327712 | tf_op jit(solution)/shard_map/ppermute | solution.py:269
  12.9 3.4 %collective-permute-start.1 = (bf16[256,256]{1,0:T(8,128)(2,1)S(1)}, bf16[256,256]{1,0:T(8,128)(2,1)S(1)}, u32[]{:S(2)}, u32[]{:S(2)}) collective-permute-start(bf16[256,256]{1,0:T(8,128)(2,1)S(1)} %get-tuple-element.26), channel_id=1, source_target_pairs={{0,256},{1,129},{2,258},{3,131},{4,260},{5,133},{6,262},{7,135},{8... | collective-permute-start | bytes 393224 | tf_op jit(solution)/shard_map/ppermute | solution.py:273
  16.3 4.9 %collective-permute-start.2 = (bf16[256,256]{1,0:T(8,128)(2,1)S(1)}, bf16[256,256]{1,0:T(8,128)(2,1)S(1)}, u32[]{:S(2)}, u32[]{:S(2)}) collective-permute-start(bf16[256,256]{1,0:T(8,128)(2,1)S(1)} %get-tuple-element.27), channel_id=1, source_target_pairs={{0,32},{1,65},{2,34},{3,67},{4,36},{5,69},{6,38},{7,71},{8,40},{9,... | collective-permute-start | bytes 393224 | tf_op jit(solution)/shard_map/ppermute | solution.py:273
  21.2 4.6 %collective-permute-start.3 = (bf16[256,256]{1,0:T(8,128)(2,1)S(1)}, bf16[256,256]{1,0:T(8,128)(2,1)S(1)}, u32[]{:S(2)}, u32[]{:S(2)}) collective-permute-start(bf16[256,256]{1,0:T(8,128)(2,1)S(1)} %get-tuple-element.28), channel_id=1, source_target_pairs={{0,8},{1,17},{2,10},{3,19},{4,12},{5,21},{6,14},{7,23},{8,0},{9,25... | collective-permute-start | bytes 393224 | tf_op jit(solution)/shard_map/ppermute | solution.py:273
  25.9 4.8 %collective-permute-start.4 = (bf16[256,256]{1,0:T(8,128)(2,1)S(1)}, bf16[256,256]{1,0:T(8,128)(2,1)S(1)}, u32[]{:S(2)}, u32[]{:S(2)}) collective-permute-start(bf16[256,256]{1,0:T(8,128)(2,1)S(1)} %get-tuple-element.25.refs_2_), channel_id=1, source_target_pairs={{0,2},{1,5},{2,0},{3,7},{4,6},{5,1},{6,4},{7,3},{8,10},{9,13},{10,... | collective-permute-start | bytes 393224 | tf_op jit(solution)/shard_map/ppermute | solution.py:273
  30.7 2.1 %shard_map.96.refs_0_.refs_4_ = bf16[1664,512]{1,0:T(8,128)(2,1)S(1)} custom-call(s32[10,512]{1,0:T(8,128)S(1)} %bitcast.6, s32[1,512]{1,0:T(1,128)S(1)} %bitcast.10, bf16[256,256]{1,0:T(8,128)(2,1)S(1)} %get-tuple-element.25.refs_2_), custom_call_target="tpu_custom_call" | custom-call | flops 2000000000 | bytes 2000000 | tf_op jit(solution)/shard_map/pallas_call | solution.py:26
  33.1 5.7 %collective-permute-start.5 = (bf16[512,256]{1,0:T(8,128)(2,1)S(1)}, bf16[512,256]{1,0:T(8,128)(2,1)S(1)}, u32[]{:S(2)}, u32[]{:S(2)}) collective-permute-start(bf16[512,256]{1,0:T(8,128)(2,1)S(1)} %shard_map.98), channel_id=1, source_target_pairs={{0,1},{1,0},{2,3},{3,2},{4,5},{5,4},{6,7},{7,6},{8,9},{9,8},{10,11... | collective-permute-start | bytes 786440 | tf_op jit(solution)/shard_map/ppermute | solution.py:269
  38.9 0.7 shard_map.97
  39.7 0.4 collective-permute-done.5.refs_3_
  40.0 2.0 %shard_map.99 = (bf16[512,256]{1,0:T(8,128)(2,1)}, bf16[512,256]{1,0:T(8,128)(2,1)}, bf16[512,256]{1,0:T(8,128)(2,1)S(1)}, bf16[512,256]{1,0:T(8,128)(2,1)S(1)}) custom-call(bf16[1664,512]{1,0:T(8,128)(2,1)S(1)} %shard_map.96.refs_0_.refs_4_, f32[512,256]{1,0:T(8,128)S(1)} %get-tuple-element.29.refs_1_, f32[512,256]{1,0:T(8,128)S(1)} %get-tuple-element.30.refs_2_, ...), custom_call_target="tpu_custom_call" | custom-call | flops 2000000000 | bytes 5000000 | tf_op jit(solution)/shard_map/pallas_call | solution.py:26
  42.0 8.7 %all-to-all-start = ((bf16[32,16,256]{2,1,0:T(8,128)(2,1)}), bf16[32,16,256]{2,1,0:T(8,128)(2,1)S(1)}, u32[]{:S(2)}, u32[]{:S(2)}) async-start(bf16[32,16,256]{2,1,0:T(8,128)(2,1)} %bitcast.3), calls=%async_computation | async-start | bytes 524288 | tf_op jit(solution)/shard_map/all_to_all | solution.py:239
  50.7 0.7 shard_map.100
  51.4 2.3 %collective-permute-start.6 = (bf16[384,256]{1,0:T(8,128)(2,1)S(1)}, bf16[384,256]{1,0:T(8,128)(2,1)S(1)}, u32[]{:S(2)}, u32[]{:S(2)}) collective-permute-start(bf16[384,256]{1,0:T(8,128)(2,1)S(1)} %get-tuple-element.35), channel_id=1, source_target_pairs={{0,1},{1,0},{2,3},{3,2},{4,5},{5,4},{6,7},{7,6},{8,9},{9,8},{10,11... | collective-permute-start | bytes 589832 | tf_op jit(solution)/shard_map/ppermute | solution.py:269
  53.7 2.1 %collective-permute-start.7 = (bf16[256,256]{1,0:T(8,128)(2,1)S(1)}, bf16[256,256]{1,0:T(8,128)(2,1)S(1)}, u32[]{:S(2)}, u32[]{:S(2)}) collective-permute-start(bf16[256,256]{1,0:T(8,128)(2,1)S(1)} %get-tuple-element.37), channel_id=1, source_target_pairs={{0,1},{1,0},{2,3},{3,2},{4,5},{5,4},{6,7},{7,6},{8,9},{9,8},{10,11... | collective-permute-start | bytes 393224 | tf_op jit(solution)/shard_map/ppermute | solution.py:269
  55.8 1.2 %collective-permute-done.7.refs_1_ = bf16[256,256]{1,0:T(8,128)(2,1)S(1)} collective-permute-done((bf16[256,256]{1,0:T(8,128)(2,1)S(1)}, bf16[256,256]{1,0:T(8,128)(2,1)S(1)}, u32[]{:S(2)}, u32[]{:S(2)}) %collective-permute-start.7) | collective-permute-done | bytes 131104 | tf_op jit(solution)/shard_map/ppermute | solution.py:269
  57.0 0.7 shard_map.104
  57.7 11.1 %all-to-all-start.1 = ((bf16[16,16,256]{2,1,0:T(8,128)(2,1)}), bf16[16,16,256]{2,1,0:T(8,128)(2,1)S(1)}, u32[]{:S(2)}, u32[]{:S(2)}) async-start(bf16[16,16,256]{2,1,0:T(8,128)(2,1)} %shard_map.104), calls=%async_computation.1 | async-start | bytes 262144 | tf_op jit(solution)/shard_map/all_to_all | solution.py:239
  68.8 3.1 %collective-permute-start.8 = (bf16[256,256]{1,0:T(8,128)(2,1)S(1)}, bf16[256,256]{1,0:T(8,128)(2,1)S(1)}, u32[]{:S(2)}, u32[]{:S(2)}) collective-permute-start(bf16[256,256]{1,0:T(8,128)(2,1)S(1)} %get-tuple-element.38), channel_id=1, source_target_pairs={{0,256},{1,129},{2,258},{3,131},{4,260},{5,133},{6,262},{7,135},{8... | collective-permute-start | bytes 393224 | tf_op jit(solution)/shard_map/ppermute | solution.py:273
  71.9 2.2 %collective-permute-start.9 = (bf16[256,256]{1,0:T(8,128)(2,1)S(1)}, bf16[256,256]{1,0:T(8,128)(2,1)S(1)}, u32[]{:S(2)}, u32[]{:S(2)}) collective-permute-start(bf16[256,256]{1,0:T(8,128)(2,1)S(1)} %get-tuple-element.39), channel_id=1, source_target_pairs={{0,32},{1,65},{2,34},{3,67},{4,36},{5,69},{6,38},{7,71},{8,40},{9,... | collective-permute-start | bytes 393224 | tf_op jit(solution)/shard_map/ppermute | solution.py:273
  74.2 2.4 %collective-permute-start.10 = (bf16[256,256]{1,0:T(8,128)(2,1)S(1)}, bf16[256,256]{1,0:T(8,128)(2,1)S(1)}, u32[]{:S(2)}, u32[]{:S(2)}) collective-permute-start(bf16[256,256]{1,0:T(8,128)(2,1)S(1)} %get-tuple-element.40), channel_id=1, source_target_pairs={{0,8},{1,17},{2,10},{3,19},{4,12},{5,21},{6,14},{7,23},{8,0},{9,25... | collective-permute-start | bytes 393224 | tf_op jit(solution)/shard_map/ppermute | solution.py:273
  76.5 4.7 %collective-permute-start.11 = (bf16[256,256]{1,0:T(8,128)(2,1)S(1)}, bf16[256,256]{1,0:T(8,128)(2,1)S(1)}, u32[]{:S(2)}, u32[]{:S(2)}) collective-permute-start(bf16[256,256]{1,0:T(8,128)(2,1)S(1)} %get-tuple-element.41), channel_id=1, source_target_pairs={{0,2},{1,5},{2,0},{3,7},{4,6},{5,1},{6,4},{7,3},{8,10},{9,13},{10,... | collective-permute-start | bytes 393224 | tf_op jit(solution)/shard_map/ppermute | solution.py:273
  81.2 0.7 shard_map.105.refs_4_
  81.9 6.8 %all-to-all-start.2 = ((bf16[32,16,256]{2,1,0:T(8,128)(2,1)}), bf16[32,16,256]{2,1,0:T(8,128)(2,1)S(1)}, u32[]{:S(2)}, u32[]{:S(2)}) async-start(bf16[32,16,256]{2,1,0:T(8,128)(2,1)} %shard_map.105.refs_4_), calls=%async_computation.2 | async-start | bytes 524288 | tf_op jit(solution)/shard_map/all_to_all | solution.py:239
  88.9 2.3 %collective-permute-start.12 = (bf16[512,256]{1,0:T(8,128)(2,1)S(1)}, bf16[512,256]{1,0:T(8,128)(2,1)S(1)}, u32[]{:S(2)}, u32[]{:S(2)}) collective-permute-start(bf16[512,256]{1,0:T(8,128)(2,1)S(1)} %shard_map.106), channel_id=1, source_target_pairs={{0,1},{1,0},{2,3},{3,2},{4,5},{5,4},{6,7},{7,6},{8,9},{9,8},{10,11... | collective-permute-start | bytes 786440 | tf_op jit(solution)/shard_map/ppermute | solution.py:269
  91.1 0.5 shard_map.103.refs_1_
  91.6 1.2 %all-to-all-done.2 = bf16[32,16,256]{2,1,0:T(8,128)(2,1)S(1)} async-done(((bf16[32,16,256]{2,1,0:T(8,128)(2,1)}), bf16[32,16,256]{2,1,0:T(8,128)(2,1)S(1)}, u32[]{:S(2)}, u32[]{:S(2)}) %all-to-all-start.2) | async-done | bytes 262176 | tf_op jit(solution)/shard_map/all_to_all | solution.py:239
  92.8 1.1 %shard_map.108 = f32[512,256]{1,0:T(8,128)} custom-call(bf16[512,256]{1,0:T(8,128)(2,1)S(1)} %bitcast.5), custom_call_target="tpu_custom_call" | custom-call | flops 100000000 | bytes 1000000 | tf_op jit(solution)/shard_map/pallas_call | solution.py:26
  93.9 1.1 %shard_map.107 = bf16[512,256]{1,0:T(8,128)(2,1)} custom-call(s32[9,1,128]{2,1,0:T(1,128)S(1)} %bitcast.9, f32[512,256]{1,0:T(8,128)S(1)} %shard_map.103.refs_1_, bf16[512,256]{1,0:T(8,128)(2,1)S(1)} %collective-permute-done.12.refs_2_), custom_call_target="tpu_custom_call" | custom-call | flops 1000000000 | bytes 1000000 | tf_op jit(solution)/shard_map/pallas_call | solution.py:26
  (33 shorter events, 0.4 us)
Async XLA Ops:
  0.6 1.0 %copy-start.1 = (bf16[512,256]{1,0:T(8,128)(2,1)S(1)}, bf16[512,256]{1,0:T(8,128)(2,1)}, u32[]{:S(2)}) copy-start(bf16[512,256]{1,0:T(8,128)(2,1)} %refs_4_.1) | copy-start | bytes 786436
  1.6 0.7 copy-start.6
  2.3 28.4 %copy-start.5 = (s32[512,10]{0,1:T(8,128)S(1)}, s32[512,10]{0,1:T(8,128)}, u32[]{:S(2)}) copy-start(s32[512,10]{0,1:T(8,128)} %param.10) | copy-start | bytes 61444
  2.3 28.5 %copy-start.8 = (s32[512]{0:T(512)S(1)}, s32[512]{0:T(512)}, u32[]{:S(2)}) copy-start(s32[512]{0:T(512)} %param.11) | copy-start | bytes 6148
  2.8 10.0 %collective-permute-start = (bf16[640,256]{1,0:T(8,128)(2,1)S(1)}, bf16[640,256]{1,0:T(8,128)(2,1)S(1)}, u32[]{:S(2)}, u32[]{:S(2)}) collective-permute-start(bf16[640,256]{1,0:T(8,128)(2,1)S(1)} %get-tuple-element.24), channel_id=1, source_target_pairs={{0,1},{1,0},{2,3},{3,2},{4,5},{5,4},{6,7},{7,6},{8,9},{9,8},{10,11... | collective-permute-start | bytes 983048 | tf_op jit(solution)/shard_map/ppermute | solution.py:269
  12.9 20.0 %collective-permute-start.1 = (bf16[256,256]{1,0:T(8,128)(2,1)S(1)}, bf16[256,256]{1,0:T(8,128)(2,1)S(1)}, u32[]{:S(2)}, u32[]{:S(2)}) collective-permute-start(bf16[256,256]{1,0:T(8,128)(2,1)S(1)} %get-tuple-element.26), channel_id=1, source_target_pairs={{0,256},{1,129},{2,258},{3,131},{4,260},{5,133},{6,262},{7,135},{8... | collective-permute-start | bytes 393224 | tf_op jit(solution)/shard_map/ppermute | solution.py:273
  16.3 16.6 %collective-permute-start.2 = (bf16[256,256]{1,0:T(8,128)(2,1)S(1)}, bf16[256,256]{1,0:T(8,128)(2,1)S(1)}, u32[]{:S(2)}, u32[]{:S(2)}) collective-permute-start(bf16[256,256]{1,0:T(8,128)(2,1)S(1)} %get-tuple-element.27), channel_id=1, source_target_pairs={{0,32},{1,65},{2,34},{3,67},{4,36},{5,69},{6,38},{7,71},{8,40},{9,... | collective-permute-start | bytes 393224 | tf_op jit(solution)/shard_map/ppermute | solution.py:273
  21.2 11.7 %collective-permute-start.3 = (bf16[256,256]{1,0:T(8,128)(2,1)S(1)}, bf16[256,256]{1,0:T(8,128)(2,1)S(1)}, u32[]{:S(2)}, u32[]{:S(2)}) collective-permute-start(bf16[256,256]{1,0:T(8,128)(2,1)S(1)} %get-tuple-element.28), channel_id=1, source_target_pairs={{0,8},{1,17},{2,10},{3,19},{4,12},{5,21},{6,14},{7,23},{8,0},{9,25... | collective-permute-start | bytes 393224 | tf_op jit(solution)/shard_map/ppermute | solution.py:273
  25.9 7.2 %collective-permute-start.4 = (bf16[256,256]{1,0:T(8,128)(2,1)S(1)}, bf16[256,256]{1,0:T(8,128)(2,1)S(1)}, u32[]{:S(2)}, u32[]{:S(2)}) collective-permute-start(bf16[256,256]{1,0:T(8,128)(2,1)S(1)} %get-tuple-element.25.refs_2_), channel_id=1, source_target_pairs={{0,2},{1,5},{2,0},{3,7},{4,6},{5,1},{6,4},{7,3},{8,10},{9,13},{10,... | collective-permute-start | bytes 393224 | tf_op jit(solution)/shard_map/ppermute | solution.py:273
  32.8 6.0 %copy-start = (bf16[256,256]{1,0:T(8,128)(2,1)S(1)}, bf16[256,256]{1,0:T(8,128)(2,1)}, u32[]{:S(2)}) copy-start(bf16[256,256]{1,0:T(8,128)(2,1)} %refs_3_.1) | copy-start | bytes 393220
  32.9 6.0 %copy-start.2 = (bf16[512,256]{1,0:T(8,128)(2,1)S(1)}, bf16[512,256]{1,0:T(8,128)(2,1)}, u32[]{:S(2)}) copy-start(bf16[512,256]{1,0:T(8,128)(2,1)} %refs_4_.1) | copy-start | bytes 786436
  33.1 6.9 %copy-start.3 = (bf16[512,256]{1,0:T(8,128)(2,1)S(1)}, bf16[512,256]{1,0:T(8,128)(2,1)}, u32[]{:S(2)}) copy-start(bf16[512,256]{1,0:T(8,128)(2,1)} %refs_6_.1) | copy-start | bytes 786436
  33.1 6.9 %copy-start.4 = (bf16[256,256]{1,0:T(8,128)(2,1)S(1)}, bf16[256,256]{1,0:T(8,128)(2,1)}, u32[]{:S(2)}) copy-start(bf16[256,256]{1,0:T(8,128)(2,1)} %refs_7_.1) | copy-start | bytes 393220
  33.1 6.9 %collective-permute-start.5 = (bf16[512,256]{1,0:T(8,128)(2,1)S(1)}, bf16[512,256]{1,0:T(8,128)(2,1)S(1)}, u32[]{:S(2)}, u32[]{:S(2)}) collective-permute-start(bf16[512,256]{1,0:T(8,128)(2,1)S(1)} %shard_map.98), channel_id=1, source_target_pairs={{0,1},{1,0},{2,3},{3,2},{4,5},{5,4},{6,7},{7,6},{8,9},{9,8},{10,11... | collective-permute-start | bytes 786440 | tf_op jit(solution)/shard_map/ppermute | solution.py:269
  42.0 14.9 %all-to-all-start = ((bf16[32,16,256]{2,1,0:T(8,128)(2,1)}), bf16[32,16,256]{2,1,0:T(8,128)(2,1)S(1)}, u32[]{:S(2)}, u32[]{:S(2)}) async-start(bf16[32,16,256]{2,1,0:T(8,128)(2,1)} %bitcast.3), calls=%async_computation | async-start | bytes 524288 | tf_op jit(solution)/shard_map/all_to_all | solution.py:239
  51.4 5.5 %collective-permute-start.6 = (bf16[384,256]{1,0:T(8,128)(2,1)S(1)}, bf16[384,256]{1,0:T(8,128)(2,1)S(1)}, u32[]{:S(2)}, u32[]{:S(2)}) collective-permute-start(bf16[384,256]{1,0:T(8,128)(2,1)S(1)} %get-tuple-element.35), channel_id=1, source_target_pairs={{0,1},{1,0},{2,3},{3,2},{4,5},{5,4},{6,7},{7,6},{8,9},{9,8},{10,11... | collective-permute-start | bytes 589832 | tf_op jit(solution)/shard_map/ppermute | solution.py:269
  53.7 3.2 %collective-permute-start.7 = (bf16[256,256]{1,0:T(8,128)(2,1)S(1)}, bf16[256,256]{1,0:T(8,128)(2,1)S(1)}, u32[]{:S(2)}, u32[]{:S(2)}) collective-permute-start(bf16[256,256]{1,0:T(8,128)(2,1)S(1)} %get-tuple-element.37), channel_id=1, source_target_pairs={{0,1},{1,0},{2,3},{3,2},{4,5},{5,4},{6,7},{7,6},{8,9},{9,8},{10,11... | collective-permute-start | bytes 393224 | tf_op jit(solution)/shard_map/ppermute | solution.py:269
  57.7 33.5 %copy-start.7 = (s32[1,9,128]{2,0,1:T(1,128)S(1)}, s32[1,9,128]{2,0,1:T(1,128)}, u32[]{:S(2)}) copy-start(s32[1,9,128]{2,0,1:T(1,128)} %param.12) | copy-start | bytes 13828
  57.7 23.5 %all-to-all-start.1 = ((bf16[16,16,256]{2,1,0:T(8,128)(2,1)}), bf16[16,16,256]{2,1,0:T(8,128)(2,1)S(1)}, u32[]{:S(2)}, u32[]{:S(2)}) async-start(bf16[16,16,256]{2,1,0:T(8,128)(2,1)} %shard_map.104), calls=%async_computation.1 | async-start | bytes 262144 | tf_op jit(solution)/shard_map/all_to_all | solution.py:239
  68.8 20.0 %collective-permute-start.8 = (bf16[256,256]{1,0:T(8,128)(2,1)S(1)}, bf16[256,256]{1,0:T(8,128)(2,1)S(1)}, u32[]{:S(2)}, u32[]{:S(2)}) collective-permute-start(bf16[256,256]{1,0:T(8,128)(2,1)S(1)} %get-tuple-element.38), channel_id=1, source_target_pairs={{0,256},{1,129},{2,258},{3,131},{4,260},{5,133},{6,262},{7,135},{8... | collective-permute-start | bytes 393224 | tf_op jit(solution)/shard_map/ppermute | solution.py:273
  71.9 16.9 %collective-permute-start.9 = (bf16[256,256]{1,0:T(8,128)(2,1)S(1)}, bf16[256,256]{1,0:T(8,128)(2,1)S(1)}, u32[]{:S(2)}, u32[]{:S(2)}) collective-permute-start(bf16[256,256]{1,0:T(8,128)(2,1)S(1)} %get-tuple-element.39), channel_id=1, source_target_pairs={{0,32},{1,65},{2,34},{3,67},{4,36},{5,69},{6,38},{7,71},{8,40},{9,... | collective-permute-start | bytes 393224 | tf_op jit(solution)/shard_map/ppermute | solution.py:273
  74.2 14.7 %collective-permute-start.10 = (bf16[256,256]{1,0:T(8,128)(2,1)S(1)}, bf16[256,256]{1,0:T(8,128)(2,1)S(1)}, u32[]{:S(2)}, u32[]{:S(2)}) collective-permute-start(bf16[256,256]{1,0:T(8,128)(2,1)S(1)} %get-tuple-element.40), channel_id=1, source_target_pairs={{0,8},{1,17},{2,10},{3,19},{4,12},{5,21},{6,14},{7,23},{8,0},{9,25... | collective-permute-start | bytes 393224 | tf_op jit(solution)/shard_map/ppermute | solution.py:273
  76.5 12.3 %collective-permute-start.11 = (bf16[256,256]{1,0:T(8,128)(2,1)S(1)}, bf16[256,256]{1,0:T(8,128)(2,1)S(1)}, u32[]{:S(2)}, u32[]{:S(2)}) collective-permute-start(bf16[256,256]{1,0:T(8,128)(2,1)S(1)} %get-tuple-element.41), channel_id=1, source_target_pairs={{0,2},{1,5},{2,0},{3,7},{4,6},{5,1},{6,4},{7,3},{8,10},{9,13},{10,... | collective-permute-start | bytes 393224 | tf_op jit(solution)/shard_map/ppermute | solution.py:273
  81.9 10.9 %all-to-all-start.2 = ((bf16[32,16,256]{2,1,0:T(8,128)(2,1)}), bf16[32,16,256]{2,1,0:T(8,128)(2,1)S(1)}, u32[]{:S(2)}, u32[]{:S(2)}) async-start(bf16[32,16,256]{2,1,0:T(8,128)(2,1)} %shard_map.105.refs_4_), calls=%async_computation.2 | async-start | bytes 524288 | tf_op jit(solution)/shard_map/all_to_all | solution.py:239
  88.9 5.1 %collective-permute-start.12 = (bf16[512,256]{1,0:T(8,128)(2,1)S(1)}, bf16[512,256]{1,0:T(8,128)(2,1)S(1)}, u32[]{:S(2)}, u32[]{:S(2)}) collective-permute-start(bf16[512,256]{1,0:T(8,128)(2,1)S(1)} %shard_map.106), channel_id=1, source_target_pairs={{0,1},{1,0},{2,3},{3,2},{4,5},{5,4},{6,7},{7,6},{8,9},{9,8},{10,11... | collective-permute-start | bytes 786440 | tf_op jit(solution)/shard_map/ppermute | solution.py:269
